TPU v7x, 512 devices: a whole 4x4x16 slice. The times are simulated.
512 devices in a mesh: tm: 16 (over z), space: 32 (over x, y, core).
Axes of the slice: x: 4, y: 4, z: 16, core: 2. Of those that a mesh axis runs over, the one named last changes fastest.
Arguments:
- right_side: float32 [64, 256, 16, 128], P('tm', 'space'), may hold values from -7 to 7, as said below
- state: float32 [64, 256, 16, 128], P('tm', 'space'), may hold values from -1 to 1
Outputs:
- correction: float32 [64, 256, 16, 128], P('tm', 'space')
Inputs may be any that keep to these rules, and one draw needn't show every extreme that they name: `right_side`: a rough field plus a smooth part.
All inputs are finite; a program needn't handle non-finite values.
Results may differ from a plain program's by a relative error of at most 0.0003.
Values sent between devices are 32-bit elements; how exact they have to be, the bound alone decides.
No kernel may reach another device: no remote copies, remote signals or barrier semaphores. Data moves between devices by JAX's collectives and lax.ppermute only.
A program may use at most 64 MiB of HBM per device.

v0:
```python
import jax
import jax.numpy as jnp
from jax import lax
from jax.sharding import PartitionSpec as P

CX = 16
CY = 128
CT = 4
CZ = 8
OV = 2
OT = 2
SWEEPS = 4
CHEB = 8


rate = 8.0
react = 0.5
damp = 0.9


def extended(x, sides, width):
    for axis, dim in sides:
        count, length = (lax.axis_size(axis), x.shape[dim])
        up = [(i, (i + 1) % count) for i in range(count)]
        down = [(j, i) for i, j in up]
        last = lax.slice_in_dim(x, length - width, length, axis=dim)
        initial = lax.slice_in_dim(x, 0, width, axis=dim)
        before = lax.ppermute(last, axis, up)
        after = lax.ppermute(initial, axis, down)
        x = jnp.concatenate([before, x, after], axis=dim)
    return x


def passed_along(x, axis, by):
    count = lax.axis_size(axis)
    pairs = [(i, i + by) for i in range(count) if 0 <= i + by < count]
    return lax.ppermute(x, axis, pairs)


def spatial_sum(padded_z, field):
    total = padded_z[:, 2:] + padded_z[:, :-2]
    total = total + jnp.roll(field, 1, axis=2) + jnp.roll(field, -1, axis=2)
    total = total + jnp.roll(field, 1, axis=3) + jnp.roll(field, -1, axis=3)
    return total


def sweep_block(rhs, coef, tmask):
    diag = rate + 6.0 + react * coef
    field = jnp.zeros_like(rhs)
    for sweep in range(SWEEPS):
        padded_z = jnp.pad(field, ((0, 0), (1, 1), (0, 0), (0, 0)))
        before = jnp.pad(field, ((1, 0), (0, 0), (0, 0), (0, 0)))[:-1]
        applied = diag * field - rate * before - spatial_sum(padded_z, field)
        field = (field + damp * (rhs - applied) / diag) * tmask[:, None, None, None]
    return field


def coarse_apply(field, coarse_coef):
    width = CY // 4
    yidx = jnp.arange(field.shape[-1], dtype=jnp.int32) % width
    yplus = jnp.where(
        yidx == width - 1, jnp.roll(field, width - 1, axis=-1), jnp.roll(field, -1, axis=-1)
    )
    yminus = jnp.where(
        yidx == 0, jnp.roll(field, -(width - 1), axis=-1), jnp.roll(field, 1, axis=-1)
    )
    beside = jnp.roll(field, 1, axis=1) + jnp.roll(field, -1, axis=1)
    beside = beside + jnp.roll(field, width, axis=2) + jnp.roll(field, -width, axis=2)
    beside = beside + yplus + yminus
    before = jnp.pad(field, ((1, 0), (0, 0), (0, 0)))[:-1]
    return 1.0 * (field - before) + (6.0 * field - beside) / 16.0 + react * coarse_coef * field


def coarse_solve(coarse_rhs, coarse_coef):
    theta = 0.8
    delta = 0.6
    diag = 1.375 + react * coarse_coef
    sol = jnp.zeros_like(coarse_rhs)
    resid = coarse_rhs
    step_dir = resid / (diag * theta)
    rho = delta / theta
    for step in range(CHEB):
        sol = sol + step_dir
        if step + 1 < CHEB:
            resid = resid - coarse_apply(step_dir, coarse_coef)
            rho_next = 1.0 / (2.0 * theta / delta - rho)
            step_dir = rho_next * rho * step_dir + 2.0 * rho_next / delta * (resid / diag)
            rho = rho_next
    return sol


def local(right_side, state):
    coef = 3.0 * state * state - 1.0
    slab = lax.axis_index("tm")
    plane = lax.axis_index("space")
    stacked = jnp.stack([right_side, coef])
    widened = extended(stacked, (("space", 2),), OV)
    earlier = passed_along(widened[:, CT - OT :], "tm", 1)
    region = jnp.concatenate([earlier, widened], axis=1)
    first = (slab > 0).astype(jnp.float32)
    tmask = jnp.concatenate([jnp.zeros((OT,), jnp.float32) + first, jnp.ones((CT,), jnp.float32)])
    field = sweep_block(region[0], region[1], tmask)
    local_part = field[OT:, OV : OV + CZ]
    padded_z = extended(local_part, (("space", 1),), 1)
    last_prev = passed_along(local_part[CT - 1 :], "tm", 1)
    before = jnp.concatenate([last_prev, local_part[:-1]], axis=0)
    applied = (
        (rate + 6.0 + react * coef) * local_part - rate * before - spatial_sum(padded_z, local_part)
    )
    after = right_side - applied
    flat = CX // 4 * (CY // 4)
    both = jnp.stack([after, coef]).reshape(2, CT, CZ // 4, 4, CX // 4, 4, CY // 4, 4)
    partial_sums = jnp.sum(both, axis=(1, 3, 5, 7)).reshape(2, CZ // 4, flat)
    coarse_steps_all = lax.axis_size("tm") * CT // 8
    coarse_planes_all = lax.axis_size("space") * CZ // 4
    slot = slab // (8 // CT)
    row = plane * (CZ // 4)
    zero = jnp.int32(0)
    padded = jnp.zeros((2, coarse_steps_all, coarse_planes_all, flat), jnp.float32)
    padded = lax.dynamic_update_slice(padded, partial_sums[:, None], (zero, slot, row, zero))
    totals = lax.psum(padded, ("tm", "space"))
    coarse = totals * (1.0 / 512.0)
    coarse_solution = coarse_solve(coarse[0], coarse[1])
    mine = lax.dynamic_slice(coarse_solution, (slot, row, zero), (1, CZ // 4, flat))
    spread = mine.reshape(1, CZ // 4, 1, CX // 4, 1, CY // 4, 1)
    spread = jnp.broadcast_to(spread, (CT, CZ // 4, 4, CX // 4, 4, CY // 4, 4)).reshape(
        CT, CZ, CX, CY
    )
    return local_part + spread


def solution(mesh):
    return jax.shard_map(
        local,
        mesh=mesh,
        in_specs=(P("tm", "space", None, None), P("tm", "space", None, None)),
        out_specs=P("tm", "space", None, None),
        check_vma=False,
    )
```

profile of v0, /device:TPU:6, one launch (start us, length us, event | category | flops | bytes accessed | tf_op | source)
XLA Modules:
  0.0 567.8 jit_solution(17794626226258929773)
XLA Ops:
  6.5 1.0 fusion.139
  7.6 0.9 pad_maximum_fusion.6
  8.5 1.9 collective-permute-start
  10.4 5.8 %collective-permute-start.1 = (f32[2,4,2,16,128]{4,3,2,1,0:T(8,128)S(1)}, f32[2,4,2,16,128]{4,3,2,1,0:T(8,128)S(1)}, u32[]{:S(2)}, u32[]{:S(2)}) collective-permute-start(f32[2,4,2,16,128]{4,3,2,1,0:T(8,128)S(1)} %get-tuple-element.56), channel_id=1, source_target_pairs={{1,0},{2,1},{3,2},{4,3},{5,4},{6,5},{7,6},{8,7},{9,8},{10,9},{11,1... | collective-permute-start | bytes 393224 | tf_op jit(solution)/shard_map/ppermute | solution.py:29
  16.2 0.7 collective-permute-done
  16.9 1.8 collective-permute-done.1
  18.7 3.8 collective-permute-start.2
  22.6 8.1 %collective-permute-done.2 = f32[2,2,12,16,128]{4,3,2,1,0:T(8,128)S(1)} collective-permute-done((f32[2,2,12,16,128]{4,3,2,1,0:T(8,128)S(1)}, f32[2,2,12,16,128]{4,3,2,1,0:T(8,128)S(1)}, u32[]{:S(2)}, u32[]{:S(2)}) %collective-permute-start.2) | collective-permute-done | bytes 393248 | tf_op jit(solution)/shard_map/ppermute | solution.py:37
  31.8 0.6 fusion.50
  33.0 0.6 fusion.49
  34.2 0.6 fusion.48
  35.2 4.4 collective-permute-start.3
  39.6 3.5 collective-permute-start.4
  43.1 1.9 collective-permute-start.5
  45.2 5.3 collective-permute-done.5
  50.8 10.1 %stack.21 = f32[1,4,2,4,4,4,32,4]{7,6,5,4,3,2,1,0:T(8,128)} reshape(f32[4,8,16,128]{3,2,1,0:T(8,128)S(1)} %get-tuple-element.169) | data formatting | bytes 524288 | tf_op jit(solution)/shard_map/stack | solution.py:112
  60.9 5.9 %copy.3 = f32[1,4,2,4,4,4,32,4]{6,7,5,4,3,2,1,0:T(4,128)S(1)} copy(f32[1,4,2,4,4,4,32,4]{7,6,5,4,3,2,1,0:T(8,128)} %stack.21) | data formatting | bytes 524288 | tf_op jit(solution)/shard_map/stack | solution.py:112
  66.8 10.1 %stack.22 = f32[1,4,2,4,4,4,32,4]{7,6,5,4,3,2,1,0:T(8,128)} reshape(f32[4,8,16,128]{3,2,1,0:T(8,128)S(1)} %get-tuple-element.170) | data formatting | bytes 524288 | tf_op jit(solution)/shard_map/stack | solution.py:112
  76.9 6.1 %copy.4 = f32[1,4,2,4,4,4,32,4]{6,7,5,4,3,2,1,0:T(4,128)S(1)} copy(f32[1,4,2,4,4,4,32,4]{7,6,5,4,3,2,1,0:T(8,128)} %stack.22) | data formatting | bytes 524288 | tf_op jit(solution)/shard_map/stack | solution.py:112
  82.9 0.7 maximum_reduce_fusion
  83.8 0.8 copy-done.1
  84.6 461.8 %all-reduce.20.cloned.1.call-done = f32[2,8,64,128]{3,2,1,0:T(8,128)} async-done(((f32[2,8,64,128]{3,2,1,0:T(8,128)}), f32[2,8,64,128]{3,2,1,0:T(8,128)}) %all-reduce.20.cloned.1.call-update) | async-done | bytes 524304 | tf_op jit(solution)/shard_map/psum | solution.py:121
  546.4 1.1 broadcast_multiply_fusion
  548.5 0.7 fusion.145
  550.1 0.6 multiply_add_fusion.4
  551.6 0.6 multiply_add_fusion.3
  553.1 0.6 multiply_add_fusion.2
  554.6 0.6 multiply_add_fusion.1
  556.0 0.7 fusion.129
  557.7 0.5 fusion.76
  558.6 1.6 broadcast_in_dim.70
  560.3 0.7 broadcast_add_fusion
  (104 shorter events, 9.5 us)
Async XLA Ops:
  6.5 12.1 %copy-start = (f32[4,8,16,128]{3,2,1,0:T(8,128)S(1)}, f32[4,8,16,128]{3,2,1,0:T(8,128)}, u32[]{:S(2)}) copy-start(f32[4,8,16,128]{3,2,1,0:T(8,128)} %param.2) | copy-start | bytes 786436
  6.5 539.9 %all-reduce.20.cloned.1.call-start = ((), (), s32[]{:S(2)}) async-start(), calls=%async_computation | async-start | bytes 1048576 | tf_op jit(solution)/shard_map/psum | solution.py:121
  8.5 8.4 %collective-permute-start = (f32[2,4,2,16,128]{4,3,2,1,0:T(8,128)S(1)}, f32[2,4,2,16,128]{4,3,2,1,0:T(8,128)S(1)}, u32[]{:S(2)}, u32[]{:S(2)}) collective-permute-start(f32[2,4,2,16,128]{4,3,2,1,0:T(8,128)S(1)} %get-tuple-element.55), channel_id=1, source_target_pairs={{0,1},{1,2},{2,3},{3,4},{4,5},{5,6},{6,7},{7,8},{8,9},{9,10},{10,1... | collective-permute-start | bytes 393224 | tf_op jit(solution)/shard_map/ppermute | solution.py:28
  10.4 8.3 %collective-permute-start.1 = (f32[2,4,2,16,128]{4,3,2,1,0:T(8,128)S(1)}, f32[2,4,2,16,128]{4,3,2,1,0:T(8,128)S(1)}, u32[]{:S(2)}, u32[]{:S(2)}) collective-permute-start(f32[2,4,2,16,128]{4,3,2,1,0:T(8,128)S(1)} %get-tuple-element.56), channel_id=1, source_target_pairs={{1,0},{2,1},{3,2},{4,3},{5,4},{6,5},{7,6},{8,7},{9,8},{10,9},{11,1... | collective-permute-start | bytes 393224 | tf_op jit(solution)/shard_map/ppermute | solution.py:29
  18.7 12.1 %collective-permute-start.2 = (f32[2,2,12,16,128]{4,3,2,1,0:T(8,128)S(1)}, f32[2,2,12,16,128]{4,3,2,1,0:T(8,128)S(1)}, u32[]{:S(2)}, u32[]{:S(2)}) collective-permute-start(f32[2,2,12,16,128]{4,3,2,1,0:T(8,128)S(1)} %pad_maximum_fusion), channel_id=1, source_target_pairs={{0,32},{32,64},{64,96},{96,128},{128,160},{160,192},{192,224},{224... | collective-permute-start | bytes 1179656 | tf_op jit(solution)/shard_map/ppermute | solution.py:37
  35.2 15.3 %copy-start.2 = (f32[4,8,16,128]{3,2,1,0:T(8,128)S(1)}, f32[4,8,16,128]{3,2,1,0:T(8,128)}, u32[]{:S(2)}) copy-start(f32[4,8,16,128]{3,2,1,0:T(8,128)} %param.3) | copy-start | bytes 786436
  35.2 15.2 %collective-permute-start.3 = (f32[1,8,16,128]{3,2,1,0:T(8,128)S(1)}, f32[1,8,16,128]{3,2,1,0:T(8,128)S(1)}, u32[]{:S(2)}, u32[]{:S(2)}) collective-permute-start(f32[1,8,16,128]{3,2,1,0:T(8,128)S(1)} %slice.795), channel_id=1, source_target_pairs={{0,32},{32,64},{64,96},{96,128},{128,160},{160,192},{192,224},{224... | collective-permute-start | bytes 196616 | tf_op jit(solution)/shard_map/ppermute | solution.py:37
  39.6 5.5 collective-permute-start.4
  43.1 7.3 %collective-permute-start.5 = (f32[4,1,16,128]{3,2,1,0:T(8,128)S(1)}, f32[4,1,16,128]{3,2,1,0:T(8,128)S(1)}, u32[]{:S(2)}, u32[]{:S(2)}) collective-permute-start(f32[4,1,16,128]{3,2,1,0:T(8,128)S(1)} %get-tuple-element.28), channel_id=1, source_target_pairs={{0,1},{1,2},{2,3},{3,4},{4,5},{5,6},{6,7},{7,8},{8,9},{9,10},{10,1... | collective-permute-start | bytes 98312 | tf_op jit(solution)/shard_map/ppermute | solution.py:28
  83.8 0.8 copy-start.1
Sparse Core Ops, SparseCore 0:
  84.7 461.6 all-reduce.19
where the time goes:
time: 569 us; the launch traced here: 568 us
  waiting for transfers between devices  478 us (84%)
  local copies, waits for them, and re-layouts  43.2 us (8%)
  starting transfers between devices  21.3 us (4%)
  between operations  14.2 us (2%)
  other arithmetic  11.3 us (2%)
    psum x1, waiting for transfers between devices, local(): totals = lax.psum(padded, ('tm', 'space'))  462 us
    another operation x4, local copies, waits for them, and re-layouts, local(): jnp.stack([after, coef]).reshape(2, CT, CZ // 4, 4, CX // 4, 4, CY // 4, 4)  32.1 us
  transfers between devices with their start and end apart: 7, of which 5 were waited for; matrix products, arithmetic and copies ran while one was open for 0% of the time, Pallas kernels for 0%

commit v1 on v0

v1 whole, which is shorter than its diff:
```python
import functools

import jax
import jax.numpy as jnp
from jax import lax
from jax.experimental import pallas as pl
from jax.experimental.pallas import tpu as pltpu
from jax.sharding import PartitionSpec as P

CX = 16
CY = 128
CT = 4
CZ = 8
OV = 2
SWEEPS = 4
CHEB = 8
LANES = 128
SLOTS = 8
NEAR = 4
GROUP = 2 * NEAR

rate = 8.0
react = 0.5
damp = 0.9
theta = 0.8
delta = 0.6

F32 = jnp.float32
PLANE = (CX, CY)
VMEM = pl.BlockSpec(memory_space=pltpu.VMEM)
SMEM = pl.BlockSpec(memory_space=pltpu.SMEM)


def params():
    return pltpu.CompilerParams(vmem_limit_bytes=32 * 1024 * 1024)


def beside(v):
    total = pltpu.roll(v, 1, 0) + pltpu.roll(v, CX - 1, 0)
    return total + (pltpu.roll(v, 1, 1) + pltpu.roll(v, CY - 1, 1))


def swept(v, first, scale, near, before):
    total = beside(v)
    for plane in near:
        if plane is not None:
            total = total + plane
    if before is not None:
        total = total + rate * before
    return (1.0 - damp) * v + first + scale * total


def first_kernel(rhs_ref, state_ref, both_ref, up_ref, down_ref):
    for t in range(CT):
        for z in range(CZ):
            s = state_ref[t, z]
            diag = (rate + 6.0 - react) + (3.0 * react) * (s * s)
            scale = damp / diag
            first = scale * rhs_ref[t, z]
            both_ref[0, t, z] = scale
            both_ref[1, t, z] = first
            if z >= CZ - OV:
                up_ref[0, t, z - (CZ - OV)] = scale
                up_ref[1, t, z - (CZ - OV)] = first
            if z < OV:
                down_ref[0, t, z] = scale
                down_ref[1, t, z] = first


def reader(which, both_ref, low_ref, high_ref):
    def read(t, z):
        if z < 0:
            return low_ref[which, t, z + OV]
        if z >= CZ:
            return high_ref[which, t, z - CZ]
        return both_ref[which, t, z]

    return read


def later_kernel(both_ref, low_ref, high_ref, out_ref):
    scale = reader(0, both_ref, low_ref, high_ref)
    first = reader(1, both_ref, low_ref, high_ref)
    a, b = CT - 2, CT - 1
    off2 = CZ
    off1 = off2 + CZ + 2
    for z in range(-2, CZ + 2):
        out_ref[off1 + z + 2] = first(b, z)
    for z in range(-1, CZ + 1):
        v = first(b, z)
        out_ref[off2 + z + 1] = swept(
            v, v, scale(b, z), (first(b, z - 1), first(b, z + 1)), first(a, z)
        )
    for z in range(CZ):
        v = first(a, z)
        second = swept(v, v, scale(a, z), (first(a, z - 1), first(a, z + 1)), None)
        out_ref[z] = swept(
            out_ref[off2 + z + 1],
            first(b, z),
            scale(b, z),
            (out_ref[off2 + z], out_ref[off2 + z + 2]),
            second,
        )


def fold_matrix(rows, columns, fine_first):
    i = lax.broadcasted_iota(jnp.int32, (rows, columns), 0)
    k = lax.broadcasted_iota(jnp.int32, (rows, columns), 1)
    fine, lane = (i, k) if fine_first else (k, i)
    return jnp.where(lax.shift_right_logical(fine, 2) == (lane & (CY // 4 - 1)), 1.0, 0.0)


def x_mask():
    x = lax.broadcasted_iota(jnp.int32, PLANE, 0)
    lane = lax.broadcasted_iota(jnp.int32, PLANE, 1)
    return jnp.where(lax.shift_right_logical(x, 2) == lax.shift_right_logical(lane, 5), 1.0, 0.0)


def main_kernel(
    rhs_ref, state_ref, both_ref, low_ref, high_ref, prev_ref, lp_ref, sums_ref, v2, v3, stack
):
    scale = reader(0, both_ref, low_ref, high_ref)
    own = reader(1, both_ref, low_ref, high_ref)
    off2 = CZ
    off1 = off2 + CZ + 2

    def first(t, z):
        return prev_ref[off1 + z + 2] if t < 0 else own(t, z)

    def second(t, z):
        return prev_ref[off2 + z + 1] if t < 0 else v2[t, z + 2]

    def third(t, z):
        return prev_ref[z] if t < 0 else v3[t, z + 1]

    for t in range(CT):
        for z in range(-2, CZ + 2):
            v = own(t, z)
            near = [own(t, q) for q in (z - 1, z + 1) if -2 <= q < CZ + 2]
            v2[t, z + 2] = swept(v, v, scale(t, z), near, first(t - 1, z))
        for z in range(-1, CZ + 1):
            near = (second(t, z - 1), second(t, z + 1))
            v3[t, z + 1] = swept(second(t, z), own(t, z), scale(t, z), near, second(t - 1, z))
        for z in range(CZ):
            near = (third(t, z - 1), third(t, z + 1))
            lp_ref[t, z] = swept(third(t, z), own(t, z), scale(t, z), near, third(t - 1, z))

    rest = []
    planes = []
    coefs = []
    for z in range(CZ):
        part = None
        square = None
        for t in range(CT):
            s = state_ref[t, z]
            q = s * s
            diag = (rate + 6.0 - react) + (3.0 * react) * q
            term = rhs_ref[t, z] - diag * lp_ref[t, z]
            part = term if part is None else part + term
            square = q if square is None else square + q
        early = lp_ref[0, z]
        for t in range(1, CT - 1):
            early = early + lp_ref[t, z]
        rest.append(part + rate * early)
        planes.append(early + lp_ref[CT - 1, z])
        coefs.append(3.0 * square - float(CT))
    for b in range(2):
        z = 4 * b
        total = planes[z] + planes[z + 1] + planes[z + 2] + planes[z + 3]
        inner = planes[z] + planes[z + 3] + 2.0 * (planes[z + 1] + planes[z + 2])
        inner = inner + (planes[4] if b == 0 else planes[3])
        value = rest[z] + rest[z + 1] + rest[z + 2] + rest[z + 3]
        stack[b] = value + beside(total) + inner
        last = lp_ref[CT - 1, z] + lp_ref[CT - 1, z + 1]
        last = last + (lp_ref[CT - 1, z + 2] + lp_ref[CT - 1, z + 3])
        stack[4 + b] = rate * last
        stack[6 + b] = coefs[z] + coefs[z + 1] + coefs[z + 2] + coefs[z + 3]
    stack[2] = planes[0]
    stack[3] = planes[CZ - 1]
    folded = jnp.dot(
        stack[...].reshape(8 * CX, CY),
        fold_matrix(CY, LANES, True),
        precision=lax.Precision.HIGHEST,
        preferred_element_type=F32,
    )
    sums = jnp.sum(folded.reshape(8, CX, LANES) * x_mask()[None], axis=1)
    sums_ref[...] = jnp.broadcast_to(sums[None], sums_ref.shape)


def slots_kernel(all_ref, out_ref):
    def row(r):
        return all_ref[:, 0, r, :] + all_ref[:, 1, r, :]

    slot = lax.broadcasted_iota(jnp.int32, (SLOTS, LANES), 0)
    rows = []
    for b in range(2):
        odd = jnp.where(slot == 0, 0.0, pltpu.roll(all_ref[:, 1, 4 + b, :], 1, 0))
        rows.append(row(b) + all_ref[:, 0, 4 + b, :] + odd)
    rows += [row(2), row(3), row(6), row(7)]
    for r, value in enumerate(rows):
        value = value * (1.0 / 512.0)
        for k in range(out_ref.shape[0]):
            out_ref[k, r] = value


def coarse_kernel(at_ref, lp_ref, here_ref, beside_ref, out_ref, found):
    index = at_ref[0]
    slot = at_ref[1]
    place = index & (GROUP - 1)
    late = place >= NEAR
    start = place & (NEAR - 1)
    devices = 3 * NEAR
    low = [beside_ref[k] for k in range(NEAR)]
    parts = []
    for k in range(devices):
        early_part = beside_ref[k] if k < NEAR else here_ref[k - NEAR]
        late_part = here_ref[k] if k < GROUP else beside_ref[k - NEAR]
        parts.append(jnp.where(late, late_part, early_part))
    n = 2 * devices
    rhs = []
    diag = []
    for k in range(devices):
        a0, a1, c0, c1 = parts[k][0], parts[k][1], parts[k][4], parts[k][5]
        if k > 0:
            a0 = a0 + parts[k - 1][3]
        if k + 1 < devices:
            a1 = a1 + parts[k + 1][2]
        rhs += [a0, a1]
        diag += [1.375 + react * c0, 1.375 + react * c1]
    lane = lax.broadcasted_iota(jnp.int32, (SLOTS, LANES), 1) & (CY // 4 - 1)
    slots = lax.broadcasted_iota(jnp.int32, (SLOTS, LANES), 0)
    width = CY // 4
    is_first, is_last, is_start = lane == 0, lane == width - 1, slots == 0

    def around(f):
        total = pltpu.roll(f, width, 1) + pltpu.roll(f, LANES - width, 1)
        after = jnp.where(is_last, pltpu.roll(f, width - 1, 1), pltpu.roll(f, LANES - 1, 1))
        before = jnp.where(is_first, pltpu.roll(f, LANES - width + 1, 1), pltpu.roll(f, 1, 1))
        return total + (after + before)

    def earlier(f):
        return jnp.where(is_start, 0.0, pltpu.roll(f, 1, 0))

    inverse = [1.0 / d for d in diag]
    resid = [r * i for r, i in zip(rhs, inverse)]
    step = [r * (1.0 / theta) for r in resid]
    mine = range(2 * NEAR, 4 * NEAR)
    sol = {r: step[r] for r in mine}
    rho = delta / theta
    for k in range(1, CHEB):
        nxt = 1.0 / (2.0 * theta / delta - rho)
        new_resid = list(resid)
        new_step = list(step)
        for r in range(1 + k, n - 1 - k):
            spread = around(step[r]) + (step[r - 1] + step[r + 1])
            flow = earlier(step[r]) + spread * (1.0 / 16.0)
            new_resid[r] = resid[r] - step[r] + flow * inverse[r]
            new_step[r] = (nxt * rho) * step[r] + (2.0 * nxt / delta) * new_resid[r]
        resid, step, rho = new_resid, new_step, nxt
        for r in mine:
            sol[r] = sol[r] + step[r]
    for r in mine:
        found[r - 2 * NEAR] = sol[r]
    mask = x_mask()
    spread = [found[2 * start + b, pl.ds(slot, 1), :] * mask for b in range(2)]
    fine = jnp.dot(
        jnp.concatenate(spread, axis=0),
        fold_matrix(LANES, CY, False),
        precision=lax.Precision.HIGHEST,
        preferred_element_type=F32,
    )
    for b in range(2):
        value = fine[b * CX : (b + 1) * CX]
        for t in range(CT):
            for z in range(4):
                out_ref[t, 4 * b + z] = lp_ref[t, 4 * b + z] + value


def call(kernel, shapes, n_in, scratch=(), smem=0):
    single = not isinstance(shapes, (list, tuple))
    outs = [shapes] if single else list(shapes)
    specs = [VMEM] * len(outs)
    return pl.pallas_call(
        kernel,
        out_shape=shapes if single else outs,
        in_specs=[SMEM] * smem + [VMEM] * n_in,
        out_specs=VMEM if single else specs,
        scratch_shapes=list(scratch),
        compiler_params=params(),
    )


def arr(*shape):
    return jax.ShapeDtypeStruct(shape, F32)


def local(right_side, state):
    slabs = lax.axis_size("tm")
    planes = lax.axis_size("space")
    slab = lax.axis_index("tm")
    plane = lax.axis_index("space")
    up = [(i, (i + 1) % planes) for i in range(planes)]
    down = [(j, i) for i, j in up]
    onward = [(i, i + 1) for i in range(slabs - 1)]

    edge = arr(2, CT, OV, CX, CY)
    both, top, bottom = call(first_kernel, [arr(2, CT, CZ, CX, CY), edge, edge], 2)(
        right_side, state
    )
    low = lax.ppermute(top, "space", up)
    high = lax.ppermute(bottom, "space", down)
    count = 3 * CZ + 6
    sent = call(later_kernel, arr(count, CX, CY), 3)(both, low, high)
    prev = lax.ppermute(sent, "tm", onward)
    lp, sums = call(
        main_kernel,
        [arr(CT, CZ, CX, CY), arr(slabs, 8, LANES)],
        6,
        [
            pltpu.VMEM((CT, CZ + 4, CX, CY), F32),
            pltpu.VMEM((CT, CZ + 2, CX, CY), F32),
            pltpu.VMEM((8, CX, CY), F32),
        ],
    )(right_side, state, both, low, high, prev)
    every = lax.all_to_all(sums, "tm", 0, 0)
    slots = call(slots_kernel, arr(GROUP, 6, SLOTS, LANES), 1)(
        every.reshape(slabs // 2, 2, 8, LANES)
    )
    groups = [[GROUP * g + k for k in range(GROUP)] for g in range(planes // GROUP)]
    shifted = [[(q + NEAR) % planes for q in group] for group in groups]
    here = lax.all_to_all(slots, "space", 0, 0, axis_index_groups=groups)
    other = lax.all_to_all(slots, "space", 0, 0, axis_index_groups=shifted)
    at = jnp.stack([plane, slab // 2]).astype(jnp.int32)
    return call(
        coarse_kernel,
        arr(CT, CZ, CX, CY),
        3,
        [pltpu.VMEM((2 * NEAR, SLOTS, LANES), F32)],
        smem=1,
    )(at, lp, here, other)


def solution(mesh):
    return jax.shard_map(
        local,
        mesh=mesh,
        in_specs=(P("tm", "space", None, None), P("tm", "space", None, None)),
        out_specs=P("tm", "space", None, None),
        check_vma=False,
    )
```

time: 569 us -> 77.7 us (0.14)
  waiting for transfers between devices: 478 us -> 14.3 us
  local copies, waits for them, and re-layouts: 43.2 us -> 1.9 us
  blocking collectives: 0 us -> 39.2 us
  between operations: 14.2 us -> 0.05 us
  other arithmetic: 11.3 us -> 0.07 us
    psum x1 -> x0, waiting for transfers between devices: 462 us -> none  [local(): totals = lax.psum(padded, ('tm', 'space'))]
    all_to_all x0 -> x2, blocking collectives: none -> 39.2 us  [the longest x1 29.6 us: local(): every = lax.all_to_all(sums, 'tm', 0, 0)]
    another operation x5 -> x0, local copies, waits for them, and re-layouts: 32.2 us -> none  [the longest x4 32.1 us: local(): jnp.stack([after, coef]).reshape(2, CT, CZ // 4, 4, CX // 4, 4, CY // 4, 4)]
    ppermute x6 -> x3, starting transfers between devices: 21.3 us -> 11.5 us  [the longest x1 5.75 us: local(): high = lax.ppermute(bottom, 'space', down)]
    ppermute x6 -> x3, waiting for transfers between devices: 15.9 us -> 7.55 us  [the longest x1 5.05 us: local(): prev = lax.ppermute(sent, 'tm', onward)]
    slice x78 -> x0, local copies, waits for them, and re-layouts: 8.05 us -> none  [the longest x12 1.62 us: coarse_apply(): jnp.roll(field, -1, axis=-1)]
    all_to_all x0 -> x1, waiting for transfers between devices: none -> 6.76 us  [local(): here = lax.all_to_all(slots, 'space', 0, 0, axis_index_groups=groups)]
    all_to_all x0 -> x1, starting transfers between devices: none -> 6.08 us  [local(): here = lax.all_to_all(slots, 'space', 0, 0, axis_index_groups=groups)]
  transfers between devices with their start and end apart: 7 -> 4, of which waited for: 5 -> 4; matrix products, arithmetic and copies ran while one was open for 0% -> 0% of each run, Pallas kernels for 0% -> 0%
where the time goes in v1:
time: 77.7 us; the launch traced here: 77.3 us
  blocking collectives  39.2 us (50%)
  starting transfers between devices  17.6 us (23%)
  waiting for transfers between devices  14.3 us (18%)
  Pallas kernels  4.18 us (5%)
  local copies, waits for them, and re-layouts  1.9 us (2%)
    all_to_all x1, blocking collectives, local(): every = lax.all_to_all(sums, 'tm', 0, 0)  29.6 us
    all_to_all x1, blocking collectives, local(): other = lax.all_to_all(slots, 'space', 0, 0, axis_index_groups=shifted)  9.57 us
    all_to_all x1, waiting for transfers between devices, local(): here = lax.all_to_all(slots, 'space', 0, 0, axis_index_groups=groups)  6.76 us
    all_to_all x1, starting transfers between devices, local(): here = lax.all_to_all(slots, 'space', 0, 0, axis_index_groups=groups)  6.08 us
    ppermute x1, starting transfers between devices, local(): high = lax.ppermute(bottom, 'space', down)  5.75 us
    ppermute x1, waiting for transfers between devices, local(): prev = lax.ppermute(sent, 'tm', onward)  5.05 us
    ppermute x1, starting transfers between devices, local(): prev = lax.ppermute(sent, 'tm', onward)  3.84 us
    pallas_call x1, Pallas kernels, local(): call(coarse_kernel, arr(CT, CZ, CX, CY), 3, [pltpu.VMEM((2 * NEAR, SLOTS,...  2.26 us
  transfers between devices with their start and end apart: 4, of which 4 were waited for; matrix products, arithmetic and copies ran while one was open for 0% of the time, Pallas kernels for 0%

profile of v1, /device:TPU:6, one launch (start us, length us, event | category | flops | bytes accessed | tf_op | source)
XLA Modules:
  0.0 77.3 jit_solution(9116786948548253636)
XLA Ops:
  0.0 0.0 copy-start
  0.0 0.9 %copy-done = f32[4,8,16,128]{3,2,1,0:T(8,128)S(1)} copy-done((f32[4,8,16,128]{3,2,1,0:T(8,128)S(1)}, f32[4,8,16,128]{3,2,1,0:T(8,128)}, u32[]{:S(2)}) %copy-start) | copy-done | bytes 262168
  1.0 0.0 copy-start.1
  1.0 0.9 %copy-done.1 = f32[4,8,16,128]{3,2,1,0:T(8,128)S(1)} copy-done((f32[4,8,16,128]{3,2,1,0:T(8,128)S(1)}, f32[4,8,16,128]{3,2,1,0:T(8,128)}, u32[]{:S(2)}) %copy-start.1) | copy-done | bytes 262168
  1.9 0.1 shard_map.28
  2.0 1.9 %collective-permute-start = (f32[2,4,2,16,128]{4,3,2,1,0:T(8,128)S(1)}, f32[2,4,2,16,128]{4,3,2,1,0:T(8,128)S(1)}, u32[]{:S(2)}, u32[]{:S(2)}) collective-permute-start(f32[2,4,2,16,128]{4,3,2,1,0:T(8,128)S(1)} %get-tuple-element.11), channel_id=1, source_target_pairs={{0,1},{1,2},{2,3},{3,4},{4,5},{5,6},{6,7},{7,8},{8,9},{9,10},{10,1... | collective-permute-start | bytes 393224 | tf_op jit(solution)/shard_map/ppermute | solution.py:310
  3.9 5.8 %collective-permute-start.1 = (f32[2,4,2,16,128]{4,3,2,1,0:T(8,128)S(1)}, f32[2,4,2,16,128]{4,3,2,1,0:T(8,128)S(1)}, u32[]{:S(2)}, u32[]{:S(2)}) collective-permute-start(f32[2,4,2,16,128]{4,3,2,1,0:T(8,128)S(1)} %get-tuple-element.12), channel_id=1, source_target_pairs={{1,0},{2,1},{3,2},{4,3},{5,4},{6,5},{7,6},{8,7},{9,8},{10,9},{11,1... | collective-permute-start | bytes 393224 | tf_op jit(solution)/shard_map/ppermute | solution.py:311
  9.7 0.7 collective-permute-done.low_ref
  10.4 1.8 %collective-permute-done.1.high_ref = f32[2,4,2,16,128]{4,3,2,1,0:T(8,128)S(1)} collective-permute-done((f32[2,4,2,16,128]{4,3,2,1,0:T(8,128)S(1)}, f32[2,4,2,16,128]{4,3,2,1,0:T(8,128)S(1)}, u32[]{:S(2)}, u32[]{:S(2)}) %collective-permute-start.1) | collective-permute-done | bytes 131104 | tf_op jit(solution)/shard_map/ppermute | solution.py:311
  12.2 0.0 copy-start.2
  12.2 0.2 shard_map.29
  12.4 3.8 %collective-permute-start.2 = (f32[30,16,128]{2,1,0:T(8,128)S(1)}, f32[30,16,128]{2,1,0:T(8,128)S(1)}, u32[]{:S(2)}, u32[]{:S(2)}) collective-permute-start(f32[30,16,128]{2,1,0:T(8,128)S(1)} %shard_map.29), channel_id=1, source_target_pairs={{0,32},{32,64},{64,96},{96,128},{128,160},{160,192},{192,224},{224... | collective-permute-start | bytes 737288 | tf_op jit(solution)/shard_map/ppermute | solution.py:314
  16.2 5.1 %collective-permute-done.2.prev_ref = f32[30,16,128]{2,1,0:T(8,128)S(1)} collective-permute-done((f32[30,16,128]{2,1,0:T(8,128)S(1)}, f32[30,16,128]{2,1,0:T(8,128)S(1)}, u32[]{:S(2)}, u32[]{:S(2)}) %collective-permute-start.2) | collective-permute-done | bytes 245792 | tf_op jit(solution)/shard_map/ppermute | solution.py:314
  21.2 0.0 copy-done.2
  21.3 0.9 %shard_map.30 = (f32[4,8,16,128]{3,2,1,0:T(8,128)S(1)}, f32[16,8,128]{2,1,0:T(8,128)S(1)}) custom-call(f32[4,8,16,128]{3,2,1,0:T(8,128)S(1)} %copy-done, f32[4,8,16,128]{3,2,1,0:T(8,128)S(1)} %copy-done.2, f32[2,4,8,16,128]{4,3,2,1,0:T(8,128)S(1)} %get-tuple-element.10.both_ref, f32[2,4,2,16,128]{4,3,2,1,0:T(8,128)S(1)} %collective-permute-done.low_ref, ...), custom_call_target="tpu_custom_call" | custom-call | tf_op jit(solution)/shard_map/pallas_call | solution.py:315
  22.2 29.6 %all_to_all.15 = f32[16,8,128]{2,1,0:T(8,128)S(1)} all-to-all(f32[16,8,128]{2,1,0:T(8,128)S(1)} %get-tuple-element.14), channel_id=1, replica_groups=mesh['tm'=16,'space'=32] {'tm'}, dimensions={0} | all-to-all | bytes 131072 | tf_op jit(solution)/shard_map/all_to_all | solution.py:325
  51.8 0.7 shard_map.31
  52.5 9.6 %all_to_all.16.beside_ref = f32[8,6,8,128]{3,2,1,0:T(8,128)S(1)} all-to-all(f32[8,6,8,128]{3,2,1,0:T(8,128)} %shard_map.31), channel_id=1, replica_groups={{4,5,6,7,8,9,10,11},{12,13,14,15,16,17,18,19},{20,21,22,23,24,25,26,27}..., dimensions={0} | all-to-all | bytes 393216 | tf_op jit(solution)/shard_map/all_to_all | solution.py:332
  62.1 6.1 %all-to-all-start.1 = ((f32[8,6,8,128]{3,2,1,0:T(8,128)}), f32[8,6,8,128]{3,2,1,0:T(8,128)S(1)}, u32[]{:S(2)}, u32[]{:S(2)}) async-start(f32[8,6,8,128]{3,2,1,0:T(8,128)} %shard_map.31), calls=%async_computation.1 | async-start | bytes 393216 | tf_op jit(solution)/shard_map/all_to_all | solution.py:331
  68.2 0.1 pad_add_fusion.at_ref
  68.3 6.8 %all-to-all-done.1.here_ref = f32[8,6,8,128]{3,2,1,0:T(8,128)S(1)} async-done(((f32[8,6,8,128]{3,2,1,0:T(8,128)}), f32[8,6,8,128]{3,2,1,0:T(8,128)S(1)}, u32[]{:S(2)}, u32[]{:S(2)}) %all-to-all-start.1) | async-done | bytes 196640 | tf_op jit(solution)/shard_map/all_to_all | solution.py:331
  75.0 2.3 %shard_map.32 = f32[4,8,16,128]{3,2,1,0:T(8,128)} custom-call(s32[2]{0:T(128)S(1)} %pad_add_fusion.at_ref, f32[4,8,16,128]{3,2,1,0:T(8,128)S(1)} %get-tuple-element.13.lp_ref, f32[8,6,8,128]{3,2,1,0:T(8,128)S(1)} %all-to-all-done.1.here_ref, f32[8,6,8,128]{3,2,1,0:T(8,128)S(1)} %all_to_all.16.beside_ref), custom_call_target="tpu_custom_call" | custom-call | tf_op jit(solution)/shard_map/pallas_call | solution.py:334
Async XLA Ops:
  0.0 0.9 %copy-start = (f32[4,8,16,128]{3,2,1,0:T(8,128)S(1)}, f32[4,8,16,128]{3,2,1,0:T(8,128)}, u32[]{:S(2)}) copy-start(f32[4,8,16,128]{3,2,1,0:T(8,128)} %rhs_ref.3) | copy-start | bytes 786436
  1.0 0.9 %copy-start.1 = (f32[4,8,16,128]{3,2,1,0:T(8,128)S(1)}, f32[4,8,16,128]{3,2,1,0:T(8,128)}, u32[]{:S(2)}) copy-start(f32[4,8,16,128]{3,2,1,0:T(8,128)} %state_ref.3) | copy-start | bytes 786436
  2.0 8.4 %collective-permute-start = (f32[2,4,2,16,128]{4,3,2,1,0:T(8,128)S(1)}, f32[2,4,2,16,128]{4,3,2,1,0:T(8,128)S(1)}, u32[]{:S(2)}, u32[]{:S(2)}) collective-permute-start(f32[2,4,2,16,128]{4,3,2,1,0:T(8,128)S(1)} %get-tuple-element.11), channel_id=1, source_target_pairs={{0,1},{1,2},{2,3},{3,4},{4,5},{5,6},{6,7},{7,8},{8,9},{9,10},{10,1... | collective-permute-start | bytes 393224 | tf_op jit(solution)/shard_map/ppermute | solution.py:310
  3.9 8.3 %collective-permute-start.1 = (f32[2,4,2,16,128]{4,3,2,1,0:T(8,128)S(1)}, f32[2,4,2,16,128]{4,3,2,1,0:T(8,128)S(1)}, u32[]{:S(2)}, u32[]{:S(2)}) collective-permute-start(f32[2,4,2,16,128]{4,3,2,1,0:T(8,128)S(1)} %get-tuple-element.12), channel_id=1, source_target_pairs={{1,0},{2,1},{3,2},{4,3},{5,4},{6,5},{7,6},{8,7},{9,8},{10,9},{11,1... | collective-permute-start | bytes 393224 | tf_op jit(solution)/shard_map/ppermute | solution.py:311
  12.2 9.1 %copy-start.2 = (f32[4,8,16,128]{3,2,1,0:T(8,128)S(1)}, f32[4,8,16,128]{3,2,1,0:T(8,128)}, u32[]{:S(2)}) copy-start(f32[4,8,16,128]{3,2,1,0:T(8,128)} %state_ref.3) | copy-start | bytes 786436
  12.4 8.9 %collective-permute-start.2 = (f32[30,16,128]{2,1,0:T(8,128)S(1)}, f32[30,16,128]{2,1,0:T(8,128)S(1)}, u32[]{:S(2)}, u32[]{:S(2)}) collective-permute-start(f32[30,16,128]{2,1,0:T(8,128)S(1)} %shard_map.29), channel_id=1, source_target_pairs={{0,32},{32,64},{64,96},{96,128},{128,160},{160,192},{192,224},{224... | collective-permute-start | bytes 737288 | tf_op jit(solution)/shard_map/ppermute | solution.py:314
  62.1 12.9 %all-to-all-start.1 = ((f32[8,6,8,128]{3,2,1,0:T(8,128)}), f32[8,6,8,128]{3,2,1,0:T(8,128)S(1)}, u32[]{:S(2)}, u32[]{:S(2)}) async-start(f32[8,6,8,128]{3,2,1,0:T(8,128)} %shard_map.31), calls=%async_computation.1 | async-start | bytes 393216 | tf_op jit(solution)/shard_map/all_to_all | solution.py:331

commit v2 on v1

v2 whole, which is shorter than its diff:
```python
import jax
import jax.numpy as jnp
from jax import lax
from jax.experimental import pallas as pl
from jax.experimental.pallas import tpu as pltpu
from jax.sharding import PartitionSpec as P

CX = 16
CY = 128
CT = 4
CZ = 8
OV = 2
SWEEPS = 4
CHEB = 8
LANES = 128
NEAR = 4
WINDOW = 16

rate = 8.0
react = 0.5
damp = 0.9
theta = 0.8
delta = 0.6

F32 = jnp.float32
PLANE = (CX, CY)
VMEM = pl.BlockSpec(memory_space=pltpu.VMEM)


def beside(v):
    total = pltpu.roll(v, 1, 0) + pltpu.roll(v, CX - 1, 0)
    return total + (pltpu.roll(v, 1, 1) + pltpu.roll(v, CY - 1, 1))


def swept(v, first, scale, near, before):
    total = beside(v)
    for plane in near:
        if plane is not None:
            total = total + plane
    if before is not None:
        total = total + rate * before
    return (1.0 - damp) * v + first + scale * total


def by_parity(body, first, second):
    odd = at_ref[0] & 1

    @pl.when(odd == 0)
    def _():
        body(first, second)

    @pl.when(odd == 1)
    def _():
        body(second, first)


def by_parity(body, first, second):
    odd = lax.axis_index("space") & 1

    @pl.when(odd == 0)
    def _():
        body(first, second)

    @pl.when(odd == 1)
    def _():
        body(second, first)


def first_kernel(rhs_ref, state_ref, own_ref, outer_ref, inner_ref):
    def body(low_ref, high_ref):
        for t in range(CT):
            for z in range(CZ):
                rhs, s = rhs_ref[t, z], state_ref[t, z]
                diag = (rate + 6.0 - react) + (3.0 * react) * (s * s)
                scale = damp / diag
                first = scale * rhs
                for which, value in enumerate((scale, first, diag, rhs)):
                    own_ref[which, t, z] = value
                if z < OV:
                    low_ref[0, t, z], low_ref[1, t, z] = scale, first
                if z >= CZ - OV:
                    high_ref[0, t, z - (CZ - OV)] = scale
                    high_ref[1, t, z - (CZ - OV)] = first

    by_parity(body, outer_ref, inner_ref)


def reader(which, own_ref, low_ref, high_ref):
    def read(t, z):
        if z < 0:
            return low_ref[which, t, z + OV]
        if z >= CZ:
            return high_ref[which, t, z - CZ]
        return own_ref[which, t, z]

    return read


def later_kernel(own_ref, outer_ref, inner_ref, out_ref):
    off2 = CZ
    off1 = off2 + CZ + 2
    a, b = CT - 2, CT - 1

    def body(low_ref, high_ref):
        scale = reader(0, own_ref, low_ref, high_ref)
        first = reader(1, own_ref, low_ref, high_ref)
        for z in range(-2, CZ + 2):
            out_ref[off1 + z + 2] = first(b, z)
        for z in range(-1, CZ + 1):
            v = first(b, z)
            near = (first(b, z - 1), first(b, z + 1))
            out_ref[off2 + z + 1] = swept(v, v, scale(b, z), near, first(a, z))
        for z in range(CZ):
            v = first(a, z)
            second = swept(v, v, scale(a, z), (first(a, z - 1), first(a, z + 1)), None)
            near = (out_ref[off2 + z], out_ref[off2 + z + 2])
            out_ref[z] = swept(out_ref[off2 + z + 1], first(b, z), scale(b, z), near, second)

    by_parity(body, outer_ref, inner_ref)


def fold_matrix(rows, columns, fine_first):
    i = lax.broadcasted_iota(jnp.int32, (rows, columns), 0)
    k = lax.broadcasted_iota(jnp.int32, (rows, columns), 1)
    fine, lane = (i, k) if fine_first else (k, i)
    return jnp.where(lax.shift_right_logical(fine, 2) == (lane & (CY // 4 - 1)), 1.0, 0.0)


def x_mask():
    x = lax.broadcasted_iota(jnp.int32, PLANE, 0)
    lane = lax.broadcasted_iota(jnp.int32, PLANE, 1)
    return jnp.where(lax.shift_right_logical(x, 2) == lax.shift_right_logical(lane, 5), 1.0, 0.0)


def main_kernel(
    own_ref,
    outer_ref,
    inner_ref,
    prev_ref,
    lp_ref,
    sums_ref,
    v2,
    v3,
    stack,
):
    off2 = CZ
    off1 = off2 + CZ + 2

    def body(low_ref, high_ref):
        scale = reader(0, own_ref, low_ref, high_ref)
        own = reader(1, own_ref, low_ref, high_ref)

        def first(t, z):
            return prev_ref[off1 + z + 2] if t < 0 else own(t, z)

        def second(t, z):
            return prev_ref[off2 + z + 1] if t < 0 else v2[t, z + 2]

        def third(t, z):
            return prev_ref[z] if t < 0 else v3[t, z + 1]

        for t in range(CT):
            for z in range(-2, CZ + 2):
                v = own(t, z)
                near = [own(t, q) for q in (z - 1, z + 1) if -2 <= q < CZ + 2]
                v2[t, z + 2] = swept(v, v, scale(t, z), near, first(t - 1, z))
            for z in range(-1, CZ + 1):
                near = (second(t, z - 1), second(t, z + 1))
                v3[t, z + 1] = swept(second(t, z), own(t, z), scale(t, z), near, second(t - 1, z))
            for z in range(CZ):
                near = (third(t, z - 1), third(t, z + 1))
                lp_ref[t, z] = swept(third(t, z), own(t, z), scale(t, z), near, third(t - 1, z))

    by_parity(body, outer_ref, inner_ref)

    rest = []
    planes = []
    coefs = []
    for z in range(CZ):
        part = None
        diags = None
        for t in range(CT):
            diag = own_ref[2, t, z]
            term = own_ref[3, t, z] - diag * lp_ref[t, z]
            part = term if part is None else part + term
            diags = diag if diags is None else diags + diag
        early = lp_ref[0, z]
        for t in range(1, CT - 1):
            early = early + lp_ref[t, z]
        rest.append(part + rate * early)
        planes.append(early + lp_ref[CT - 1, z])
        coefs.append((diags - CT * (rate + 6.0)) * (1.0 / react))
    for b in range(2):
        z = 4 * b
        total = planes[z] + planes[z + 1] + planes[z + 2] + planes[z + 3]
        inner = planes[z] + planes[z + 3] + 2.0 * (planes[z + 1] + planes[z + 2])
        inner = inner + (planes[4] if b == 0 else planes[3])
        value = rest[z] + rest[z + 1] + rest[z + 2] + rest[z + 3]
        stack[b] = value + beside(total) + inner
        last = lp_ref[CT - 1, z] + lp_ref[CT - 1, z + 1]
        last = last + (lp_ref[CT - 1, z + 2] + lp_ref[CT - 1, z + 3])
        stack[4 + b] = rate * last
        stack[6 + b] = coefs[z] + coefs[z + 1] + coefs[z + 2] + coefs[z + 3]
    stack[2] = planes[0]
    stack[3] = planes[CZ - 1]
    folded = jnp.dot(
        stack[...].reshape(8 * CX, CY),
        fold_matrix(CY, LANES, True),
        precision=lax.Precision.HIGHEST,
        preferred_element_type=F32,
    )
    sums = jnp.sum(folded.reshape(8, CX, LANES) * x_mask()[None], axis=1)
    sums_ref[...] = jnp.broadcast_to(sums[None], sums_ref.shape)


def window_kernel(all_ref, out_ref, rows):
    plane = lax.axis_index("space")
    count = all_ref.shape[0]
    parts = [all_ref[lax.rem(plane + (count - NEAR + k), count)] for k in range(2 * NEAR + 1)]
    for k, part in enumerate(parts):
        low, high = part[0:1], part[1:2]
        if k > 0:
            low = low + parts[k - 1][3:4]
        if k < 2 * NEAR:
            high = high + parts[k + 1][2:3]
        if k > 0:
            rows[0, 2 * k - 1 : 2 * k] = low
            rows[1, 2 * k - 1 : 2 * k] = part[4:5]
            rows[2, 2 * k - 1 : 2 * k] = part[6:7]
        if k < 2 * NEAR:
            rows[0, 2 * k : 2 * k + 1] = high
            rows[1, 2 * k : 2 * k + 1] = part[5:6]
            rows[2, 2 * k : 2 * k + 1] = part[7:8]
    value = rows[...]
    for k in range(out_ref.shape[0]):
        out_ref[k] = value


def coarse_steps(all_ref, bound_ref):
    shape = (WINDOW, LANES)
    lane = lax.broadcasted_iota(jnp.int32, shape, 1) & (CY // 4 - 1)
    row = lax.broadcasted_iota(jnp.int32, shape, 0)
    width = CY // 4
    is_first, is_last = lane == 0, lane == width - 1
    bottom, top = row == 0, row == WINDOW - 1

    def around(f):
        total = pltpu.roll(f, width, 1) + pltpu.roll(f, LANES - width, 1)
        after = jnp.where(is_last, pltpu.roll(f, width - 1, 1), pltpu.roll(f, LANES - 1, 1))
        before = jnp.where(is_first, pltpu.roll(f, LANES - width + 1, 1), pltpu.roll(f, 1, 1))
        below = jnp.where(bottom, 0.0, pltpu.roll(f, 1, 0))
        above = jnp.where(top, 0.0, pltpu.roll(f, WINDOW - 1, 0))
        return total + (after + before) + (below + above)

    slots = all_ref.shape[0] // 2
    inverse = []
    resid = []
    for k in range(slots):
        rhs = all_ref[2 * k, 0] + all_ref[2 * k, 1] + all_ref[2 * k + 1, 0]
        if k > 0:
            rhs = rhs + all_ref[2 * k - 1, 1]
        elif bound_ref is not None:
            rhs = rhs + bound_ref[4]
        coef = all_ref[2 * k, 2] + all_ref[2 * k + 1, 2]
        inv = 1.0 / (1.375 + (react / 512.0) * coef)
        inverse.append(inv)
        resid.append((rhs * (1.0 / 512.0)) * inv)
    step = [r * (1.0 / theta) for r in resid]
    sol = list(step)
    rho = delta / theta
    last = []
    for m in range(1, CHEB):
        nxt = 1.0 / (2.0 * theta / delta - rho)
        last.append(step[-1])
        flows = []
        for k in range(slots):
            flow = around(step[k]) * (1.0 / 16.0)
            if k > 0:
                flow = flow + step[k - 1]
            elif bound_ref is not None:
                flow = flow + (bound_ref[m - 1] if m <= 4 else swapped(bound_ref[7 - m]))
            flows.append(flow)
        for k in range(slots):
            resid[k] = resid[k] - step[k] + flows[k] * inverse[k]
            step[k] = (nxt * rho) * step[k] + (2.0 * nxt / delta) * resid[k]
            sol[k] = sol[k] + step[k]
        rho = nxt
    return sol, last


def swapped(v):
    return jnp.concatenate([v[WINDOW // 2 :], v[: WINDOW // 2]], axis=0)


def bound_kernel(all_ref, out_ref):
    _, last = coarse_steps(all_ref, None)
    row = lax.broadcasted_iota(jnp.int32, (WINDOW, LANES), 0)
    for m in range(3):
        used = (row > m) & (row < WINDOW - 1 - m)
        out_ref[m] = jnp.where(used, last[m], swapped(last[6 - m]))
    out_ref[3] = last[3]
    out_ref[4] = all_ref[all_ref.shape[0] - 1, 1]


def coarse_kernel(lp_ref, all_ref, bound_ref, out_ref, found):
    sol, _ = coarse_steps(all_ref, bound_ref)
    for k, value in enumerate(sol):
        found[k] = value
    slot = lax.rem(lax.axis_index("tm"), all_ref.shape[0]) // 2
    mask = x_mask()
    mine = 2 * NEAR - 1
    spread = [found[slot, mine + b : mine + b + 1] * mask for b in range(2)]
    fine = jnp.dot(
        jnp.concatenate(spread, axis=0),
        fold_matrix(LANES, CY, False),
        precision=lax.Precision.HIGHEST,
        preferred_element_type=F32,
    )
    for b in range(2):
        value = fine[b * CX : (b + 1) * CX]
        for t in range(CT):
            for z in range(4):
                out_ref[t, 4 * b + z] = lp_ref[t, 4 * b + z] + value


def call(kernel, shapes, count, scratch=()):
    single = not isinstance(shapes, (list, tuple))
    return pl.pallas_call(
        kernel,
        out_shape=shapes if single else list(shapes),
        in_specs=[VMEM] * count,
        out_specs=VMEM if single else [VMEM] * len(shapes),
        scratch_shapes=list(scratch),
        compiler_params=pltpu.CompilerParams(vmem_limit_bytes=32 << 20),
    )


def arr(*shape):
    return jax.ShapeDtypeStruct(shape, F32)


def local(right_side, state):
    slabs = lax.axis_size("tm")
    planes = lax.axis_size("space")
    half = slabs // 2
    across = [(k, (k + 1) % planes) for k in range(1, planes, 2)]
    across += [(b, a) for a, b in across]
    within = [(k, k + 1) for k in range(0, planes, 2)]
    within += [(b, a) for a, b in within]
    onward = [(i, i + 1) for i in range(slabs - 1)]

    edge = arr(2, CT, OV, CX, CY)
    own, outer, inner = call(first_kernel, [arr(4, CT, CZ, CX, CY), edge, edge], 2)(
        right_side, state
    )
    outer = lax.ppermute(outer, "space", across)
    inner = lax.ppermute(inner, "space", within)
    sent = call(later_kernel, arr(3 * CZ + 6, CX, CY), 3)(own, outer, inner)
    prev = lax.ppermute(sent, "tm", onward)
    lp, sums = call(
        main_kernel,
        [arr(CT, CZ, CX, CY), arr(planes, 8, LANES)],
        4,
        [
            pltpu.VMEM((CT, CZ + 4, CX, CY), F32),
            pltpu.VMEM((CT, CZ + 2, CX, CY), F32),
            pltpu.VMEM((8, CX, CY), F32),
        ],
    )(own, outer, inner, prev)
    column = lax.all_to_all(sums, "space", 0, 0)
    window = call(
        window_kernel,
        arr(half, 3, WINDOW, LANES),
        1,
        [pltpu.VMEM((3, WINDOW, LANES), F32)],
    )(column)
    halves = [list(range(half)), list(range(half, slabs))]
    every = lax.all_to_all(window, "tm", 0, 0, axis_index_groups=halves)
    last = call(bound_kernel, arr(5, WINDOW, LANES), 1)(every)
    quarter = half // 2
    serve = [(i, i + quarter) for i in range(quarter, half)]
    serve += [(i, i + half + quarter) for i in range(quarter)]
    bound = lax.ppermute(last, "tm", serve)
    return call(
        coarse_kernel,
        arr(CT, CZ, CX, CY),
        3,
        [pltpu.VMEM((half // 2, WINDOW, LANES), F32)],
    )(lp, every, bound)


def solution(mesh):
    return jax.shard_map(
        local,
        mesh=mesh,
        in_specs=(P("tm", "space", None, None), P("tm", "space", None, None)),
        out_specs=P("tm", "space", None, None),
        check_vma=False,
    )
```

time: 77.7 us -> 68.7 us (0.88)
  waiting for transfers between devices: 14.3 us -> 9.11 us
  starting transfers between devices: 17.6 us -> 13.2 us
    all_to_all x1 -> x0, waiting for transfers between devices: 6.76 us -> none  [local(): here = lax.all_to_all(slots, 'space', 0, 0, axis_index_groups=groups)]
    all_to_all x1 -> x0, starting transfers between devices: 6.08 us -> none  [local(): here = lax.all_to_all(slots, 'space', 0, 0, axis_index_groups=groups)]
    ppermute x2 -> x3, starting transfers between devices: 7.67 us -> 9.34 us  [the longest x1 4.62 us: local(): outer = lax.ppermute(outer, 'space', across)]
    ppermute x2 -> x3, waiting for transfers between devices: 2.5 us -> 4.15 us  [the longest x1 2.31 us: local(): bound = lax.ppermute(last, 'tm', serve)]
    pallas_call x5 -> x6, Pallas kernels: 4.18 us -> 3.65 us  [the longest x1 1.69 us: local(): call(coarse_kernel, arr(CT, CZ, CX, CY), 3, [pltpu.VMEM((half // 2, WINDO...]
    unnamed x6 -> x4, local copies, waits for them, and re-layouts: 1.9 us -> 1.9 us
  transfers between devices with their start and end apart: 4 -> 4, of which waited for: 4 -> 3; matrix products, arithmetic and copies ran while one was open for 0% -> 0% of each run, Pallas kernels for 0% -> 0%
where the time goes in v2:
time: 68.7 us; the launch traced here: 67.7 us
  blocking collectives  39.8 us (58%)
  starting transfers between devices  13.2 us (19%)
  waiting for transfers between devices  9.11 us (13%)
  Pallas kernels  3.65 us (5%)
  local copies, waits for them, and re-layouts  1.9 us (3%)
    all_to_all x1, blocking collectives, local(): every = lax.all_to_all(window, 'tm', 0, 0, axis_index_groups=halves)  26.3 us
    all_to_all x1, blocking collectives, local(): column = lax.all_to_all(sums, 'space', 0, 0)  13.5 us
    ppermute x1, waiting for transfers between devices, local(): prev = lax.ppermute(sent, 'tm', onward)  4.96 us
    ppermute x1, starting transfers between devices, local(): outer = lax.ppermute(outer, 'space', across)  4.62 us
    ppermute x1, starting transfers between devices, local(): prev = lax.ppermute(sent, 'tm', onward)  3.84 us
    ppermute x1, starting transfers between devices, local(): bound = lax.ppermute(last, 'tm', serve)  2.8 us
    ppermute x1, waiting for transfers between devices, local(): bound = lax.ppermute(last, 'tm', serve)  2.31 us
    ppermute x1, starting transfers between devices, local(): inner = lax.ppermute(inner, 'space', within)  1.92 us
  transfers between devices with their start and end apart: 4, of which 3 were waited for; matrix products, arithmetic and copies ran while one was open for 0% of the time, Pallas kernels for 0%

profile of v2, /device:TPU:6, one launch (start us, length us, event | category | flops | bytes accessed | tf_op | source)
XLA Modules:
  0.0 67.7 jit_solution(997839968399815274)
XLA Ops:
  0.0 0.0 copy-start
  0.0 0.9 %copy-done = f32[4,8,16,128]{3,2,1,0:T(8,128)S(1)} copy-done((f32[4,8,16,128]{3,2,1,0:T(8,128)S(1)}, f32[4,8,16,128]{3,2,1,0:T(8,128)}, u32[]{:S(2)}) %copy-start) | copy-done | bytes 262168
  1.0 0.0 copy-start.1
  1.0 0.9 %copy-done.1 = f32[4,8,16,128]{3,2,1,0:T(8,128)S(1)} copy-done((f32[4,8,16,128]{3,2,1,0:T(8,128)S(1)}, f32[4,8,16,128]{3,2,1,0:T(8,128)}, u32[]{:S(2)}) %copy-start.1) | copy-done | bytes 262168
  1.9 0.1 shard_map.28
  2.0 4.6 %collective-permute-start = (f32[2,4,2,16,128]{4,3,2,1,0:T(8,128)S(1)}, f32[2,4,2,16,128]{4,3,2,1,0:T(8,128)S(1)}, u32[]{:S(2)}, u32[]{:S(2)}) collective-permute-start(f32[2,4,2,16,128]{4,3,2,1,0:T(8,128)S(1)} %get-tuple-element.11), channel_id=1, source_target_pairs={{1,2},{3,4},{5,6},{7,8},{9,10},{11,12},{13,14},{15,16},{17,18},{19... | collective-permute-start | bytes 393224 | tf_op jit(solution)/shard_map/ppermute | solution.py:356
  6.6 1.9 %collective-permute-start.1 = (f32[2,4,2,16,128]{4,3,2,1,0:T(8,128)S(1)}, f32[2,4,2,16,128]{4,3,2,1,0:T(8,128)S(1)}, u32[]{:S(2)}, u32[]{:S(2)}) collective-permute-start(f32[2,4,2,16,128]{4,3,2,1,0:T(8,128)S(1)} %get-tuple-element.12), channel_id=1, source_target_pairs={{0,1},{2,3},{4,5},{6,7},{8,9},{10,11},{12,13},{14,15},{16,17},{18,... | collective-permute-start | bytes 393224 | tf_op jit(solution)/shard_map/ppermute | solution.py:357
  8.6 1.8 %collective-permute-done.outer_ref = f32[2,4,2,16,128]{4,3,2,1,0:T(8,128)S(1)} collective-permute-done((f32[2,4,2,16,128]{4,3,2,1,0:T(8,128)S(1)}, f32[2,4,2,16,128]{4,3,2,1,0:T(8,128)S(1)}, u32[]{:S(2)}, u32[]{:S(2)}) %collective-permute-start) | collective-permute-done | bytes 131104 | tf_op jit(solution)/shard_map/ppermute | solution.py:356
  10.4 0.0 collective-permute-done.1.inner_ref
  10.4 0.2 shard_map.29
  10.6 3.8 %collective-permute-start.2 = (f32[30,16,128]{2,1,0:T(8,128)S(1)}, f32[30,16,128]{2,1,0:T(8,128)S(1)}, u32[]{:S(2)}, u32[]{:S(2)}) collective-permute-start(f32[30,16,128]{2,1,0:T(8,128)S(1)} %shard_map.29), channel_id=1, source_target_pairs={{0,32},{32,64},{64,96},{96,128},{128,160},{160,192},{192,224},{224... | collective-permute-start | bytes 737288 | tf_op jit(solution)/shard_map/ppermute | solution.py:359
  14.4 5.0 %collective-permute-done.2.prev_ref = f32[30,16,128]{2,1,0:T(8,128)S(1)} collective-permute-done((f32[30,16,128]{2,1,0:T(8,128)S(1)}, f32[30,16,128]{2,1,0:T(8,128)S(1)}, u32[]{:S(2)}, u32[]{:S(2)}) %collective-permute-start.2) | collective-permute-done | bytes 245792 | tf_op jit(solution)/shard_map/ppermute | solution.py:359
  19.4 1.1 %shard_map.30 = (f32[4,8,16,128]{3,2,1,0:T(8,128)S(1)}, f32[32,8,128]{2,1,0:T(8,128)S(1)}) custom-call(f32[4,4,8,16,128]{4,3,2,1,0:T(8,128)S(1)} %get-tuple-element.10.own_ref, f32[2,4,2,16,128]{4,3,2,1,0:T(8,128)S(1)} %collective-permute-done.outer_ref, f32[2,4,2,16,128]{4,3,2,1,0:T(8,128)S(1)} %collective-permute-done.1.inner_ref, ...), custom_call_target="tpu_custom_call" | custom-call | tf_op jit(solution)/shard_map/pallas_call | solution.py:360
  20.5 13.5 %all_to_all.10.all_ref = f32[32,8,128]{2,1,0:T(8,128)S(1)} all-to-all(f32[32,8,128]{2,1,0:T(8,128)S(1)} %get-tuple-element.14), channel_id=1, replica_groups=mesh['tm'=16,'space'=32] {'space'}, dimensions={0} | all-to-all | bytes 262144 | tf_op jit(solution)/shard_map/all_to_all | solution.py:370
  34.0 26.3 %all_to_all.11.all_ref = f32[8,3,16,128]{3,2,1,0:T(8,128)S(1)} all-to-all(f32[8,3,16,128]{3,2,1,0:T(8,128)S(1)} %shard_map.31), channel_id=1, replica_groups={{0,32,64,96,128,160,192,224},{256,288,320,352,384,416,448,480},{1,33,65..., dimensions={0} | all-to-all | bytes 393216 | tf_op jit(solution)/shard_map/all_to_all | solution.py:378
  60.3 0.5 shard_map.32
  60.9 2.8 %collective-permute-start.3 = (f32[5,16,128]{2,1,0:T(8,128)S(1)}, f32[5,16,128]{2,1,0:T(8,128)S(1)}, u32[]{:S(2)}, u32[]{:S(2)}) collective-permute-start(f32[5,16,128]{2,1,0:T(8,128)S(1)} %shard_map.32), channel_id=1, source_target_pairs={{128,256},{160,288},{192,320},{224,352},{0,384},{32,416},{64,448},... | collective-permute-start | bytes 122888 | tf_op jit(solution)/shard_map/ppermute | solution.py:383
  63.7 2.3 %collective-permute-done.3.bound_ref = f32[5,16,128]{2,1,0:T(8,128)S(1)} collective-permute-done((f32[5,16,128]{2,1,0:T(8,128)S(1)}, f32[5,16,128]{2,1,0:T(8,128)S(1)}, u32[]{:S(2)}, u32[]{:S(2)}) %collective-permute-start.3) | collective-permute-done | bytes 40992 | tf_op jit(solution)/shard_map/ppermute | solution.py:383
  66.0 1.7 %shard_map.33 = f32[4,8,16,128]{3,2,1,0:T(8,128)} custom-call(f32[4,8,16,128]{3,2,1,0:T(8,128)S(1)} %get-tuple-element.13.lp_ref, f32[8,3,16,128]{3,2,1,0:T(8,128)S(1)} %all_to_all.11.all_ref, f32[5,16,128]{2,1,0:T(8,128)S(1)} %collective-permute-done.3.bound_ref), custom_call_target="tpu_custom_call" | custom-call | tf_op jit(solution)/shard_map/pallas_call | solution.py:384
  (1 shorter events, 0.0 us)
Async XLA Ops:
  0.0 0.9 %copy-start = (f32[4,8,16,128]{3,2,1,0:T(8,128)S(1)}, f32[4,8,16,128]{3,2,1,0:T(8,128)}, u32[]{:S(2)}) copy-start(f32[4,8,16,128]{3,2,1,0:T(8,128)} %rhs_ref.1) | copy-start | bytes 786436
  1.0 0.9 %copy-start.1 = (f32[4,8,16,128]{3,2,1,0:T(8,128)S(1)}, f32[4,8,16,128]{3,2,1,0:T(8,128)}, u32[]{:S(2)}) copy-start(f32[4,8,16,128]{3,2,1,0:T(8,128)} %state_ref.1) | copy-start | bytes 786436
  2.0 8.4 %collective-permute-start = (f32[2,4,2,16,128]{4,3,2,1,0:T(8,128)S(1)}, f32[2,4,2,16,128]{4,3,2,1,0:T(8,128)S(1)}, u32[]{:S(2)}, u32[]{:S(2)}) collective-permute-start(f32[2,4,2,16,128]{4,3,2,1,0:T(8,128)S(1)} %get-tuple-element.11), channel_id=1, source_target_pairs={{1,2},{3,4},{5,6},{7,8},{9,10},{11,12},{13,14},{15,16},{17,18},{19... | collective-permute-start | bytes 393224 | tf_op jit(solution)/shard_map/ppermute | solution.py:356
  6.6 3.8 %collective-permute-start.1 = (f32[2,4,2,16,128]{4,3,2,1,0:T(8,128)S(1)}, f32[2,4,2,16,128]{4,3,2,1,0:T(8,128)S(1)}, u32[]{:S(2)}, u32[]{:S(2)}) collective-permute-start(f32[2,4,2,16,128]{4,3,2,1,0:T(8,128)S(1)} %get-tuple-element.12), channel_id=1, source_target_pairs={{0,1},{2,3},{4,5},{6,7},{8,9},{10,11},{12,13},{14,15},{16,17},{18,... | collective-permute-start | bytes 393224 | tf_op jit(solution)/shard_map/ppermute | solution.py:357
  10.6 8.8 %collective-permute-start.2 = (f32[30,16,128]{2,1,0:T(8,128)S(1)}, f32[30,16,128]{2,1,0:T(8,128)S(1)}, u32[]{:S(2)}, u32[]{:S(2)}) collective-permute-start(f32[30,16,128]{2,1,0:T(8,128)S(1)} %shard_map.29), channel_id=1, source_target_pairs={{0,32},{32,64},{64,96},{96,128},{128,160},{160,192},{192,224},{224... | collective-permute-start | bytes 737288 | tf_op jit(solution)/shard_map/ppermute | solution.py:359
  60.9 5.1 %collective-permute-start.3 = (f32[5,16,128]{2,1,0:T(8,128)S(1)}, f32[5,16,128]{2,1,0:T(8,128)S(1)}, u32[]{:S(2)}, u32[]{:S(2)}) collective-permute-start(f32[5,16,128]{2,1,0:T(8,128)S(1)} %shard_map.32), channel_id=1, source_target_pairs={{128,256},{160,288},{192,320},{224,352},{0,384},{32,416},{64,448},... | collective-permute-start | bytes 122888 | tf_op jit(solution)/shard_map/ppermute | solution.py:383

commit v3 on v2

--- a/solution.py
+++ b/solution.py
@@ -132,11 +132,63 @@
     return jnp.where(lax.shift_right_logical(x, 2) == lax.shift_right_logical(lane, 5), 1.0, 0.0)
 
 
+def early_kernel(own_ref, outer_ref, inner_ref, v2_ref, v3_ref, v4_ref):
+    def body(low_ref, high_ref):
+        scale = reader(0, own_ref, low_ref, high_ref)
+        first = reader(1, own_ref, low_ref, high_ref)
+        for t in range(1, CT):
+            for z in range(-2, CZ + 2):
+                v = first(t, z)
+                near = [first(t, q) for q in (z - 1, z + 1) if -2 <= q < CZ + 2]
+                v2_ref[t - 1, z + 2] = swept(v, v, scale(t, z), near, first(t - 1, z))
+        for t in range(2, CT):
+            for z in range(-1, CZ + 1):
+                near = (v2_ref[t - 1, z + 1], v2_ref[t - 1, z + 3])
+                v3_ref[t - 2, z + 1] = swept(
+                    v2_ref[t - 1, z + 2], first(t, z), scale(t, z), near, v2_ref[t - 2, z + 2]
+                )
+        t = CT - 1
+        for z in range(CZ):
+            near = (v3_ref[t - 2, z], v3_ref[t - 2, z + 2])
+            v4_ref[z] = swept(
+                v3_ref[t - 2, z + 1], first(t, z), scale(t, z), near, v3_ref[t - 3, z + 1]
+            )
+
+    by_parity(body, outer_ref, inner_ref)
+
+
+def fold(planes):
+    folded = jnp.dot(
+        planes.reshape(-1, CY),
+        fold_matrix(CY, LANES, True),
+        precision=lax.Precision.HIGHEST,
+        preferred_element_type=F32,
+    )
+    return jnp.sum(folded.reshape(-1, CX, LANES) * x_mask()[None], axis=1)
+
+
+def coef_kernel(own_ref, out_ref, stack):
+    stack[...] = jnp.zeros_like(stack)
+    for b in range(2):
+        total = None
+        for t in range(CT):
+            for z in range(4 * b, 4 * b + 4):
+                diag = own_ref[2, t, z]
+                total = diag if total is None else total + diag
+        stack[4 + b] = (total - 4 * CT * (rate + 6.0)) * (1.0 / react)
+    out_ref[...] = fold(stack[...])
+
+
 def main_kernel(
     own_ref,
     outer_ref,
     inner_ref,
+    v2_ref,
+    v3_ref,
+    v4_ref,
     prev_ref,
+    coef_ref,
+    other_coef_ref,
     lp_ref,
     sums_ref,
     v2,
@@ -150,66 +202,63 @@
         scale = reader(0, own_ref, low_ref, high_ref)
         own = reader(1, own_ref, low_ref, high_ref)
 
-        def first(t, z):
-            return prev_ref[off1 + z + 2] if t < 0 else own(t, z)
-
         def second(t, z):
-            return prev_ref[off2 + z + 1] if t < 0 else v2[t, z + 2]
+            if t < 0:
+                return prev_ref[off2 + z + 1]
+            return v2[z + 2] if t == 0 else v2_ref[t - 1, z + 2]
 
         def third(t, z):
-            return prev_ref[z] if t < 0 else v3[t, z + 1]
-
-        for t in range(CT):
-            for z in range(-2, CZ + 2):
-                v = own(t, z)
-                near = [own(t, q) for q in (z - 1, z + 1) if -2 <= q < CZ + 2]
-                v2[t, z + 2] = swept(v, v, scale(t, z), near, first(t - 1, z))
+            if t < 0:
+                return prev_ref[z]
+            return v3[t, z + 1] if t < 2 else v3_ref[t - 2, z + 1]
+
+        for z in range(-2, CZ + 2):
+            v = own(0, z)
+            near = [own(0, q) for q in (z - 1, z + 1) if -2 <= q < CZ + 2]
+            v2[z + 2] = swept(v, v, scale(0, z), near, prev_ref[off1 + z + 2])
+        for t in range(2):
             for z in range(-1, CZ + 1):
                 near = (second(t, z - 1), second(t, z + 1))
                 v3[t, z + 1] = swept(second(t, z), own(t, z), scale(t, z), near, second(t - 1, z))
+        for t in range(CT - 1):
             for z in range(CZ):
                 near = (third(t, z - 1), third(t, z + 1))
                 lp_ref[t, z] = swept(third(t, z), own(t, z), scale(t, z), near, third(t - 1, z))
 
     by_parity(body, outer_ref, inner_ref)
+    for z in range(CZ):
+        lp_ref[CT - 1, z] = v4_ref[z]
 
     rest = []
     planes = []
-    coefs = []
     for z in range(CZ):
         part = None
-        diags = None
         for t in range(CT):
-            diag = own_ref[2, t, z]
-            term = own_ref[3, t, z] - diag * lp_ref[t, z]
+            term = own_ref[3, t, z] - own_ref[2, t, z] * lp_ref[t, z]
             part = term if part is None else part + term
-            diags = diag if diags is None else diags + diag
         early = lp_ref[0, z]
         for t in range(1, CT - 1):
             early = early + lp_ref[t, z]
         rest.append(part + rate * early)
         planes.append(early + lp_ref[CT - 1, z])
-        coefs.append((diags - CT * (rate + 6.0)) * (1.0 / react))
+    odd = (lax.axis_index("tm") & 1) == 1
     for b in range(2):
         z = 4 * b
         total = planes[z] + planes[z + 1] + planes[z + 2] + planes[z + 3]
         inner = planes[z] + planes[z + 3] + 2.0 * (planes[z + 1] + planes[z + 2])
         inner = inner + (planes[4] if b == 0 else planes[3])
         value = rest[z] + rest[z + 1] + rest[z + 2] + rest[z + 3]
-        stack[b] = value + beside(total) + inner
+        value = value + beside(total) + inner
         last = lp_ref[CT - 1, z] + lp_ref[CT - 1, z + 1]
-        last = last + (lp_ref[CT - 1, z + 2] + lp_ref[CT - 1, z + 3])
-        stack[4 + b] = rate * last
-        stack[6 + b] = coefs[z] + coefs[z + 1] + coefs[z + 2] + coefs[z + 3]
+        last = rate * (last + (lp_ref[CT - 1, z + 2] + lp_ref[CT - 1, z + 3]))
+        stack[b] = jnp.where(odd, value, value + last)
+        stack[4 + b] = jnp.where(odd, last, 0.0)
     stack[2] = planes[0]
     stack[3] = planes[CZ - 1]
-    folded = jnp.dot(
-        stack[...].reshape(8 * CX, CY),
-        fold_matrix(CY, LANES, True),
-        precision=lax.Precision.HIGHEST,
-        preferred_element_type=F32,
-    )
-    sums = jnp.sum(folded.reshape(8, CX, LANES) * x_mask()[None], axis=1)
+    stack[6] = jnp.zeros(PLANE, F32)
+    stack[7] = jnp.zeros(PLANE, F32)
+    coef = coef_ref[...] + other_coef_ref[...]
+    sums = fold(stack[...]) + jnp.where(odd, 0.0, coef)
     sums_ref[...] = jnp.broadcast_to(sums[None], sums_ref.shape)
 
 
@@ -226,11 +275,9 @@
         if k > 0:
             rows[0, 2 * k - 1 : 2 * k] = low
             rows[1, 2 * k - 1 : 2 * k] = part[4:5]
-            rows[2, 2 * k - 1 : 2 * k] = part[6:7]
         if k < 2 * NEAR:
             rows[0, 2 * k : 2 * k + 1] = high
             rows[1, 2 * k : 2 * k + 1] = part[5:6]
-            rows[2, 2 * k : 2 * k + 1] = part[7:8]
     value = rows[...]
     for k in range(out_ref.shape[0]):
         out_ref[k] = value
@@ -256,12 +303,12 @@
     inverse = []
     resid = []
     for k in range(slots):
-        rhs = all_ref[2 * k, 0] + all_ref[2 * k, 1] + all_ref[2 * k + 1, 0]
+        rhs = all_ref[2 * k, 0] + all_ref[2 * k + 1, 0]
         if k > 0:
             rhs = rhs + all_ref[2 * k - 1, 1]
         elif bound_ref is not None:
             rhs = rhs + bound_ref[4]
-        coef = all_ref[2 * k, 2] + all_ref[2 * k + 1, 2]
+        coef = all_ref[2 * k, 1]
         inv = 1.0 / (1.375 + (react / 512.0) * coef)
         inverse.append(inv)
         resid.append((rhs * (1.0 / 512.0)) * inv)
@@ -292,35 +339,63 @@
     return jnp.concatenate([v[WINDOW // 2 :], v[: WINDOW // 2]], axis=0)
 
 
-def bound_kernel(all_ref, out_ref):
-    _, last = coarse_steps(all_ref, None)
-    row = lax.broadcasted_iota(jnp.int32, (WINDOW, LANES), 0)
-    for m in range(3):
-        used = (row > m) & (row < WINDOW - 1 - m)
-        out_ref[m] = jnp.where(used, last[m], swapped(last[6 - m]))
-    out_ref[3] = last[3]
-    out_ref[4] = all_ref[all_ref.shape[0] - 1, 1]
-
-
-def coarse_kernel(lp_ref, all_ref, bound_ref, out_ref, found):
-    sol, _ = coarse_steps(all_ref, bound_ref)
+def bound_kernel(all_ref, out_ref, mine_ref, found):
+    @pl.when(lax.axis_index("tm") < all_ref.shape[0])
+    def _():
+        sol, last = coarse_steps(all_ref, None)
+        row = lax.broadcasted_iota(jnp.int32, (WINDOW, LANES), 0)
+        for m in range(3):
+            used = (row > m) & (row < WINDOW - 1 - m)
+            out_ref[m] = jnp.where(used, last[m], swapped(last[6 - m]))
+        out_ref[3] = last[3]
+        out_ref[4] = all_ref[all_ref.shape[0] - 1, 1]
+        mine_ref[...] = own_slot(sol, found)
+
+
+def own_slot(sol, found):
     for k, value in enumerate(sol):
         found[k] = value
-    slot = lax.rem(lax.axis_index("tm"), all_ref.shape[0]) // 2
+    return found[lax.rem(lax.axis_index("tm"), 2 * len(sol)) // 2]
+
+
+def spread(window):
     mask = x_mask()
     mine = 2 * NEAR - 1
-    spread = [found[slot, mine + b : mine + b + 1] * mask for b in range(2)]
+    both = [window[mine + b : mine + b + 1] * mask for b in range(2)]
     fine = jnp.dot(
-        jnp.concatenate(spread, axis=0),
+        jnp.concatenate(both, axis=0),
         fold_matrix(LANES, CY, False),
         precision=lax.Precision.HIGHEST,
         preferred_element_type=F32,
     )
-    for b in range(2):
-        value = fine[b * CX : (b + 1) * CX]
+    return [fine[b * CX : (b + 1) * CX] for b in range(2)]
+
+
+def result_kernel(lp_ref, mine_ref, out_ref):
+    for b, value in enumerate(spread(mine_ref[...])):
         for t in range(CT):
-            for z in range(4):
-                out_ref[t, 4 * b + z] = lp_ref[t, 4 * b + z] + value
+            for z in range(4 * b, 4 * b + 4):
+                out_ref[t, z] = lp_ref[t, z] + value
+
+
+def second_half_kernel(lp_ref, all_ref, bound_ref, _, out_ref, found, result, sems):
+    @pl.when(lax.axis_index("tm") >= all_ref.shape[0])
+    def _():
+        sol, _ = coarse_steps(all_ref, bound_ref)
+        values = spread(own_slot(sol, found))
+        copies = []
+        for t in range(CT):
+            for b, value in enumerate(values):
+                for z in range(4 * b, 4 * b + 4):
+                    result[t, z] = lp_ref[t, z] + value
+                part = pl.ds(4 * b, 4)
+                copy = pltpu.make_async_copy(
+                    result.at[t, part], out_ref.at[t, part], sems.at[2 * t + b]
+                )
+                copy.start()
+                copies.append(copy)
+        for copy in copies:
+            copy.wait()
 
 
 def call(kernel, shapes, count, scratch=()):
@@ -357,36 +432,54 @@
     inner = lax.ppermute(inner, "space", within)
     sent = call(later_kernel, arr(3 * CZ + 6, CX, CY), 3)(own, outer, inner)
     prev = lax.ppermute(sent, "tm", onward)
+    v2, v3, v4 = call(
+        early_kernel,
+        [arr(CT - 1, CZ + 4, CX, CY), arr(CT - 2, CZ + 2, CX, CY), arr(CZ, CX, CY)],
+        3,
+    )(own, outer, inner)
+    coef = call(coef_kernel, arr(8, LANES), 1, [pltpu.VMEM((8, CX, CY), F32)])(own)
+    other_coef = lax.ppermute(coef, "tm", [(i, i - 1) for i in range(1, slabs, 2)])
     lp, sums = call(
         main_kernel,
         [arr(CT, CZ, CX, CY), arr(planes, 8, LANES)],
-        4,
+        9,
         [
-            pltpu.VMEM((CT, CZ + 4, CX, CY), F32),
-            pltpu.VMEM((CT, CZ + 2, CX, CY), F32),
+            pltpu.VMEM((CZ + 4, CX, CY), F32),
+            pltpu.VMEM((2, CZ + 2, CX, CY), F32),
             pltpu.VMEM((8, CX, CY), F32),
         ],
-    )(own, outer, inner, prev)
+    )(own, outer, inner, v2, v3, v4, prev, coef, other_coef)
     column = lax.all_to_all(sums, "space", 0, 0)
     window = call(
         window_kernel,
-        arr(half, 3, WINDOW, LANES),
+        arr(half, 2, WINDOW, LANES),
         1,
-        [pltpu.VMEM((3, WINDOW, LANES), F32)],
+        [pltpu.VMEM((2, WINDOW, LANES), F32)],
     )(column)
     halves = [list(range(half)), list(range(half, slabs))]
     every = lax.all_to_all(window, "tm", 0, 0, axis_index_groups=halves)
-    last = call(bound_kernel, arr(5, WINDOW, LANES), 1)(every)
+    found = pltpu.VMEM((half // 2, WINDOW, LANES), F32)
+    last, mine = call(bound_kernel, [arr(5, WINDOW, LANES), arr(WINDOW, LANES)], 1, [found])(every)
     quarter = half // 2
     serve = [(i, i + quarter) for i in range(quarter, half)]
     serve += [(i, i + half + quarter) for i in range(quarter)]
     bound = lax.ppermute(last, "tm", serve)
-    return call(
-        coarse_kernel,
-        arr(CT, CZ, CX, CY),
-        3,
-        [pltpu.VMEM((half // 2, WINDOW, LANES), F32)],
-    )(lp, every, bound)
+    shape = arr(CT, CZ, CX, CY)
+    result = call(result_kernel, shape, 2)(lp, mine)
+    anywhere = pl.BlockSpec(memory_space=pl.ANY)
+    return pl.pallas_call(
+        second_half_kernel,
+        out_shape=shape,
+        in_specs=[VMEM, VMEM, VMEM, anywhere],
+        out_specs=anywhere,
+        scratch_shapes=[
+            found,
+            pltpu.VMEM((CT, CZ, CX, CY), F32),
+            pltpu.SemaphoreType.DMA((2 * CT,)),
+        ],
+        input_output_aliases={3: 0},
+        compiler_params=pltpu.CompilerParams(vmem_limit_bytes=32 << 20),
+    )(lp, every, bound, result)
 
 
 def solution(mesh):

time: 68.7 us -> 63.8 us (0.929)
  blocking collectives: 39.8 us -> 37.1 us
  waiting for transfers between devices: 9.11 us -> 7.09 us
    ppermute x1, waiting for transfers between devices: 4.96 us -> 0.01 us  [local(): prev = lax.ppermute(sent, 'tm', onward)]
    ppermute x0 -> x1, waiting for transfers between devices: none -> 3.77 us  [local(): lax.ppermute(coef, 'tm', [(i, i - 1) for i in range(1, slabs, 2)])]
    all_to_all x1, blocking collectives: 26.3 us -> 23.9 us  [local(): every = lax.all_to_all(window, 'tm', 0, 0, axis_index_groups=halves)]
    ppermute x0 -> x1, starting transfers between devices: none -> 1.29 us  [local(): lax.ppermute(coef, 'tm', [(i, i - 1) for i in range(1, slabs, 2)])]
    ppermute x1, starting transfers between devices: 2.8 us -> 1.6 us  [local(): bound = lax.ppermute(last, 'tm', serve)]
    ppermute x1, waiting for transfers between devices: 2.31 us -> 1.47 us  [local(): bound = lax.ppermute(last, 'tm', serve)]
    pallas_call x4 -> x7, Pallas kernels: 3.37 us -> 3.04 us  [the longest x1 0.89 us: local(): result = call(result_kernel, shape, 2)(lp, mine)]
  transfers between devices with their start and end apart: 4 -> 5, of which waited for: 3 -> 3; matrix products, arithmetic and copies ran while one was open for 0% -> 0% of each run, Pallas kernels for 0% -> 2%
where the time goes in v3:
time: 63.8 us; the launch traced here: 62.8 us
  blocking collectives  37.1 us (58%)
  starting transfers between devices  13.3 us (21%)
  waiting for transfers between devices  7.09 us (11%)
  Pallas kernels  3.33 us (5%)
  local copies, waits for them, and re-layouts  1.9 us (3%)
    all_to_all x1, blocking collectives, local(): every = lax.all_to_all(window, 'tm', 0, 0, axis_index_groups=halves)  23.9 us
    all_to_all x1, blocking collectives, local(): column = lax.all_to_all(sums, 'space', 0, 0)  13.2 us
    ppermute x1, starting transfers between devices, local(): outer = lax.ppermute(outer, 'space', across)  4.62 us
    ppermute x1, starting transfers between devices, local(): prev = lax.ppermute(sent, 'tm', onward)  3.84 us
    ppermute x1, waiting for transfers between devices, local(): lax.ppermute(coef, 'tm', [(i, i - 1) for i in range(1, slabs, 2)])  3.77 us
    ppermute x1, starting transfers between devices, local(): inner = lax.ppermute(inner, 'space', within)  1.92 us
    unnamed x4, local copies, waits for them, and re-layouts  1.9 us
    ppermute x1, waiting for transfers between devices, local(): outer = lax.ppermute(outer, 'space', across)  1.84 us
  transfers between devices with their start and end apart: 5, of which 3 were waited for; matrix products, arithmetic and copies ran while one was open for 0% of the time, Pallas kernels for 2%

profile of v3, /device:TPU:6, one launch (start us, length us, event | category | flops | bytes accessed | tf_op | source)
XLA Modules:
  0.0 62.8 jit_solution(12719102618395870587)
XLA Ops:
  0.0 0.0 copy-start
  0.0 0.9 %copy-done = f32[4,8,16,128]{3,2,1,0:T(8,128)S(1)} copy-done((f32[4,8,16,128]{3,2,1,0:T(8,128)S(1)}, f32[4,8,16,128]{3,2,1,0:T(8,128)}, u32[]{:S(2)}) %copy-start) | copy-done | bytes 262168
  1.0 0.0 copy-start.1
  1.0 0.9 %copy-done.1 = f32[4,8,16,128]{3,2,1,0:T(8,128)S(1)} copy-done((f32[4,8,16,128]{3,2,1,0:T(8,128)S(1)}, f32[4,8,16,128]{3,2,1,0:T(8,128)}, u32[]{:S(2)}) %copy-start.1) | copy-done | bytes 262168
  1.9 0.1 shard_map.28
  2.0 4.6 %collective-permute-start = (f32[2,4,2,16,128]{4,3,2,1,0:T(8,128)S(1)}, f32[2,4,2,16,128]{4,3,2,1,0:T(8,128)S(1)}, u32[]{:S(2)}, u32[]{:S(2)}) collective-permute-start(f32[2,4,2,16,128]{4,3,2,1,0:T(8,128)S(1)} %get-tuple-element.16), channel_id=1, source_target_pairs={{1,2},{3,4},{5,6},{7,8},{9,10},{11,12},{13,14},{15,16},{17,18},{19... | collective-permute-start | bytes 393224 | tf_op jit(solution)/shard_map/ppermute | solution.py:431
  6.6 1.9 %collective-permute-start.1 = (f32[2,4,2,16,128]{4,3,2,1,0:T(8,128)S(1)}, f32[2,4,2,16,128]{4,3,2,1,0:T(8,128)S(1)}, u32[]{:S(2)}, u32[]{:S(2)}) collective-permute-start(f32[2,4,2,16,128]{4,3,2,1,0:T(8,128)S(1)} %get-tuple-element.17), channel_id=1, source_target_pairs={{0,1},{2,3},{4,5},{6,7},{8,9},{10,11},{12,13},{14,15},{16,17},{18,... | collective-permute-start | bytes 393224 | tf_op jit(solution)/shard_map/ppermute | solution.py:432
  8.6 1.8 %collective-permute-done.outer_ref = f32[2,4,2,16,128]{4,3,2,1,0:T(8,128)S(1)} collective-permute-done((f32[2,4,2,16,128]{4,3,2,1,0:T(8,128)S(1)}, f32[2,4,2,16,128]{4,3,2,1,0:T(8,128)S(1)}, u32[]{:S(2)}, u32[]{:S(2)}) %collective-permute-start) | collective-permute-done | bytes 131104 | tf_op jit(solution)/shard_map/ppermute | solution.py:431
  10.4 0.0 collective-permute-done.1.inner_ref
  10.4 0.2 shard_map.30
  10.6 3.8 %collective-permute-start.2 = (f32[30,16,128]{2,1,0:T(8,128)S(1)}, f32[30,16,128]{2,1,0:T(8,128)S(1)}, u32[]{:S(2)}, u32[]{:S(2)}) collective-permute-start(f32[30,16,128]{2,1,0:T(8,128)S(1)} %shard_map.30), channel_id=1, source_target_pairs={{0,32},{32,64},{64,96},{96,128},{128,160},{160,192},{192,224},{224... | collective-permute-start | bytes 737288 | tf_op jit(solution)/shard_map/ppermute | solution.py:434
  14.4 0.2 shard_map.31.coef_ref
  14.7 1.3 %collective-permute-start.3 = (f32[8,128]{1,0:T(8,128)S(1)}, f32[8,128]{1,0:T(8,128)S(1)}, u32[]{:S(2)}, u32[]{:S(2)}) collective-permute-start(f32[8,128]{1,0:T(8,128)S(1)} %shard_map.31.coef_ref), channel_id=1, source_target_pairs={{32,0},{96,64},{160,128},{224,192},{288,256},{352,320},{416,384},{... | collective-permute-start | bytes 12296 | tf_op jit(solution)/shard_map/ppermute | solution.py:441
  16.0 0.4 shard_map.29
  16.4 3.8 %collective-permute-done.3.other_coef_ref = f32[8,128]{1,0:T(8,128)S(1)} collective-permute-done((f32[8,128]{1,0:T(8,128)S(1)}, f32[8,128]{1,0:T(8,128)S(1)}, u32[]{:S(2)}, u32[]{:S(2)}) %collective-permute-start.3) | collective-permute-done | bytes 4128 | tf_op jit(solution)/shard_map/ppermute | solution.py:441
  20.2 0.0 collective-permute-done.2.prev_ref
  20.2 0.7 %shard_map.32 = (f32[4,8,16,128]{3,2,1,0:T(8,128)S(1)}, f32[32,8,128]{2,1,0:T(8,128)S(1)}) custom-call(f32[4,4,8,16,128]{4,3,2,1,0:T(8,128)S(1)} %get-tuple-element.15.own_ref, f32[2,4,2,16,128]{4,3,2,1,0:T(8,128)S(1)} %collective-permute-done.outer_ref, f32[2,4,2,16,128]{4,3,2,1,0:T(8,128)S(1)} %collective-permute-done.1.inner_ref, ...), custom_call_target="tpu_custom_call" | custom-call | tf_op jit(solution)/shard_map/pallas_call | solution.py:442
  20.9 13.2 %all_to_all.10.all_ref = f32[32,8,128]{2,1,0:T(8,128)S(1)} all-to-all(f32[32,8,128]{2,1,0:T(8,128)S(1)} %get-tuple-element.22), channel_id=1, replica_groups=mesh['tm'=16,'space'=32] {'space'}, dimensions={0} | all-to-all | bytes 262144 | tf_op jit(solution)/shard_map/all_to_all | solution.py:452
  34.1 23.9 %all_to_all.11.all_ref = f32[8,2,16,128]{3,2,1,0:T(8,128)S(1)} all-to-all(f32[8,2,16,128]{3,2,1,0:T(8,128)S(1)} %shard_map.33), channel_id=1, replica_groups={{0,32,64,96,128,160,192,224},{256,288,320,352,384,416,448,480},{1,33,65..., dimensions={0} | all-to-all | bytes 262144 | tf_op jit(solution)/shard_map/all_to_all | solution.py:460
  58.0 0.7 %shard_map.34 = (f32[5,16,128]{2,1,0:T(8,128)S(1)}, f32[16,128]{1,0:T(8,128)S(1)}) custom-call(f32[8,2,16,128]{3,2,1,0:T(8,128)S(1)} %all_to_all.11.all_ref), custom_call_target="tpu_custom_call" | custom-call | tf_op jit(solution)/shard_map/pallas_call | solution.py:462
  58.7 1.6 %collective-permute-start.4 = (f32[5,16,128]{2,1,0:T(8,128)S(1)}, f32[5,16,128]{2,1,0:T(8,128)S(1)}, u32[]{:S(2)}, u32[]{:S(2)}) collective-permute-start(f32[5,16,128]{2,1,0:T(8,128)S(1)} %get-tuple-element.23), channel_id=1, source_target_pairs={{128,256},{160,288},{192,320},{224,352},{0,384},{32,416},{64,448},... | collective-permute-start | bytes 122888 | tf_op jit(solution)/shard_map/ppermute | solution.py:466
  60.3 0.9 %shard_map.35._ = f32[4,8,16,128]{3,2,1,0:T(8,128)} custom-call(f32[4,8,16,128]{3,2,1,0:T(8,128)S(1)} %get-tuple-element.21.lp_ref, f32[16,128]{1,0:T(8,128)S(1)} %get-tuple-element.24.mine_ref), custom_call_target="tpu_custom_call" | custom-call | tf_op jit(solution)/shard_map/pallas_call | solution.py:468
  61.2 1.5 %collective-permute-done.4.bound_ref = f32[5,16,128]{2,1,0:T(8,128)S(1)} collective-permute-done((f32[5,16,128]{2,1,0:T(8,128)S(1)}, f32[5,16,128]{2,1,0:T(8,128)S(1)}, u32[]{:S(2)}, u32[]{:S(2)}) %collective-permute-start.4) | collective-permute-done | bytes 40992 | tf_op jit(solution)/shard_map/ppermute | solution.py:466
  62.7 0.1 shard_map.36
  (1 shorter events, 0.0 us)
Async XLA Ops:
  0.0 0.9 %copy-start = (f32[4,8,16,128]{3,2,1,0:T(8,128)S(1)}, f32[4,8,16,128]{3,2,1,0:T(8,128)}, u32[]{:S(2)}) copy-start(f32[4,8,16,128]{3,2,1,0:T(8,128)} %rhs_ref.1) | copy-start | bytes 786436
  1.0 0.9 %copy-start.1 = (f32[4,8,16,128]{3,2,1,0:T(8,128)S(1)}, f32[4,8,16,128]{3,2,1,0:T(8,128)}, u32[]{:S(2)}) copy-start(f32[4,8,16,128]{3,2,1,0:T(8,128)} %state_ref.1) | copy-start | bytes 786436
  2.0 8.4 %collective-permute-start = (f32[2,4,2,16,128]{4,3,2,1,0:T(8,128)S(1)}, f32[2,4,2,16,128]{4,3,2,1,0:T(8,128)S(1)}, u32[]{:S(2)}, u32[]{:S(2)}) collective-permute-start(f32[2,4,2,16,128]{4,3,2,1,0:T(8,128)S(1)} %get-tuple-element.16), channel_id=1, source_target_pairs={{1,2},{3,4},{5,6},{7,8},{9,10},{11,12},{13,14},{15,16},{17,18},{19... | collective-permute-start | bytes 393224 | tf_op jit(solution)/shard_map/ppermute | solution.py:431
  6.6 3.8 %collective-permute-start.1 = (f32[2,4,2,16,128]{4,3,2,1,0:T(8,128)S(1)}, f32[2,4,2,16,128]{4,3,2,1,0:T(8,128)S(1)}, u32[]{:S(2)}, u32[]{:S(2)}) collective-permute-start(f32[2,4,2,16,128]{4,3,2,1,0:T(8,128)S(1)} %get-tuple-element.17), channel_id=1, source_target_pairs={{0,1},{2,3},{4,5},{6,7},{8,9},{10,11},{12,13},{14,15},{16,17},{18,... | collective-permute-start | bytes 393224 | tf_op jit(solution)/shard_map/ppermute | solution.py:432
  10.6 9.6 %collective-permute-start.2 = (f32[30,16,128]{2,1,0:T(8,128)S(1)}, f32[30,16,128]{2,1,0:T(8,128)S(1)}, u32[]{:S(2)}, u32[]{:S(2)}) collective-permute-start(f32[30,16,128]{2,1,0:T(8,128)S(1)} %shard_map.30), channel_id=1, source_target_pairs={{0,32},{32,64},{64,96},{96,128},{128,160},{160,192},{192,224},{224... | collective-permute-start | bytes 737288 | tf_op jit(solution)/shard_map/ppermute | solution.py:434
  14.7 5.5 %collective-permute-start.3 = (f32[8,128]{1,0:T(8,128)S(1)}, f32[8,128]{1,0:T(8,128)S(1)}, u32[]{:S(2)}, u32[]{:S(2)}) collective-permute-start(f32[8,128]{1,0:T(8,128)S(1)} %shard_map.31.coef_ref), channel_id=1, source_target_pairs={{32,0},{96,64},{160,128},{224,192},{288,256},{352,320},{416,384},{... | collective-permute-start | bytes 12296 | tf_op jit(solution)/shard_map/ppermute | solution.py:441
  58.7 4.0 %collective-permute-start.4 = (f32[5,16,128]{2,1,0:T(8,128)S(1)}, f32[5,16,128]{2,1,0:T(8,128)S(1)}, u32[]{:S(2)}, u32[]{:S(2)}) collective-permute-start(f32[5,16,128]{2,1,0:T(8,128)S(1)} %get-tuple-element.23), channel_id=1, source_target_pairs={{128,256},{160,288},{192,320},{224,352},{0,384},{32,416},{64,448},... | collective-permute-start | bytes 122888 | tf_op jit(solution)/shard_map/ppermute | solution.py:466

commit v4 on v3

--- a/solution.py
+++ b/solution.py
@@ -66,11 +66,11 @@
         body(second, first)
 
 
-def first_kernel(rhs_ref, state_ref, own_ref, outer_ref, inner_ref):
+def first_kernel(loaded_ref, own_ref, outer_ref, inner_ref):
     def body(low_ref, high_ref):
         for t in range(CT):
             for z in range(CZ):
-                rhs, s = rhs_ref[t, z], state_ref[t, z]
+                rhs, s = loaded_ref[0, t, z], loaded_ref[1, t, z]
                 diag = (rate + 6.0 - react) + (3.0 * react) * (s * s)
                 scale = damp / diag
                 first = scale * rhs
@@ -425,8 +425,8 @@
     onward = [(i, i + 1) for i in range(slabs - 1)]
 
     edge = arr(2, CT, OV, CX, CY)
-    own, outer, inner = call(first_kernel, [arr(4, CT, CZ, CX, CY), edge, edge], 2)(
-        right_side, state
+    own, outer, inner = call(first_kernel, [arr(4, CT, CZ, CX, CY), edge, edge], 1)(
+        jnp.stack([right_side, state])
     )
     outer = lax.ppermute(outer, "space", across)
     inner = lax.ppermute(inner, "space", within)
@@ -461,8 +461,8 @@
     found = pltpu.VMEM((half // 2, WINDOW, LANES), F32)
     last, mine = call(bound_kernel, [arr(5, WINDOW, LANES), arr(WINDOW, LANES)], 1, [found])(every)
     quarter = half // 2
-    serve = [(i, i + quarter) for i in range(quarter, half)]
-    serve += [(i, i + half + quarter) for i in range(quarter)]
+    serve = [(i, i + quarter) for i in range(quarter, half)] + [(0, slabs - 1), (1, slabs - 2)]
+    serve += [(i, half + quarter + i - 2) for i in range(2, quarter)]
     bound = lax.ppermute(last, "tm", serve)
     shape = arr(CT, CZ, CX, CY)
     result = call(result_kernel, shape, 2)(lp, mine)

time: 63.8 us -> 63.3 us (level)
  local copies, waits for them, and re-layouts: 1.9 us -> 0 us
  other arithmetic: 0 us -> 1.06 us
    unnamed x4 -> x0, local copies, waits for them, and re-layouts: 1.9 us -> none
    another operation x0 -> x1, other arithmetic: none -> 1.06 us  [local(): jnp.stack([right_side, state])]
where the time goes in v4:
time: 63.3 us; the launch traced here: 62.2 us
  blocking collectives  37.1 us (59%)
  starting transfers between devices  13.2 us (21%)
  waiting for transfers between devices  7.43 us (12%)
  Pallas kernels  3.34 us (5%)
  other arithmetic  1.06 us (2%)
    all_to_all x1, blocking collectives, local(): every = lax.all_to_all(window, 'tm', 0, 0, axis_index_groups=halves)  23.9 us
    all_to_all x1, blocking collectives, local(): column = lax.all_to_all(sums, 'space', 0, 0)  13.2 us
    ppermute x1, starting transfers between devices, local(): outer = lax.ppermute(outer, 'space', across)  4.63 us
    ppermute x1, starting transfers between devices, local(): prev = lax.ppermute(sent, 'tm', onward)  3.84 us
    ppermute x1, waiting for transfers between devices, local(): lax.ppermute(coef, 'tm', [(i, i - 1) for i in range(1, slabs, 2)])  3.77 us
    ppermute x1, starting transfers between devices, local(): inner = lax.ppermute(inner, 'space', within)  1.92 us
    ppermute x1, waiting for transfers between devices, local(): outer = lax.ppermute(outer, 'space', across)  1.83 us
    ppermute x1, waiting for transfers between devices, local(): bound = lax.ppermute(last, 'tm', serve)  1.82 us
  transfers between devices with their start and end apart: 5, of which 3 were waited for; matrix products, arithmetic and copies ran while one was open for 0% of the time, Pallas kernels for 2%

profile of v4, /device:TPU:6, one launch (start us, length us, event | category | flops | bytes accessed | tf_op | source)
XLA Modules:
  0.0 62.2 jit_solution(9512316504622074097)
XLA Ops:
  0.0 1.1 %pad_maximum_fusion.loaded_ref = f32[2,4,8,16,128]{4,3,2,1,0:T(8,128)S(1)} fusion(f32[1,4,8,16,128]{4,3,2,1,0:T(8,128)} %bitcast.2, f32[1,4,8,16,128]{4,3,2,1,0:T(8,128)} %bitcast.3), kind=kLoop, calls=%fused_computation | loop fusion | flops 131072 | bytes 1048576 | tf_op jit(solution)/shard_map/stack | solution.py:429
  1.1 0.1 shard_map.28
  1.2 4.6 %collective-permute-start = (f32[2,4,2,16,128]{4,3,2,1,0:T(8,128)S(1)}, f32[2,4,2,16,128]{4,3,2,1,0:T(8,128)S(1)}, u32[]{:S(2)}, u32[]{:S(2)}) collective-permute-start(f32[2,4,2,16,128]{4,3,2,1,0:T(8,128)S(1)} %get-tuple-element.16), channel_id=1, source_target_pairs={{1,2},{3,4},{5,6},{7,8},{9,10},{11,12},{13,14},{15,16},{17,18},{19... | collective-permute-start | bytes 393224 | tf_op jit(solution)/shard_map/ppermute | solution.py:431
  5.8 1.9 %collective-permute-start.1 = (f32[2,4,2,16,128]{4,3,2,1,0:T(8,128)S(1)}, f32[2,4,2,16,128]{4,3,2,1,0:T(8,128)S(1)}, u32[]{:S(2)}, u32[]{:S(2)}) collective-permute-start(f32[2,4,2,16,128]{4,3,2,1,0:T(8,128)S(1)} %get-tuple-element.17), channel_id=1, source_target_pairs={{0,1},{2,3},{4,5},{6,7},{8,9},{10,11},{12,13},{14,15},{16,17},{18,... | collective-permute-start | bytes 393224 | tf_op jit(solution)/shard_map/ppermute | solution.py:432
  7.7 1.8 %collective-permute-done.outer_ref = f32[2,4,2,16,128]{4,3,2,1,0:T(8,128)S(1)} collective-permute-done((f32[2,4,2,16,128]{4,3,2,1,0:T(8,128)S(1)}, f32[2,4,2,16,128]{4,3,2,1,0:T(8,128)S(1)}, u32[]{:S(2)}, u32[]{:S(2)}) %collective-permute-start) | collective-permute-done | bytes 131104 | tf_op jit(solution)/shard_map/ppermute | solution.py:431
  9.6 0.0 collective-permute-done.1.inner_ref
  9.6 0.2 shard_map.30
  9.8 3.8 %collective-permute-start.2 = (f32[30,16,128]{2,1,0:T(8,128)S(1)}, f32[30,16,128]{2,1,0:T(8,128)S(1)}, u32[]{:S(2)}, u32[]{:S(2)}) collective-permute-start(f32[30,16,128]{2,1,0:T(8,128)S(1)} %shard_map.30), channel_id=1, source_target_pairs={{0,32},{32,64},{64,96},{96,128},{128,160},{160,192},{192,224},{224... | collective-permute-start | bytes 737288 | tf_op jit(solution)/shard_map/ppermute | solution.py:434
  13.6 0.2 shard_map.31.coef_ref
  13.9 1.3 %collective-permute-start.3 = (f32[8,128]{1,0:T(8,128)S(1)}, f32[8,128]{1,0:T(8,128)S(1)}, u32[]{:S(2)}, u32[]{:S(2)}) collective-permute-start(f32[8,128]{1,0:T(8,128)S(1)} %shard_map.31.coef_ref), channel_id=1, source_target_pairs={{32,0},{96,64},{160,128},{224,192},{288,256},{352,320},{416,384},{... | collective-permute-start | bytes 12296 | tf_op jit(solution)/shard_map/ppermute | solution.py:441
  15.2 0.4 shard_map.29
  15.6 3.8 %collective-permute-done.3.other_coef_ref = f32[8,128]{1,0:T(8,128)S(1)} collective-permute-done((f32[8,128]{1,0:T(8,128)S(1)}, f32[8,128]{1,0:T(8,128)S(1)}, u32[]{:S(2)}, u32[]{:S(2)}) %collective-permute-start.3) | collective-permute-done | bytes 4128 | tf_op jit(solution)/shard_map/ppermute | solution.py:441
  19.4 0.0 collective-permute-done.2.prev_ref
  19.4 0.7 %shard_map.32 = (f32[4,8,16,128]{3,2,1,0:T(8,128)S(1)}, f32[32,8,128]{2,1,0:T(8,128)S(1)}) custom-call(f32[4,4,8,16,128]{4,3,2,1,0:T(8,128)S(1)} %get-tuple-element.15.own_ref, f32[2,4,2,16,128]{4,3,2,1,0:T(8,128)S(1)} %collective-permute-done.outer_ref, f32[2,4,2,16,128]{4,3,2,1,0:T(8,128)S(1)} %collective-permute-done.1.inner_ref, ...), custom_call_target="tpu_custom_call" | custom-call | tf_op jit(solution)/shard_map/pallas_call | solution.py:442
  20.0 13.2 %all_to_all.10.all_ref = f32[32,8,128]{2,1,0:T(8,128)S(1)} all-to-all(f32[32,8,128]{2,1,0:T(8,128)S(1)} %get-tuple-element.22), channel_id=1, replica_groups=mesh['tm'=16,'space'=32] {'space'}, dimensions={0} | all-to-all | bytes 262144 | tf_op jit(solution)/shard_map/all_to_all | solution.py:452
  33.3 23.9 %all_to_all.11.all_ref = f32[8,2,16,128]{3,2,1,0:T(8,128)S(1)} all-to-all(f32[8,2,16,128]{3,2,1,0:T(8,128)S(1)} %shard_map.33), channel_id=1, replica_groups={{0,32,64,96,128,160,192,224},{256,288,320,352,384,416,448,480},{1,33,65..., dimensions={0} | all-to-all | bytes 262144 | tf_op jit(solution)/shard_map/all_to_all | solution.py:460
  57.2 0.7 %shard_map.34 = (f32[5,16,128]{2,1,0:T(8,128)S(1)}, f32[16,128]{1,0:T(8,128)S(1)}) custom-call(f32[8,2,16,128]{3,2,1,0:T(8,128)S(1)} %all_to_all.11.all_ref), custom_call_target="tpu_custom_call" | custom-call | tf_op jit(solution)/shard_map/pallas_call | solution.py:462
  57.9 1.5 %collective-permute-start.4 = (f32[5,16,128]{2,1,0:T(8,128)S(1)}, f32[5,16,128]{2,1,0:T(8,128)S(1)}, u32[]{:S(2)}, u32[]{:S(2)}) collective-permute-start(f32[5,16,128]{2,1,0:T(8,128)S(1)} %get-tuple-element.23), channel_id=1, source_target_pairs={{128,256},{160,288},{192,320},{224,352},{0,480},{32,448},{64,384},... | collective-permute-start | bytes 122888 | tf_op jit(solution)/shard_map/ppermute | solution.py:466
  59.5 0.9 %shard_map.35._ = f32[4,8,16,128]{3,2,1,0:T(8,128)} custom-call(f32[4,8,16,128]{3,2,1,0:T(8,128)S(1)} %get-tuple-element.21.lp_ref, f32[16,128]{1,0:T(8,128)S(1)} %get-tuple-element.24.mine_ref), custom_call_target="tpu_custom_call" | custom-call | tf_op jit(solution)/shard_map/pallas_call | solution.py:468
  60.3 1.8 %collective-permute-done.4.bound_ref = f32[5,16,128]{2,1,0:T(8,128)S(1)} collective-permute-done((f32[5,16,128]{2,1,0:T(8,128)S(1)}, f32[5,16,128]{2,1,0:T(8,128)S(1)}, u32[]{:S(2)}, u32[]{:S(2)}) %collective-permute-start.4) | collective-permute-done | bytes 40992 | tf_op jit(solution)/shard_map/ppermute | solution.py:466
  62.2 0.1 shard_map.36
  (1 shorter events, 0.0 us)
Async XLA Ops:
  1.2 8.4 %collective-permute-start = (f32[2,4,2,16,128]{4,3,2,1,0:T(8,128)S(1)}, f32[2,4,2,16,128]{4,3,2,1,0:T(8,128)S(1)}, u32[]{:S(2)}, u32[]{:S(2)}) collective-permute-start(f32[2,4,2,16,128]{4,3,2,1,0:T(8,128)S(1)} %get-tuple-element.16), channel_id=1, source_target_pairs={{1,2},{3,4},{5,6},{7,8},{9,10},{11,12},{13,14},{15,16},{17,18},{19... | collective-permute-start | bytes 393224 | tf_op jit(solution)/shard_map/ppermute | solution.py:431
  5.8 3.8 %collective-permute-start.1 = (f32[2,4,2,16,128]{4,3,2,1,0:T(8,128)S(1)}, f32[2,4,2,16,128]{4,3,2,1,0:T(8,128)S(1)}, u32[]{:S(2)}, u32[]{:S(2)}) collective-permute-start(f32[2,4,2,16,128]{4,3,2,1,0:T(8,128)S(1)} %get-tuple-element.17), channel_id=1, source_target_pairs={{0,1},{2,3},{4,5},{6,7},{8,9},{10,11},{12,13},{14,15},{16,17},{18,... | collective-permute-start | bytes 393224 | tf_op jit(solution)/shard_map/ppermute | solution.py:432
  9.8 9.6 %collective-permute-start.2 = (f32[30,16,128]{2,1,0:T(8,128)S(1)}, f32[30,16,128]{2,1,0:T(8,128)S(1)}, u32[]{:S(2)}, u32[]{:S(2)}) collective-permute-start(f32[30,16,128]{2,1,0:T(8,128)S(1)} %shard_map.30), channel_id=1, source_target_pairs={{0,32},{32,64},{64,96},{96,128},{128,160},{160,192},{192,224},{224... | collective-permute-start | bytes 737288 | tf_op jit(solution)/shard_map/ppermute | solution.py:434
  13.9 5.5 %collective-permute-start.3 = (f32[8,128]{1,0:T(8,128)S(1)}, f32[8,128]{1,0:T(8,128)S(1)}, u32[]{:S(2)}, u32[]{:S(2)}) collective-permute-start(f32[8,128]{1,0:T(8,128)S(1)} %shard_map.31.coef_ref), channel_id=1, source_target_pairs={{32,0},{96,64},{160,128},{224,192},{288,256},{352,320},{416,384},{... | collective-permute-start | bytes 12296 | tf_op jit(solution)/shard_map/ppermute | solution.py:441
  57.9 4.3 %collective-permute-start.4 = (f32[5,16,128]{2,1,0:T(8,128)S(1)}, f32[5,16,128]{2,1,0:T(8,128)S(1)}, u32[]{:S(2)}, u32[]{:S(2)}) collective-permute-start(f32[5,16,128]{2,1,0:T(8,128)S(1)} %get-tuple-element.23), channel_id=1, source_target_pairs={{128,256},{160,288},{192,320},{224,352},{0,480},{32,448},{64,384},... | collective-permute-start | bytes 122888 | tf_op jit(solution)/shard_map/ppermute | solution.py:466

commit v5 on v4

--- a/solution.py
+++ b/solution.py
@@ -132,38 +132,52 @@
     return jnp.where(lax.shift_right_logical(x, 2) == lax.shift_right_logical(lane, 5), 1.0, 0.0)
 
 
-def early_kernel(own_ref, outer_ref, inner_ref, v2_ref, v3_ref, v4_ref):
+def early_kernel(own_ref, outer_ref, inner_ref, v2_ref, v3_ref, v4_ref, rest_ref):
     def body(low_ref, high_ref):
         scale = reader(0, own_ref, low_ref, high_ref)
         first = reader(1, own_ref, low_ref, high_ref)
-        for t in range(1, CT):
+        for t in range(CT):
             for z in range(-2, CZ + 2):
                 v = first(t, z)
                 near = [first(t, q) for q in (z - 1, z + 1) if -2 <= q < CZ + 2]
-                v2_ref[t - 1, z + 2] = swept(v, v, scale(t, z), near, first(t - 1, z))
+                before = first(t - 1, z) if t > 0 else None
+                v2_ref[t, z + 2] = swept(v, v, scale(t, z), near, before)
+        for t in range(1, CT):
+            for z in range(-1, CZ + 1):
+                near = (v2_ref[t, z + 1], v2_ref[t, z + 3])
+                before = v2_ref[t - 1, z + 2] if t > 1 else None
+                v3_ref[t - 1, z + 1] = swept(
+                    v2_ref[t, z + 2], first(t, z), scale(t, z), near, before
+                )
         for t in range(2, CT):
-            for z in range(-1, CZ + 1):
-                near = (v2_ref[t - 1, z + 1], v2_ref[t - 1, z + 3])
-                v3_ref[t - 2, z + 1] = swept(
-                    v2_ref[t - 1, z + 2], first(t, z), scale(t, z), near, v2_ref[t - 2, z + 2]
+            for z in range(CZ):
+                near = (v3_ref[t - 1, z], v3_ref[t - 1, z + 2])
+                before = v3_ref[t - 2, z + 1] if t > 2 else None
+                v4_ref[t - 2, z] = swept(
+                    v3_ref[t - 1, z + 1], first(t, z), scale(t, z), near, before
                 )
-        t = CT - 1
-        for z in range(CZ):
-            near = (v3_ref[t - 2, z], v3_ref[t - 2, z + 2])
-            v4_ref[z] = swept(
-                v3_ref[t - 2, z + 1], first(t, z), scale(t, z), near, v3_ref[t - 3, z + 1]
-            )
 
     by_parity(body, outer_ref, inner_ref)
+    for z in range(CZ):
+        rest = own_ref[3, 0, z] - own_ref[2, CT - 1, z] * v4_ref[1, z]
+        for t in range(1, CT):
+            rest = rest + own_ref[3, t, z]
+        rest_ref[z] = rest
+
+
+def exact_dot(x, ones):
+    parts = []
+    for _ in range(3):
+        part = x.astype(jnp.bfloat16)
+        parts.append(part)
+        x = x - part.astype(F32)
+    ones = ones.astype(jnp.bfloat16)
+    high, mid, low = (jnp.dot(part, ones, preferred_element_type=F32) for part in parts)
+    return high + (mid + low)
 
 
 def fold(planes):
-    folded = jnp.dot(
-        planes.reshape(-1, CY),
-        fold_matrix(CY, LANES, True),
-        precision=lax.Precision.HIGHEST,
-        preferred_element_type=F32,
-    )
+    folded = exact_dot(planes.reshape(-1, CY), fold_matrix(CY, LANES, True))
     return jnp.sum(folded.reshape(-1, CX, LANES) * x_mask()[None], axis=1)
 
 
@@ -186,6 +200,7 @@
     v2_ref,
     v3_ref,
     v4_ref,
+    rest_ref,
     prev_ref,
     coef_ref,
     other_coef_ref,
@@ -201,46 +216,36 @@
     def body(low_ref, high_ref):
         scale = reader(0, own_ref, low_ref, high_ref)
         own = reader(1, own_ref, low_ref, high_ref)
-
-        def second(t, z):
-            if t < 0:
-                return prev_ref[off2 + z + 1]
-            return v2[z + 2] if t == 0 else v2_ref[t - 1, z + 2]
-
-        def third(t, z):
-            if t < 0:
-                return prev_ref[z]
-            return v3[t, z + 1] if t < 2 else v3_ref[t - 2, z + 1]
-
         for z in range(-2, CZ + 2):
-            v = own(0, z)
-            near = [own(0, q) for q in (z - 1, z + 1) if -2 <= q < CZ + 2]
-            v2[z + 2] = swept(v, v, scale(0, z), near, prev_ref[off1 + z + 2])
-        for t in range(2):
-            for z in range(-1, CZ + 1):
-                near = (second(t, z - 1), second(t, z + 1))
-                v3[t, z + 1] = swept(second(t, z), own(t, z), scale(t, z), near, second(t - 1, z))
-        for t in range(CT - 1):
-            for z in range(CZ):
-                near = (third(t, z - 1), third(t, z + 1))
-                lp_ref[t, z] = swept(third(t, z), own(t, z), scale(t, z), near, third(t - 1, z))
+            v2[z + 2] = v2_ref[0, z + 2] + rate * scale(0, z) * prev_ref[off1 + z + 2]
+        for z in range(-1, CZ + 1):
+            near = (v2[z + 1], v2[z + 3])
+            before = prev_ref[off2 + z + 1]
+            v3[0, z + 1] = swept(v2[z + 2], own(0, z), scale(0, z), near, before)
+            v3[1, z + 1] = v3_ref[0, z + 1] + rate * scale(1, z) * v2[z + 2]
 
     by_parity(body, outer_ref, inner_ref)
-    for z in range(CZ):
-        lp_ref[CT - 1, z] = v4_ref[z]
 
     rest = []
     planes = []
     for z in range(CZ):
-        part = None
-        for t in range(CT):
-            term = own_ref[3, t, z] - own_ref[2, t, z] * lp_ref[t, z]
-            part = term if part is None else part + term
-        early = lp_ref[0, z]
-        for t in range(1, CT - 1):
-            early = early + lp_ref[t, z]
+        part = rest_ref[z]
+        early = None
+        for t in range(CT - 1):
+            scale = own_ref[0, t, z]
+            if t < 2:
+                before = prev_ref[z] if t == 0 else v3[0, z + 1]
+                near = (v3[t, z], v3[t, z + 2])
+                value = swept(v3[t, z + 1], own_ref[1, t, z], scale, near, before)
+            else:
+                value = v4_ref[0, z] + rate * scale * v3[1, z + 1]
+            lp_ref[t, z] = value
+            part = part - own_ref[2, t, z] * value
+            early = value if early is None else early + value
+        value = v4_ref[1, z]
+        lp_ref[CT - 1, z] = value
         rest.append(part + rate * early)
-        planes.append(early + lp_ref[CT - 1, z])
+        planes.append(early + value)
     odd = (lax.axis_index("tm") & 1) == 1
     for b in range(2):
         z = 4 * b
@@ -249,16 +254,15 @@
         inner = inner + (planes[4] if b == 0 else planes[3])
         value = rest[z] + rest[z + 1] + rest[z + 2] + rest[z + 3]
         value = value + beside(total) + inner
-        last = lp_ref[CT - 1, z] + lp_ref[CT - 1, z + 1]
-        last = rate * (last + (lp_ref[CT - 1, z + 2] + lp_ref[CT - 1, z + 3]))
+        last = v4_ref[1, z] + v4_ref[1, z + 1]
+        last = rate * (last + (v4_ref[1, z + 2] + v4_ref[1, z + 3]))
         stack[b] = jnp.where(odd, value, value + last)
         stack[4 + b] = jnp.where(odd, last, 0.0)
     stack[2] = planes[0]
     stack[3] = planes[CZ - 1]
-    stack[6] = jnp.zeros(PLANE, F32)
-    stack[7] = jnp.zeros(PLANE, F32)
     coef = coef_ref[...] + other_coef_ref[...]
-    sums = fold(stack[...]) + jnp.where(odd, 0.0, coef)
+    none = jnp.zeros((2, LANES), F32)
+    sums = jnp.concatenate([fold(stack[...]), none], axis=0) + jnp.where(odd, 0.0, coef)
     sums_ref[...] = jnp.broadcast_to(sums[None], sums_ref.shape)
 
 
@@ -307,7 +311,7 @@
         if k > 0:
             rhs = rhs + all_ref[2 * k - 1, 1]
         elif bound_ref is not None:
-            rhs = rhs + bound_ref[4]
+            rhs = rhs + handed(bound_ref, 4)
         coef = all_ref[2 * k, 1]
         inv = 1.0 / (1.375 + (react / 512.0) * coef)
         inverse.append(inv)
@@ -325,7 +329,7 @@
             if k > 0:
                 flow = flow + step[k - 1]
             elif bound_ref is not None:
-                flow = flow + (bound_ref[m - 1] if m <= 4 else swapped(bound_ref[7 - m]))
+                flow = flow + handed(bound_ref, m - 1 if m <= 4 else m)
             flows.append(flow)
         for k in range(slots):
             resid[k] = resid[k] - step[k] + flows[k] * inverse[k]
@@ -339,6 +343,15 @@
     return jnp.concatenate([v[WINDOW // 2 :], v[: WINDOW // 2]], axis=0)
 
 
+def handed(bound_ref, k):
+    if k == 3:
+        none = jnp.zeros((WINDOW // 4, LANES), F32)
+        return jnp.concatenate([none, bound_ref[6], none], axis=0)
+    at = (0, 2, 4, None, 7, 4, 2, 0)[k]
+    both = (bound_ref[at], bound_ref[at + 1])
+    return jnp.concatenate(both if k <= 4 else both[::-1], axis=0)
+
+
 def bound_kernel(all_ref, out_ref, mine_ref, found):
     @pl.when(lax.axis_index("tm") < all_ref.shape[0])
     def _():
@@ -346,9 +359,12 @@
         row = lax.broadcasted_iota(jnp.int32, (WINDOW, LANES), 0)
         for m in range(3):
             used = (row > m) & (row < WINDOW - 1 - m)
-            out_ref[m] = jnp.where(used, last[m], swapped(last[6 - m]))
-        out_ref[3] = last[3]
-        out_ref[4] = all_ref[all_ref.shape[0] - 1, 1]
+            block = jnp.where(used, last[m], swapped(last[6 - m]))
+            out_ref[2 * m], out_ref[2 * m + 1] = block[: WINDOW // 2], block[WINDOW // 2 :]
+        out_ref[6] = last[3][WINDOW // 4 : 3 * WINDOW // 4]
+        for h in range(2):
+            half = pl.ds(h * WINDOW // 2, WINDOW // 2)
+            out_ref[7 + h] = all_ref[all_ref.shape[0] - 1, 1, half]
         mine_ref[...] = own_slot(sol, found)
 
 
@@ -362,12 +378,7 @@
     mask = x_mask()
     mine = 2 * NEAR - 1
     both = [window[mine + b : mine + b + 1] * mask for b in range(2)]
-    fine = jnp.dot(
-        jnp.concatenate(both, axis=0),
-        fold_matrix(LANES, CY, False),
-        precision=lax.Precision.HIGHEST,
-        preferred_element_type=F32,
-    )
+    fine = exact_dot(jnp.concatenate(both, axis=0), fold_matrix(LANES, CY, False))
     return [fine[b * CX : (b + 1) * CX] for b in range(2)]
 
 
@@ -432,9 +443,14 @@
     inner = lax.ppermute(inner, "space", within)
     sent = call(later_kernel, arr(3 * CZ + 6, CX, CY), 3)(own, outer, inner)
     prev = lax.ppermute(sent, "tm", onward)
-    v2, v3, v4 = call(
+    v2, v3, v4, rest = call(
         early_kernel,
-        [arr(CT - 1, CZ + 4, CX, CY), arr(CT - 2, CZ + 2, CX, CY), arr(CZ, CX, CY)],
+        [
+            arr(CT, CZ + 4, CX, CY),
+            arr(CT - 1, CZ + 2, CX, CY),
+            arr(CT - 2, CZ, CX, CY),
+            arr(CZ, CX, CY),
+        ],
         3,
     )(own, outer, inner)
     coef = call(coef_kernel, arr(8, LANES), 1, [pltpu.VMEM((8, CX, CY), F32)])(own)
@@ -442,13 +458,13 @@
     lp, sums = call(
         main_kernel,
         [arr(CT, CZ, CX, CY), arr(planes, 8, LANES)],
-        9,
+        10,
         [
             pltpu.VMEM((CZ + 4, CX, CY), F32),
             pltpu.VMEM((2, CZ + 2, CX, CY), F32),
-            pltpu.VMEM((8, CX, CY), F32),
+            pltpu.VMEM((6, CX, CY), F32),
         ],
-    )(own, outer, inner, v2, v3, v4, prev, coef, other_coef)
+    )(own, outer, inner, v2, v3, v4, rest, prev, coef, other_coef)
     column = lax.all_to_all(sums, "space", 0, 0)
     window = call(
         window_kernel,
@@ -459,10 +475,10 @@
     halves = [list(range(half)), list(range(half, slabs))]
     every = lax.all_to_all(window, "tm", 0, 0, axis_index_groups=halves)
     found = pltpu.VMEM((half // 2, WINDOW, LANES), F32)
-    last, mine = call(bound_kernel, [arr(5, WINDOW, LANES), arr(WINDOW, LANES)], 1, [found])(every)
+    last, mine = call(bound_kernel, [arr(9, WINDOW // 2, LANES), arr(WINDOW, LANES)], 1, [found])(every)
     quarter = half // 2
-    serve = [(i, i + quarter) for i in range(quarter, half)] + [(0, slabs - 1), (1, slabs - 2)]
-    serve += [(i, half + quarter + i - 2) for i in range(2, quarter)]
+    order = (0, 2, 1, 3, 5, 6, 4, 7) if half == 8 else tuple(range(half))
+    serve = [((quarter + k) % half, half + order[k]) for k in range(half)]
     bound = lax.ppermute(last, "tm", serve)
     shape = arr(CT, CZ, CX, CY)
     result = call(result_kernel, shape, 2)(lp, mine)

time: 63.3 us -> 62.5 us (0.987)
  the two profiles are of different devices: /device:TPU:6 before, /device:TPU:320 now
where the time goes in v5:
time: 62.5 us; the launch traced here: 62.2 us
  blocking collectives  28.2 us (45%)
  waiting for transfers between devices  14.7 us (24%)
  starting transfers between devices  14 us (22%)
  Pallas kernels  4.18 us (7%)
  other arithmetic  1.06 us (2%)
    all_to_all x1, blocking collectives, local(): every = lax.all_to_all(window, 'tm', 0, 0, axis_index_groups=halves)  16.6 us
    all_to_all x1, blocking collectives, local(): column = lax.all_to_all(sums, 'space', 0, 0)  11.6 us
    ppermute x1, waiting for transfers between devices, local(): bound = lax.ppermute(last, 'tm', serve)  8.48 us
    ppermute x1, starting transfers between devices, local(): outer = lax.ppermute(outer, 'space', across)  6.56 us
    ppermute x1, waiting for transfers between devices, local(): lax.ppermute(coef, 'tm', [(i, i - 1) for i in range(1, slabs, 2)])  3.65 us
    ppermute x1, starting transfers between devices, local(): prev = lax.ppermute(sent, 'tm', onward)  2.93 us
    ppermute x1, starting transfers between devices, local(): inner = lax.ppermute(inner, 'space', within)  1.92 us
    pallas_call x1, Pallas kernels, local(): pl.pallas_call(second_half_kernel, out_shape=shape, in_specs=[VMEM, VMEM,...  1.71 us
  transfers between devices with their start and end apart: 5, of which 5 were waited for; matrix products, arithmetic and copies ran while one was open for 0% of the time, Pallas kernels for 3%

profile of v5, /device:TPU:320, one launch (start us, length us, event | category | flops | bytes accessed | tf_op | source)
XLA Modules:
  0.0 62.2 jit_solution(7687966068037765084)
XLA Ops:
  0.0 1.1 %pad_maximum_fusion.loaded_ref = f32[2,4,8,16,128]{4,3,2,1,0:T(8,128)S(1)} fusion(f32[1,4,8,16,128]{4,3,2,1,0:T(8,128)} %bitcast.2, f32[1,4,8,16,128]{4,3,2,1,0:T(8,128)} %bitcast.3), kind=kLoop, calls=%fused_computation | loop fusion | flops 131072 | bytes 1048576 | tf_op jit(solution)/shard_map/stack | solution.py:440
  1.1 0.1 shard_map.28
  1.2 6.6 %collective-permute-start = (f32[2,4,2,16,128]{4,3,2,1,0:T(8,128)S(1)}, f32[2,4,2,16,128]{4,3,2,1,0:T(8,128)S(1)}, u32[]{:S(2)}, u32[]{:S(2)}) collective-permute-start(f32[2,4,2,16,128]{4,3,2,1,0:T(8,128)S(1)} %get-tuple-element.17), channel_id=1, source_target_pairs={{1,2},{3,4},{5,6},{7,8},{9,10},{11,12},{13,14},{15,16},{17,18},{19... | collective-permute-start | bytes 393224 | tf_op jit(solution)/shard_map/ppermute | solution.py:442
  7.7 1.9 %collective-permute-start.1 = (f32[2,4,2,16,128]{4,3,2,1,0:T(8,128)S(1)}, f32[2,4,2,16,128]{4,3,2,1,0:T(8,128)S(1)}, u32[]{:S(2)}, u32[]{:S(2)}) collective-permute-start(f32[2,4,2,16,128]{4,3,2,1,0:T(8,128)S(1)} %get-tuple-element.18), channel_id=1, source_target_pairs={{0,1},{2,3},{4,5},{6,7},{8,9},{10,11},{12,13},{14,15},{16,17},{18,... | collective-permute-start | bytes 393224 | tf_op jit(solution)/shard_map/ppermute | solution.py:443
  9.7 1.1 %collective-permute-done.outer_ref = f32[2,4,2,16,128]{4,3,2,1,0:T(8,128)S(1)} collective-permute-done((f32[2,4,2,16,128]{4,3,2,1,0:T(8,128)S(1)}, f32[2,4,2,16,128]{4,3,2,1,0:T(8,128)S(1)}, u32[]{:S(2)}, u32[]{:S(2)}) %collective-permute-start) | collective-permute-done | bytes 131104 | tf_op jit(solution)/shard_map/ppermute | solution.py:442
  10.8 0.2 collective-permute-done.1.inner_ref
  11.0 0.2 shard_map.30
  11.2 2.9 %collective-permute-start.2 = (f32[30,16,128]{2,1,0:T(8,128)S(1)}, f32[30,16,128]{2,1,0:T(8,128)S(1)}, u32[]{:S(2)}, u32[]{:S(2)}) collective-permute-start(f32[30,16,128]{2,1,0:T(8,128)S(1)} %shard_map.30), channel_id=1, source_target_pairs={{0,32},{32,64},{64,96},{96,128},{128,160},{160,192},{192,224},{224... | collective-permute-start | bytes 737288 | tf_op jit(solution)/shard_map/ppermute | solution.py:445
  14.1 0.2 shard_map.31.coef_ref
  14.3 1.3 %collective-permute-start.3 = (f32[8,128]{1,0:T(8,128)S(1)}, f32[8,128]{1,0:T(8,128)S(1)}, u32[]{:S(2)}, u32[]{:S(2)}) collective-permute-start(f32[8,128]{1,0:T(8,128)S(1)} %shard_map.31.coef_ref), channel_id=1, source_target_pairs={{32,0},{96,64},{160,128},{224,192},{288,256},{352,320},{416,384},{... | collective-permute-start | bytes 12296 | tf_op jit(solution)/shard_map/ppermute | solution.py:457
  15.6 0.5 shard_map.29
  16.2 3.6 %collective-permute-done.3.other_coef_ref = f32[8,128]{1,0:T(8,128)S(1)} collective-permute-done((f32[8,128]{1,0:T(8,128)S(1)}, f32[8,128]{1,0:T(8,128)S(1)}, u32[]{:S(2)}, u32[]{:S(2)}) %collective-permute-start.3) | collective-permute-done | bytes 4128 | tf_op jit(solution)/shard_map/ppermute | solution.py:457
  19.8 1.3 %collective-permute-done.2.prev_ref = f32[30,16,128]{2,1,0:T(8,128)S(1)} collective-permute-done((f32[30,16,128]{2,1,0:T(8,128)S(1)}, f32[30,16,128]{2,1,0:T(8,128)S(1)}, u32[]{:S(2)}, u32[]{:S(2)}) %collective-permute-start.2) | collective-permute-done | bytes 245792 | tf_op jit(solution)/shard_map/ppermute | solution.py:445
  21.1 0.5 shard_map.32
  21.6 11.6 %all_to_all.10.all_ref = f32[32,8,128]{2,1,0:T(8,128)S(1)} all-to-all(f32[32,8,128]{2,1,0:T(8,128)S(1)} %get-tuple-element.24), channel_id=1, replica_groups=mesh['tm'=16,'space'=32] {'space'}, dimensions={0} | all-to-all | bytes 262144 | tf_op jit(solution)/shard_map/all_to_all | solution.py:468
  33.2 16.6 %all_to_all.11.all_ref = f32[8,2,16,128]{3,2,1,0:T(8,128)S(1)} all-to-all(f32[8,2,16,128]{3,2,1,0:T(8,128)S(1)} %shard_map.33), channel_id=1, replica_groups={{0,32,64,96,128,160,192,224},{256,288,320,352,384,416,448,480},{1,33,65..., dimensions={0} | all-to-all | bytes 262144 | tf_op jit(solution)/shard_map/all_to_all | solution.py:476
  49.9 1.3 %collective-permute-start.4 = (f32[9,8,128]{2,1,0:T(8,128)S(1)}, f32[9,8,128]{2,1,0:T(8,128)S(1)}, u32[]{:S(2)}, u32[]{:S(2)}) collective-permute-start(f32[9,8,128]{2,1,0:T(8,128)S(1)} %get-tuple-element.25), channel_id=1, source_target_pairs={{128,256},{160,320},{192,288},{224,352},{0,416},{32,448},{64,384},... | collective-permute-start | bytes 110600 | tf_op jit(solution)/shard_map/ppermute | solution.py:482
  51.2 0.9 %shard_map.35._ = f32[4,8,16,128]{3,2,1,0:T(8,128)} custom-call(f32[4,8,16,128]{3,2,1,0:T(8,128)S(1)} %get-tuple-element.23.lp_ref, f32[16,128]{1,0:T(8,128)S(1)} %get-tuple-element.26.mine_ref), custom_call_target="tpu_custom_call" | custom-call | tf_op jit(solution)/shard_map/pallas_call | solution.py:484
  52.0 8.5 %collective-permute-done.4.bound_ref = f32[9,8,128]{2,1,0:T(8,128)S(1)} collective-permute-done((f32[9,8,128]{2,1,0:T(8,128)S(1)}, f32[9,8,128]{2,1,0:T(8,128)S(1)}, u32[]{:S(2)}, u32[]{:S(2)}) %collective-permute-start.4) | collective-permute-done | bytes 36896 | tf_op jit(solution)/shard_map/ppermute | solution.py:482
  60.5 1.7 %shard_map.36 = f32[4,8,16,128]{3,2,1,0:T(8,128)} custom-call(f32[4,8,16,128]{3,2,1,0:T(8,128)S(1)} %get-tuple-element.23.lp_ref, f32[8,2,16,128]{3,2,1,0:T(8,128)S(1)} %all_to_all.11.all_ref, f32[9,8,128]{2,1,0:T(8,128)S(1)} %collective-permute-done.4.bound_ref, f32[4,8,16,128]{3,2,1,0:T(8,128)} %shard_map.35._), custom_call_target="tpu_custom_call", output_to_operand_aliasing={{}: (3, {})} | custom-call | tf_op jit(solution)/shard_map/pallas_call | solution.py:486
  (2 shorter events, 0.0 us)
Async XLA Ops:
  1.2 9.6 %collective-permute-start = (f32[2,4,2,16,128]{4,3,2,1,0:T(8,128)S(1)}, f32[2,4,2,16,128]{4,3,2,1,0:T(8,128)S(1)}, u32[]{:S(2)}, u32[]{:S(2)}) collective-permute-start(f32[2,4,2,16,128]{4,3,2,1,0:T(8,128)S(1)} %get-tuple-element.17), channel_id=1, source_target_pairs={{1,2},{3,4},{5,6},{7,8},{9,10},{11,12},{13,14},{15,16},{17,18},{19... | collective-permute-start | bytes 393224 | tf_op jit(solution)/shard_map/ppermute | solution.py:442
  7.7 3.2 %collective-permute-start.1 = (f32[2,4,2,16,128]{4,3,2,1,0:T(8,128)S(1)}, f32[2,4,2,16,128]{4,3,2,1,0:T(8,128)S(1)}, u32[]{:S(2)}, u32[]{:S(2)}) collective-permute-start(f32[2,4,2,16,128]{4,3,2,1,0:T(8,128)S(1)} %get-tuple-element.18), channel_id=1, source_target_pairs={{0,1},{2,3},{4,5},{6,7},{8,9},{10,11},{12,13},{14,15},{16,17},{18,... | collective-permute-start | bytes 393224 | tf_op jit(solution)/shard_map/ppermute | solution.py:443
  11.2 9.9 %collective-permute-start.2 = (f32[30,16,128]{2,1,0:T(8,128)S(1)}, f32[30,16,128]{2,1,0:T(8,128)S(1)}, u32[]{:S(2)}, u32[]{:S(2)}) collective-permute-start(f32[30,16,128]{2,1,0:T(8,128)S(1)} %shard_map.30), channel_id=1, source_target_pairs={{0,32},{32,64},{64,96},{96,128},{128,160},{160,192},{192,224},{224... | collective-permute-start | bytes 737288 | tf_op jit(solution)/shard_map/ppermute | solution.py:445
  14.3 5.5 %collective-permute-start.3 = (f32[8,128]{1,0:T(8,128)S(1)}, f32[8,128]{1,0:T(8,128)S(1)}, u32[]{:S(2)}, u32[]{:S(2)}) collective-permute-start(f32[8,128]{1,0:T(8,128)S(1)} %shard_map.31.coef_ref), channel_id=1, source_target_pairs={{32,0},{96,64},{160,128},{224,192},{288,256},{352,320},{416,384},{... | collective-permute-start | bytes 12296 | tf_op jit(solution)/shard_map/ppermute | solution.py:457
  49.9 10.6 %collective-permute-start.4 = (f32[9,8,128]{2,1,0:T(8,128)S(1)}, f32[9,8,128]{2,1,0:T(8,128)S(1)}, u32[]{:S(2)}, u32[]{:S(2)}) collective-permute-start(f32[9,8,128]{2,1,0:T(8,128)S(1)} %get-tuple-element.25), channel_id=1, source_target_pairs={{128,256},{160,320},{192,288},{224,352},{0,416},{32,448},{64,384},... | collective-permute-start | bytes 110600 | tf_op jit(solution)/shard_map/ppermute | solution.py:482

commit v6 on v5

--- a/solution.py
+++ b/solution.py
@@ -15,6 +15,9 @@
 LANES = 128
 NEAR = 4
 WINDOW = 16
+TURN = 20
+EARLY = (7, 6, 5, 4, 3, 2, 1, 0)
+LATE = (3, 0, 1, 2, 4, 5, 6, 7)
 
 rate = 8.0
 react = 0.5
@@ -269,7 +272,7 @@
 def window_kernel(all_ref, out_ref, rows):
     plane = lax.axis_index("space")
     count = all_ref.shape[0]
-    parts = [all_ref[lax.rem(plane + (count - NEAR + k), count)] for k in range(2 * NEAR + 1)]
+    parts = [all_ref[lax.rem(plane + (2 * count - TURN - NEAR + k), count)] for k in range(2 * NEAR + 1)]
     for k, part in enumerate(parts):
         low, high = part[0:1], part[1:2]
         if k > 0:
@@ -288,31 +291,31 @@
 
 
 def coarse_steps(all_ref, bound_ref):
-    shape = (WINDOW, LANES)
-    lane = lax.broadcasted_iota(jnp.int32, shape, 1) & (CY // 4 - 1)
-    row = lax.broadcasted_iota(jnp.int32, shape, 0)
+    lane = lax.broadcasted_iota(jnp.int32, (WINDOW, LANES), 1) & (CY // 4 - 1)
     width = CY // 4
     is_first, is_last = lane == 0, lane == width - 1
-    bottom, top = row == 0, row == WINDOW - 1
 
     def around(f):
         total = pltpu.roll(f, width, 1) + pltpu.roll(f, LANES - width, 1)
         after = jnp.where(is_last, pltpu.roll(f, width - 1, 1), pltpu.roll(f, LANES - 1, 1))
         before = jnp.where(is_first, pltpu.roll(f, LANES - width + 1, 1), pltpu.roll(f, 1, 1))
-        below = jnp.where(bottom, 0.0, pltpu.roll(f, 1, 0))
-        above = jnp.where(top, 0.0, pltpu.roll(f, WINDOW - 1, 0))
-        return total + (after + before) + (below + above)
+        return (total + (pltpu.roll(f, 1, 0) + pltpu.roll(f, WINDOW - 1, 0))) + (after + before)
 
     slots = all_ref.shape[0] // 2
+    order = EARLY if bound_ref is None else LATE
+
+    def slab(k, which):
+        return all_ref[order.index(k), which]
+
     inverse = []
     resid = []
     for k in range(slots):
-        rhs = all_ref[2 * k, 0] + all_ref[2 * k + 1, 0]
+        rhs = slab(2 * k, 0) + slab(2 * k + 1, 0)
         if k > 0:
-            rhs = rhs + all_ref[2 * k - 1, 1]
+            rhs = rhs + slab(2 * k - 1, 1)
         elif bound_ref is not None:
             rhs = rhs + handed(bound_ref, 4)
-        coef = all_ref[2 * k, 1]
+        coef = slab(2 * k, 1)
         inv = 1.0 / (1.375 + (react / 512.0) * coef)
         inverse.append(inv)
         resid.append((rhs * (1.0 / 512.0)) * inv)
@@ -320,19 +323,21 @@
     sol = list(step)
     rho = delta / theta
     last = []
+    beside = [i * (1.0 / 16.0) for i in inverse]
     for m in range(1, CHEB):
         nxt = 1.0 / (2.0 * theta / delta - rho)
         last.append(step[-1])
-        flows = []
+        known = []
         for k in range(slots):
-            flow = around(step[k]) * (1.0 / 16.0)
+            value = resid[k] - step[k]
             if k > 0:
-                flow = flow + step[k - 1]
+                value = value + step[k - 1] * inverse[k]
             elif bound_ref is not None:
-                flow = flow + handed(bound_ref, m - 1 if m <= 4 else m)
-            flows.append(flow)
+                value = value + handed(bound_ref, m - 1 if m <= 4 else m) * inverse[k]
+            known.append(value)
         for k in range(slots):
-            resid[k] = resid[k] - step[k] + flows[k] * inverse[k]
+            resid[k] = known[k] + around(step[k]) * beside[k]
+        for k in range(slots):
             step[k] = (nxt * rho) * step[k] + (2.0 * nxt / delta) * resid[k]
             sol[k] = sol[k] + step[k]
         rho = nxt
@@ -364,7 +369,7 @@
         out_ref[6] = last[3][WINDOW // 4 : 3 * WINDOW // 4]
         for h in range(2):
             half = pl.ds(h * WINDOW // 2, WINDOW // 2)
-            out_ref[7 + h] = all_ref[all_ref.shape[0] - 1, 1, half]
+            out_ref[7 + h] = all_ref[EARLY.index(all_ref.shape[0] - 1), 1, half]
         mine_ref[...] = own_slot(sol, found)
 
 
@@ -465,14 +470,16 @@
             pltpu.VMEM((6, CX, CY), F32),
         ],
     )(own, outer, inner, v2, v3, v4, rest, prev, coef, other_coef)
-    column = lax.all_to_all(sums, "space", 0, 0)
+    column = lax.all_to_all(
+        sums, "space", 0, 0, axis_index_groups=[[(p + TURN) % planes for p in range(planes)]]
+    )
     window = call(
         window_kernel,
         arr(half, 2, WINDOW, LANES),
         1,
         [pltpu.VMEM((2, WINDOW, LANES), F32)],
     )(column)
-    halves = [list(range(half)), list(range(half, slabs))]
+    halves = [list(EARLY), [half + k for k in LATE]]
     every = lax.all_to_all(window, "tm", 0, 0, axis_index_groups=halves)
     found = pltpu.VMEM((half // 2, WINDOW, LANES), F32)
     last, mine = call(bound_kernel, [arr(9, WINDOW // 2, LANES), arr(WINDOW, LANES)], 1, [found])(every)

time: 62.5 us -> 59.5 us (0.952)
  the two profiles are of different devices: /device:TPU:320 before, /device:TPU:6 now
where the time goes in v6:
time: 59.5 us; the launch traced here: 59 us
  blocking collectives  32.7 us (55%)
  starting transfers between devices  15.2 us (26%)
  waiting for transfers between devices  6.65 us (11%)
  Pallas kernels  3.25 us (5%)
  other arithmetic  1.06 us (2%)
    all_to_all x1, blocking collectives, local(): every = lax.all_to_all(window, 'tm', 0, 0, axis_index_groups=halves)  18.8 us
    all_to_all x1, blocking collectives, local(): lax.all_to_all(sums, 'space', 0, 0, axis_index_groups=[[(p + TURN) % plan...  13.9 us
    ppermute x1, starting transfers between devices, local(): outer = lax.ppermute(outer, 'space', across)  4.63 us
    ppermute x1, starting transfers between devices, local(): prev = lax.ppermute(sent, 'tm', onward)  3.84 us
    ppermute x1, waiting for transfers between devices, local(): lax.ppermute(coef, 'tm', [(i, i - 1) for i in range(1, slabs, 2)])  3.65 us
    ppermute x1, starting transfers between devices, local(): bound = lax.ppermute(last, 'tm', serve)  3.56 us
    ppermute x1, starting transfers between devices, local(): inner = lax.ppermute(inner, 'space', within)  1.92 us
    ppermute x1, waiting for transfers between devices, local(): outer = lax.ppermute(outer, 'space', across)  1.83 us
  transfers between devices with their start and end apart: 5, of which 3 were waited for; matrix products, arithmetic and copies ran while one was open for 0% of the time, Pallas kernels for 3%

profile of v6, /device:TPU:6, one launch (start us, length us, event | category | flops | bytes accessed | tf_op | source)
XLA Modules:
  0.0 59.0 jit_solution(4602928077127558869)
XLA Ops:
  0.0 1.1 %pad_maximum_fusion.loaded_ref = f32[2,4,8,16,128]{4,3,2,1,0:T(8,128)S(1)} fusion(f32[1,4,8,16,128]{4,3,2,1,0:T(8,128)} %bitcast.2, f32[1,4,8,16,128]{4,3,2,1,0:T(8,128)} %bitcast.3), kind=kLoop, calls=%fused_computation | loop fusion | flops 131072 | bytes 1048576 | tf_op jit(solution)/shard_map/stack | solution.py:445
  1.1 0.1 shard_map.28
  1.2 4.6 %collective-permute-start = (f32[2,4,2,16,128]{4,3,2,1,0:T(8,128)S(1)}, f32[2,4,2,16,128]{4,3,2,1,0:T(8,128)S(1)}, u32[]{:S(2)}, u32[]{:S(2)}) collective-permute-start(f32[2,4,2,16,128]{4,3,2,1,0:T(8,128)S(1)} %get-tuple-element.17), channel_id=1, source_target_pairs={{1,2},{3,4},{5,6},{7,8},{9,10},{11,12},{13,14},{15,16},{17,18},{19... | collective-permute-start | bytes 393224 | tf_op jit(solution)/shard_map/ppermute | solution.py:447
  5.8 1.9 %collective-permute-start.1 = (f32[2,4,2,16,128]{4,3,2,1,0:T(8,128)S(1)}, f32[2,4,2,16,128]{4,3,2,1,0:T(8,128)S(1)}, u32[]{:S(2)}, u32[]{:S(2)}) collective-permute-start(f32[2,4,2,16,128]{4,3,2,1,0:T(8,128)S(1)} %get-tuple-element.18), channel_id=1, source_target_pairs={{0,1},{2,3},{4,5},{6,7},{8,9},{10,11},{12,13},{14,15},{16,17},{18,... | collective-permute-start | bytes 393224 | tf_op jit(solution)/shard_map/ppermute | solution.py:448
  7.7 1.8 %collective-permute-done.outer_ref = f32[2,4,2,16,128]{4,3,2,1,0:T(8,128)S(1)} collective-permute-done((f32[2,4,2,16,128]{4,3,2,1,0:T(8,128)S(1)}, f32[2,4,2,16,128]{4,3,2,1,0:T(8,128)S(1)}, u32[]{:S(2)}, u32[]{:S(2)}) %collective-permute-start) | collective-permute-done | bytes 131104 | tf_op jit(solution)/shard_map/ppermute | solution.py:447
  9.6 0.0 collective-permute-done.1.inner_ref
  9.6 0.2 shard_map.30
  9.8 3.8 %collective-permute-start.2 = (f32[30,16,128]{2,1,0:T(8,128)S(1)}, f32[30,16,128]{2,1,0:T(8,128)S(1)}, u32[]{:S(2)}, u32[]{:S(2)}) collective-permute-start(f32[30,16,128]{2,1,0:T(8,128)S(1)} %shard_map.30), channel_id=1, source_target_pairs={{0,32},{32,64},{64,96},{96,128},{128,160},{160,192},{192,224},{224... | collective-permute-start | bytes 737288 | tf_op jit(solution)/shard_map/ppermute | solution.py:450
  13.6 0.2 shard_map.31.coef_ref
  13.8 1.3 %collective-permute-start.3 = (f32[8,128]{1,0:T(8,128)S(1)}, f32[8,128]{1,0:T(8,128)S(1)}, u32[]{:S(2)}, u32[]{:S(2)}) collective-permute-start(f32[8,128]{1,0:T(8,128)S(1)} %shard_map.31.coef_ref), channel_id=1, source_target_pairs={{32,0},{96,64},{160,128},{224,192},{288,256},{352,320},{416,384},{... | collective-permute-start | bytes 12296 | tf_op jit(solution)/shard_map/ppermute | solution.py:462
  15.1 0.5 shard_map.29
  15.7 3.6 %collective-permute-done.3.other_coef_ref = f32[8,128]{1,0:T(8,128)S(1)} collective-permute-done((f32[8,128]{1,0:T(8,128)S(1)}, f32[8,128]{1,0:T(8,128)S(1)}, u32[]{:S(2)}, u32[]{:S(2)}) %collective-permute-start.3) | collective-permute-done | bytes 4128 | tf_op jit(solution)/shard_map/ppermute | solution.py:462
  19.3 0.0 collective-permute-done.2.prev_ref
  19.3 0.5 shard_map.32
  19.9 13.9 %all_to_all.10.all_ref = f32[32,8,128]{2,1,0:T(8,128)S(1)} all-to-all(f32[32,8,128]{2,1,0:T(8,128)S(1)} %get-tuple-element.24), channel_id=1, replica_groups={{20,21,22,23,24,25,26,27,28,29,30,31,0,1,2,3,4,5,6,7,8,9,10,11,12,13,14..., dimensions={0} | all-to-all | bytes 262144 | tf_op jit(solution)/shard_map/all_to_all | solution.py:473
  33.8 18.8 %all_to_all.11.all_ref = f32[8,2,16,128]{3,2,1,0:T(8,128)S(1)} all-to-all(f32[8,2,16,128]{3,2,1,0:T(8,128)S(1)} %shard_map.33), channel_id=1, replica_groups={{224,192,160,128,96,64,32,0},{352,256,288,320,384,416,448,480},{225,193..., dimensions={0} | all-to-all | bytes 262144 | tf_op jit(solution)/shard_map/all_to_all | solution.py:483
  52.6 0.7 %shard_map.34 = (f32[9,8,128]{2,1,0:T(8,128)S(1)}, f32[16,128]{1,0:T(8,128)S(1)}) custom-call(f32[8,2,16,128]{3,2,1,0:T(8,128)S(1)} %all_to_all.11.all_ref), custom_call_target="tpu_custom_call" | custom-call | tf_op jit(solution)/shard_map/pallas_call | solution.py:485
  53.3 3.6 %collective-permute-start.4 = (f32[9,8,128]{2,1,0:T(8,128)S(1)}, f32[9,8,128]{2,1,0:T(8,128)S(1)}, u32[]{:S(2)}, u32[]{:S(2)}) collective-permute-start(f32[9,8,128]{2,1,0:T(8,128)S(1)} %get-tuple-element.25), channel_id=1, source_target_pairs={{128,256},{160,320},{192,288},{224,352},{0,416},{32,448},{64,384},... | collective-permute-start | bytes 110600 | tf_op jit(solution)/shard_map/ppermute | solution.py:489
  56.9 0.9 %shard_map.35._ = f32[4,8,16,128]{3,2,1,0:T(8,128)} custom-call(f32[4,8,16,128]{3,2,1,0:T(8,128)S(1)} %get-tuple-element.23.lp_ref, f32[16,128]{1,0:T(8,128)S(1)} %get-tuple-element.26.mine_ref), custom_call_target="tpu_custom_call" | custom-call | tf_op jit(solution)/shard_map/pallas_call | solution.py:491
  57.8 1.2 %collective-permute-done.4.bound_ref = f32[9,8,128]{2,1,0:T(8,128)S(1)} collective-permute-done((f32[9,8,128]{2,1,0:T(8,128)S(1)}, f32[9,8,128]{2,1,0:T(8,128)S(1)}, u32[]{:S(2)}, u32[]{:S(2)}) %collective-permute-start.4) | collective-permute-done | bytes 36896 | tf_op jit(solution)/shard_map/ppermute | solution.py:489
  58.9 0.1 shard_map.36
  (1 shorter events, 0.0 us)
Async XLA Ops:
  1.2 8.4 %collective-permute-start = (f32[2,4,2,16,128]{4,3,2,1,0:T(8,128)S(1)}, f32[2,4,2,16,128]{4,3,2,1,0:T(8,128)S(1)}, u32[]{:S(2)}, u32[]{:S(2)}) collective-permute-start(f32[2,4,2,16,128]{4,3,2,1,0:T(8,128)S(1)} %get-tuple-element.17), channel_id=1, source_target_pairs={{1,2},{3,4},{5,6},{7,8},{9,10},{11,12},{13,14},{15,16},{17,18},{19... | collective-permute-start | bytes 393224 | tf_op jit(solution)/shard_map/ppermute | solution.py:447
  5.8 3.8 %collective-permute-start.1 = (f32[2,4,2,16,128]{4,3,2,1,0:T(8,128)S(1)}, f32[2,4,2,16,128]{4,3,2,1,0:T(8,128)S(1)}, u32[]{:S(2)}, u32[]{:S(2)}) collective-permute-start(f32[2,4,2,16,128]{4,3,2,1,0:T(8,128)S(1)} %get-tuple-element.18), channel_id=1, source_target_pairs={{0,1},{2,3},{4,5},{6,7},{8,9},{10,11},{12,13},{14,15},{16,17},{18,... | collective-permute-start | bytes 393224 | tf_op jit(solution)/shard_map/ppermute | solution.py:448
  9.8 9.5 %collective-permute-start.2 = (f32[30,16,128]{2,1,0:T(8,128)S(1)}, f32[30,16,128]{2,1,0:T(8,128)S(1)}, u32[]{:S(2)}, u32[]{:S(2)}) collective-permute-start(f32[30,16,128]{2,1,0:T(8,128)S(1)} %shard_map.30), channel_id=1, source_target_pairs={{0,32},{32,64},{64,96},{96,128},{128,160},{160,192},{192,224},{224... | collective-permute-start | bytes 737288 | tf_op jit(solution)/shard_map/ppermute | solution.py:450
  13.8 5.5 %collective-permute-start.3 = (f32[8,128]{1,0:T(8,128)S(1)}, f32[8,128]{1,0:T(8,128)S(1)}, u32[]{:S(2)}, u32[]{:S(2)}) collective-permute-start(f32[8,128]{1,0:T(8,128)S(1)} %shard_map.31.coef_ref), channel_id=1, source_target_pairs={{32,0},{96,64},{160,128},{224,192},{288,256},{352,320},{416,384},{... | collective-permute-start | bytes 12296 | tf_op jit(solution)/shard_map/ppermute | solution.py:462
  53.3 5.6 %collective-permute-start.4 = (f32[9,8,128]{2,1,0:T(8,128)S(1)}, f32[9,8,128]{2,1,0:T(8,128)S(1)}, u32[]{:S(2)}, u32[]{:S(2)}) collective-permute-start(f32[9,8,128]{2,1,0:T(8,128)S(1)} %get-tuple-element.25), channel_id=1, source_target_pairs={{128,256},{160,320},{192,288},{224,352},{0,416},{32,448},{64,384},... | collective-permute-start | bytes 110600 | tf_op jit(solution)/shard_map/ppermute | solution.py:489

commit v7 on v6

--- a/solution.py
+++ b/solution.py
@@ -16,8 +16,8 @@
 NEAR = 4
 WINDOW = 16
 TURN = 20
-EARLY = (7, 6, 5, 4, 3, 2, 1, 0)
-LATE = (3, 0, 1, 2, 4, 5, 6, 7)
+EARLY = (5, 0, 1, 2, 3, 4, 6, 7)
+LATE = (3, 7, 6, 5, 4, 2, 1, 0)
 
 rate = 8.0
 react = 0.5
@@ -99,25 +99,70 @@
     return read
 
 
-def later_kernel(own_ref, outer_ref, inner_ref, out_ref):
-    off2 = CZ
-    off1 = off2 + CZ + 2
+def inner_kernel(own_ref, out_ref):
+    a, b = CT - 2, CT - 1
+
+    def scale(t, z):
+        return own_ref[0, t, z]
+
+    def first(t, z):
+        return own_ref[1, t, z]
+
+    for z in range(CZ):
+        out_ref[z] = first(b, z)
+    for z in range(1, CZ - 1):
+        v = first(b, z)
+        near = (first(b, z - 1), first(b, z + 1))
+        out_ref[CZ + z - 1] = swept(v, v, scale(b, z), near, first(a, z))
+    for z in range(2, CZ - 2):
+        v = first(a, z)
+        second = swept(v, v, scale(a, z), (first(a, z - 1), first(a, z + 1)), None)
+        near = (out_ref[CZ + z - 2], out_ref[CZ + z])
+        out_ref[2 * CZ + z - 4] = swept(
+            out_ref[CZ + z - 1], first(b, z), scale(b, z), near, second
+        )
+
+
+FIRST_ENDS = (-2, -1, CZ, CZ + 1)
+SECOND_ENDS = (-1, 0, CZ - 1, CZ)
+THIRD_ENDS = (0, 1, CZ - 2, CZ - 1)
+
+
+def earlier_step(inside_ref, ends_ref):
+    def first(z):
+        return ends_ref[FIRST_ENDS.index(z)] if z in FIRST_ENDS else inside_ref[z]
+
+    def second(z):
+        if z in SECOND_ENDS:
+            return ends_ref[4 + SECOND_ENDS.index(z)]
+        return inside_ref[CZ + z - 1]
+
+    def third(z):
+        if z in THIRD_ENDS:
+            return ends_ref[8 + THIRD_ENDS.index(z)]
+        return inside_ref[2 * CZ + z - 4]
+
+    return first, second, third
+
+
+def later_kernel(own_ref, outer_ref, inner_ref, inside_ref, out_ref):
     a, b = CT - 2, CT - 1
 
     def body(low_ref, high_ref):
         scale = reader(0, own_ref, low_ref, high_ref)
         first = reader(1, own_ref, low_ref, high_ref)
-        for z in range(-2, CZ + 2):
-            out_ref[off1 + z + 2] = first(b, z)
-        for z in range(-1, CZ + 1):
+        _, second, _ = earlier_step(inside_ref, out_ref)
+        for k, z in enumerate(FIRST_ENDS):
+            out_ref[k] = first(b, z)
+        for k, z in enumerate(SECOND_ENDS):
             v = first(b, z)
             near = (first(b, z - 1), first(b, z + 1))
-            out_ref[off2 + z + 1] = swept(v, v, scale(b, z), near, first(a, z))
-        for z in range(CZ):
+            out_ref[4 + k] = swept(v, v, scale(b, z), near, first(a, z))
+        for k, z in enumerate(THIRD_ENDS):
             v = first(a, z)
-            second = swept(v, v, scale(a, z), (first(a, z - 1), first(a, z + 1)), None)
-            near = (out_ref[off2 + z], out_ref[off2 + z + 2])
-            out_ref[z] = swept(out_ref[off2 + z + 1], first(b, z), scale(b, z), near, second)
+            before = swept(v, v, scale(a, z), (first(a, z - 1), first(a, z + 1)), None)
+            near = (second(z - 1), second(z + 1))
+            out_ref[8 + k] = swept(second(z), first(b, z), scale(b, z), near, before)
 
     by_parity(body, outer_ref, inner_ref)
 
@@ -204,7 +249,8 @@
     v3_ref,
     v4_ref,
     rest_ref,
-    prev_ref,
+    inside_ref,
+    ends_ref,
     coef_ref,
     other_coef_ref,
     lp_ref,
@@ -213,17 +259,16 @@
     v3,
     stack,
 ):
-    off2 = CZ
-    off1 = off2 + CZ + 2
+    first_before, second_before, third_before = earlier_step(inside_ref, ends_ref)
 
     def body(low_ref, high_ref):
         scale = reader(0, own_ref, low_ref, high_ref)
         own = reader(1, own_ref, low_ref, high_ref)
         for z in range(-2, CZ + 2):
-            v2[z + 2] = v2_ref[0, z + 2] + rate * scale(0, z) * prev_ref[off1 + z + 2]
+            v2[z + 2] = v2_ref[0, z + 2] + rate * scale(0, z) * first_before(z)
         for z in range(-1, CZ + 1):
             near = (v2[z + 1], v2[z + 3])
-            before = prev_ref[off2 + z + 1]
+            before = second_before(z)
             v3[0, z + 1] = swept(v2[z + 2], own(0, z), scale(0, z), near, before)
             v3[1, z + 1] = v3_ref[0, z + 1] + rate * scale(1, z) * v2[z + 2]
 
@@ -237,7 +282,7 @@
         for t in range(CT - 1):
             scale = own_ref[0, t, z]
             if t < 2:
-                before = prev_ref[z] if t == 0 else v3[0, z + 1]
+                before = third_before(z) if t == 0 else v3[0, z + 1]
                 near = (v3[t, z], v3[t, z + 2])
                 value = swept(v3[t, z + 1], own_ref[1, t, z], scale, near, before)
             else:
@@ -446,8 +491,10 @@
     )
     outer = lax.ppermute(outer, "space", across)
     inner = lax.ppermute(inner, "space", within)
-    sent = call(later_kernel, arr(3 * CZ + 6, CX, CY), 3)(own, outer, inner)
-    prev = lax.ppermute(sent, "tm", onward)
+    inside = call(inner_kernel, arr(3 * CZ - 6, CX, CY), 1)(own)
+    passed = lax.ppermute(inside, "tm", onward)
+    sent = call(later_kernel, arr(12, CX, CY), 4)(own, outer, inner, inside)
+    ends = lax.ppermute(sent, "tm", onward)
     v2, v3, v4, rest = call(
         early_kernel,
         [
@@ -463,13 +510,13 @@
     lp, sums = call(
         main_kernel,
         [arr(CT, CZ, CX, CY), arr(planes, 8, LANES)],
-        10,
+        11,
         [
             pltpu.VMEM((CZ + 4, CX, CY), F32),
             pltpu.VMEM((2, CZ + 2, CX, CY), F32),
             pltpu.VMEM((6, CX, CY), F32),
         ],
-    )(own, outer, inner, v2, v3, v4, rest, prev, coef, other_coef)
+    )(own, outer, inner, v2, v3, v4, rest, passed, ends, coef, other_coef)
     column = lax.all_to_all(
         sums, "space", 0, 0, axis_index_groups=[[(p + TURN) % planes for p in range(planes)]]
     )
@@ -484,7 +531,7 @@
     found = pltpu.VMEM((half // 2, WINDOW, LANES), F32)
     last, mine = call(bound_kernel, [arr(9, WINDOW // 2, LANES), arr(WINDOW, LANES)], 1, [found])(every)
     quarter = half // 2
-    order = (0, 2, 1, 3, 5, 6, 4, 7) if half == 8 else tuple(range(half))
+    order = (0, 2, 1, 3, 4, 5, 6, 7) if half == 8 else tuple(range(half))
     serve = [((quarter + k) % half, half + order[k]) for k in range(half)]
     bound = lax.ppermute(last, "tm", serve)
     shape = arr(CT, CZ, CX, CY)

time: 59.5 us -> 59 us (level)
  starting transfers between devices: 15.2 us -> 18.6 us
  waiting for transfers between devices: 6.65 us -> 4.39 us
  blocking collectives: 32.7 us -> 31 us
    ppermute x1 -> x2, starting transfers between devices: 3.84 us -> 7.65 us  [the longest x1 3.83 us: local(): passed = lax.ppermute(inside, 'tm', onward)]
    all_to_all x1, blocking collectives: 13.9 us -> 11.8 us  [local(): lax.all_to_all(sums, 'space', 0, 0, axis_index_groups=[[(p + TURN) % plan...]
    ppermute x1, waiting for transfers between devices: 1.83 us -> 0.01 us  [local(): outer = lax.ppermute(outer, 'space', across)]
  transfers between devices with their start and end apart: 5 -> 6, of which waited for: 3 -> 2; matrix products, arithmetic and copies ran while one was open for 0% -> 0% of each run, Pallas kernels for 3% -> 3%
where the time goes in v7:
time: 59 us; the launch traced here: 58.6 us
  blocking collectives  31 us (53%)
  starting transfers between devices  18.6 us (32%)
  waiting for transfers between devices  4.39 us (7%)
  Pallas kernels  3.4 us (6%)
  other arithmetic  1.06 us (2%)
    all_to_all x1, blocking collectives, local(): every = lax.all_to_all(window, 'tm', 0, 0, axis_index_groups=halves)  19.2 us
    all_to_all x1, blocking collectives, local(): lax.all_to_all(sums, 'space', 0, 0, axis_index_groups=[[(p + TURN) % plan...  11.8 us
    ppermute x1, starting transfers between devices, local(): outer = lax.ppermute(outer, 'space', across)  4.63 us
    ppermute x1, starting transfers between devices, local(): passed = lax.ppermute(inside, 'tm', onward)  3.83 us
    ppermute x1, starting transfers between devices, local(): ends = lax.ppermute(sent, 'tm', onward)  3.82 us
    ppermute x1, waiting for transfers between devices, local(): lax.ppermute(coef, 'tm', [(i, i - 1) for i in range(1, slabs, 2)])  3.64 us
    ppermute x1, starting transfers between devices, local(): bound = lax.ppermute(last, 'tm', serve)  3.15 us
    ppermute x1, starting transfers between devices, local(): inner = lax.ppermute(inner, 'space', within)  1.92 us
  transfers between devices with their start and end apart: 6, of which 2 were waited for; matrix products, arithmetic and copies ran while one was open for 0% of the time, Pallas kernels for 3%

profile of v7, /device:TPU:6, one launch (start us, length us, event | category | flops | bytes accessed | tf_op | source)
XLA Modules:
  0.0 58.6 jit_solution(277576537389836992)
XLA Ops:
  0.0 1.1 %pad_maximum_fusion.loaded_ref = f32[2,4,8,16,128]{4,3,2,1,0:T(8,128)S(1)} fusion(f32[1,4,8,16,128]{4,3,2,1,0:T(8,128)} %bitcast.2, f32[1,4,8,16,128]{4,3,2,1,0:T(8,128)} %bitcast.3), kind=kLoop, calls=%fused_computation | loop fusion | flops 131072 | bytes 1048576 | tf_op jit(solution)/shard_map/stack | solution.py:490
  1.1 0.1 shard_map.28
  1.2 4.6 %collective-permute-start = (f32[2,4,2,16,128]{4,3,2,1,0:T(8,128)S(1)}, f32[2,4,2,16,128]{4,3,2,1,0:T(8,128)S(1)}, u32[]{:S(2)}, u32[]{:S(2)}) collective-permute-start(f32[2,4,2,16,128]{4,3,2,1,0:T(8,128)S(1)} %get-tuple-element.17), channel_id=1, source_target_pairs={{1,2},{3,4},{5,6},{7,8},{9,10},{11,12},{13,14},{15,16},{17,18},{19... | collective-permute-start | bytes 393224 | tf_op jit(solution)/shard_map/ppermute | solution.py:492
  5.8 1.9 %collective-permute-start.1 = (f32[2,4,2,16,128]{4,3,2,1,0:T(8,128)S(1)}, f32[2,4,2,16,128]{4,3,2,1,0:T(8,128)S(1)}, u32[]{:S(2)}, u32[]{:S(2)}) collective-permute-start(f32[2,4,2,16,128]{4,3,2,1,0:T(8,128)S(1)} %get-tuple-element.18), channel_id=1, source_target_pairs={{0,1},{2,3},{4,5},{6,7},{8,9},{10,11},{12,13},{14,15},{16,17},{18,... | collective-permute-start | bytes 393224 | tf_op jit(solution)/shard_map/ppermute | solution.py:493
  7.7 0.2 shard_map.30.inside_ref
  7.9 3.8 %collective-permute-start.2 = (f32[18,16,128]{2,1,0:T(8,128)S(1)}, f32[18,16,128]{2,1,0:T(8,128)S(1)}, u32[]{:S(2)}, u32[]{:S(2)}) collective-permute-start(f32[18,16,128]{2,1,0:T(8,128)S(1)} %shard_map.30.inside_ref), channel_id=1, source_target_pairs={{0,32},{32,64},{64,96},{96,128},{128,160},{160,192},{192,224},{224... | collective-permute-start | bytes 442376 | tf_op jit(solution)/shard_map/ppermute | solution.py:495
  11.8 0.0 collective-permute-done.outer_ref
  11.8 0.0 collective-permute-done.1.inner_ref
  11.8 0.2 shard_map.31
  12.0 3.8 %collective-permute-start.3 = (f32[12,16,128]{2,1,0:T(8,128)S(1)}, f32[12,16,128]{2,1,0:T(8,128)S(1)}, u32[]{:S(2)}, u32[]{:S(2)}) collective-permute-start(f32[12,16,128]{2,1,0:T(8,128)S(1)} %shard_map.31), channel_id=1, source_target_pairs={{0,32},{32,64},{64,96},{96,128},{128,160},{160,192},{192,224},{224... | collective-permute-start | bytes 294920 | tf_op jit(solution)/shard_map/ppermute | solution.py:497
  15.8 0.2 shard_map.32.coef_ref
  16.0 1.3 %collective-permute-start.4 = (f32[8,128]{1,0:T(8,128)S(1)}, f32[8,128]{1,0:T(8,128)S(1)}, u32[]{:S(2)}, u32[]{:S(2)}) collective-permute-start(f32[8,128]{1,0:T(8,128)S(1)} %shard_map.32.coef_ref), channel_id=1, source_target_pairs={{32,0},{96,64},{160,128},{224,192},{288,256},{352,320},{416,384},{... | collective-permute-start | bytes 12296 | tf_op jit(solution)/shard_map/ppermute | solution.py:509
  17.3 0.6 shard_map.29
  17.8 3.6 %collective-permute-done.4.other_coef_ref = f32[8,128]{1,0:T(8,128)S(1)} collective-permute-done((f32[8,128]{1,0:T(8,128)S(1)}, f32[8,128]{1,0:T(8,128)S(1)}, u32[]{:S(2)}, u32[]{:S(2)}) %collective-permute-start.4) | collective-permute-done | bytes 4128 | tf_op jit(solution)/shard_map/ppermute | solution.py:509
  21.5 0.0 collective-permute-done.2.inside_ref
  21.5 0.0 collective-permute-done.3.ends_ref
  21.5 0.5 shard_map.33
  22.0 11.8 %all_to_all.10.all_ref = f32[32,8,128]{2,1,0:T(8,128)S(1)} all-to-all(f32[32,8,128]{2,1,0:T(8,128)S(1)} %get-tuple-element.24), channel_id=1, replica_groups={{20,21,22,23,24,25,26,27,28,29,30,31,0,1,2,3,4,5,6,7,8,9,10,11,12,13,14..., dimensions={0} | all-to-all | bytes 262144 | tf_op jit(solution)/shard_map/all_to_all | solution.py:520
  33.8 19.2 %all_to_all.11.all_ref = f32[8,2,16,128]{3,2,1,0:T(8,128)S(1)} all-to-all(f32[8,2,16,128]{3,2,1,0:T(8,128)S(1)} %shard_map.34), channel_id=1, replica_groups={{160,0,32,64,96,128,192,224},{352,480,448,416,384,320,288,256},{161,1,3..., dimensions={0} | all-to-all | bytes 262144 | tf_op jit(solution)/shard_map/all_to_all | solution.py:530
  53.0 0.7 %shard_map.35 = (f32[9,8,128]{2,1,0:T(8,128)S(1)}, f32[16,128]{1,0:T(8,128)S(1)}) custom-call(f32[8,2,16,128]{3,2,1,0:T(8,128)S(1)} %all_to_all.11.all_ref), custom_call_target="tpu_custom_call" | custom-call | tf_op jit(solution)/shard_map/pallas_call | solution.py:532
  53.7 3.2 %collective-permute-start.5 = (f32[9,8,128]{2,1,0:T(8,128)S(1)}, f32[9,8,128]{2,1,0:T(8,128)S(1)}, u32[]{:S(2)}, u32[]{:S(2)}) collective-permute-start(f32[9,8,128]{2,1,0:T(8,128)S(1)} %get-tuple-element.25), channel_id=1, source_target_pairs={{128,256},{160,320},{192,288},{224,352},{0,384},{32,416},{64,448},... | collective-permute-start | bytes 110600 | tf_op jit(solution)/shard_map/ppermute | solution.py:536
  56.9 0.9 %shard_map.36._ = f32[4,8,16,128]{3,2,1,0:T(8,128)} custom-call(f32[4,8,16,128]{3,2,1,0:T(8,128)S(1)} %get-tuple-element.23.lp_ref, f32[16,128]{1,0:T(8,128)S(1)} %get-tuple-element.26.mine_ref), custom_call_target="tpu_custom_call" | custom-call | tf_op jit(solution)/shard_map/pallas_call | solution.py:538
  57.8 0.7 %collective-permute-done.5.bound_ref = f32[9,8,128]{2,1,0:T(8,128)S(1)} collective-permute-done((f32[9,8,128]{2,1,0:T(8,128)S(1)}, f32[9,8,128]{2,1,0:T(8,128)S(1)}, u32[]{:S(2)}, u32[]{:S(2)}) %collective-permute-start.5) | collective-permute-done | bytes 36896 | tf_op jit(solution)/shard_map/ppermute | solution.py:536
  58.5 0.1 shard_map.37
  (1 shorter events, 0.0 us)
Async XLA Ops:
  1.2 10.6 %collective-permute-start = (f32[2,4,2,16,128]{4,3,2,1,0:T(8,128)S(1)}, f32[2,4,2,16,128]{4,3,2,1,0:T(8,128)S(1)}, u32[]{:S(2)}, u32[]{:S(2)}) collective-permute-start(f32[2,4,2,16,128]{4,3,2,1,0:T(8,128)S(1)} %get-tuple-element.17), channel_id=1, source_target_pairs={{1,2},{3,4},{5,6},{7,8},{9,10},{11,12},{13,14},{15,16},{17,18},{19... | collective-permute-start | bytes 393224 | tf_op jit(solution)/shard_map/ppermute | solution.py:492
  5.8 6.0 %collective-permute-start.1 = (f32[2,4,2,16,128]{4,3,2,1,0:T(8,128)S(1)}, f32[2,4,2,16,128]{4,3,2,1,0:T(8,128)S(1)}, u32[]{:S(2)}, u32[]{:S(2)}) collective-permute-start(f32[2,4,2,16,128]{4,3,2,1,0:T(8,128)S(1)} %get-tuple-element.18), channel_id=1, source_target_pairs={{0,1},{2,3},{4,5},{6,7},{8,9},{10,11},{12,13},{14,15},{16,17},{18,... | collective-permute-start | bytes 393224 | tf_op jit(solution)/shard_map/ppermute | solution.py:493
  7.9 13.6 %collective-permute-start.2 = (f32[18,16,128]{2,1,0:T(8,128)S(1)}, f32[18,16,128]{2,1,0:T(8,128)S(1)}, u32[]{:S(2)}, u32[]{:S(2)}) collective-permute-start(f32[18,16,128]{2,1,0:T(8,128)S(1)} %shard_map.30.inside_ref), channel_id=1, source_target_pairs={{0,32},{32,64},{64,96},{96,128},{128,160},{160,192},{192,224},{224... | collective-permute-start | bytes 442376 | tf_op jit(solution)/shard_map/ppermute | solution.py:495
  12.0 9.5 %collective-permute-start.3 = (f32[12,16,128]{2,1,0:T(8,128)S(1)}, f32[12,16,128]{2,1,0:T(8,128)S(1)}, u32[]{:S(2)}, u32[]{:S(2)}) collective-permute-start(f32[12,16,128]{2,1,0:T(8,128)S(1)} %shard_map.31), channel_id=1, source_target_pairs={{0,32},{32,64},{64,96},{96,128},{128,160},{160,192},{192,224},{224... | collective-permute-start | bytes 294920 | tf_op jit(solution)/shard_map/ppermute | solution.py:497
  16.0 5.5 %collective-permute-start.4 = (f32[8,128]{1,0:T(8,128)S(1)}, f32[8,128]{1,0:T(8,128)S(1)}, u32[]{:S(2)}, u32[]{:S(2)}) collective-permute-start(f32[8,128]{1,0:T(8,128)S(1)} %shard_map.32.coef_ref), channel_id=1, source_target_pairs={{32,0},{96,64},{160,128},{224,192},{288,256},{352,320},{416,384},{... | collective-permute-start | bytes 12296 | tf_op jit(solution)/shard_map/ppermute | solution.py:509
  53.7 4.8 %collective-permute-start.5 = (f32[9,8,128]{2,1,0:T(8,128)S(1)}, f32[9,8,128]{2,1,0:T(8,128)S(1)}, u32[]{:S(2)}, u32[]{:S(2)}) collective-permute-start(f32[9,8,128]{2,1,0:T(8,128)S(1)} %get-tuple-element.25), channel_id=1, source_target_pairs={{128,256},{160,320},{192,288},{224,352},{0,384},{32,416},{64,448},... | collective-permute-start | bytes 110600 | tf_op jit(solution)/shard_map/ppermute | solution.py:536

commit v8 on v7

--- a/solution.py
+++ b/solution.py
@@ -15,9 +15,9 @@
 LANES = 128
 NEAR = 4
 WINDOW = 16
-TURN = 20
-EARLY = (5, 0, 1, 2, 3, 4, 6, 7)
-LATE = (3, 7, 6, 5, 4, 2, 1, 0)
+TURN = 4
+EARLY = (5, 7, 6, 4, 3, 2, 1, 0)
+LATE = (2, 7, 6, 5, 4, 3, 1, 0)
 
 rate = 8.0
 react = 0.5
@@ -531,7 +531,7 @@
     found = pltpu.VMEM((half // 2, WINDOW, LANES), F32)
     last, mine = call(bound_kernel, [arr(9, WINDOW // 2, LANES), arr(WINDOW, LANES)], 1, [found])(every)
     quarter = half // 2
-    order = (0, 2, 1, 3, 4, 5, 6, 7) if half == 8 else tuple(range(half))
+    order = (0, 2, 1, 3, 6, 5, 4, 7) if half == 8 else tuple(range(half))
     serve = [((quarter + k) % half, half + order[k]) for k in range(half)]
     bound = lax.ppermute(last, "tm", serve)
     shape = arr(CT, CZ, CX, CY)

time: 59 us -> 58.6 us (level)
  the two profiles are of different devices: /device:TPU:6 before, /device:TPU:256 now
where the time goes in v8:
time: 58.6 us; the launch traced here: 58.3 us
  blocking collectives  24.6 us (42%)
  starting transfers between devices  16.9 us (29%)
  waiting for transfers between devices  11.2 us (19%)
  Pallas kernels  4.32 us (7%)
  other arithmetic  1.06 us (2%)
    all_to_all x1, blocking collectives, local(): every = lax.all_to_all(window, 'tm', 0, 0, axis_index_groups=halves)  14.1 us
    all_to_all x1, blocking collectives, local(): lax.all_to_all(sums, 'space', 0, 0, axis_index_groups=[[(p + TURN) % plan...  10.5 us
    ppermute x1, waiting for transfers between devices, local(): bound = lax.ppermute(last, 'tm', serve)  7.58 us
    ppermute x1, starting transfers between devices, local(): outer = lax.ppermute(outer, 'space', across)  6.56 us
    ppermute x1, waiting for transfers between devices, local(): lax.ppermute(coef, 'tm', [(i, i - 1) for i in range(1, slabs, 2)])  3.64 us
    ppermute x1, starting transfers between devices, local(): passed = lax.ppermute(inside, 'tm', onward)  2.93 us
    ppermute x1, starting transfers between devices, local(): ends = lax.ppermute(sent, 'tm', onward)  2.93 us
    ppermute x1, starting transfers between devices, local(): inner = lax.ppermute(inner, 'space', within)  1.92 us
  transfers between devices with their start and end apart: 6, of which 2 were waited for; matrix products, arithmetic and copies ran while one was open for 0% of the time, Pallas kernels for 3%

profile of v8, /device:TPU:256, one launch (start us, length us, event | category | flops | bytes accessed | tf_op | source)
XLA Modules:
  0.0 58.3 jit_solution(3829896819556235404)
XLA Ops:
  0.0 1.1 %pad_maximum_fusion.loaded_ref = f32[2,4,8,16,128]{4,3,2,1,0:T(8,128)S(1)} fusion(f32[1,4,8,16,128]{4,3,2,1,0:T(8,128)} %bitcast.2, f32[1,4,8,16,128]{4,3,2,1,0:T(8,128)} %bitcast.3), kind=kLoop, calls=%fused_computation | loop fusion | flops 131072 | bytes 1048576 | tf_op jit(solution)/shard_map/stack | solution.py:490
  1.1 0.1 shard_map.28
  1.2 6.6 %collective-permute-start = (f32[2,4,2,16,128]{4,3,2,1,0:T(8,128)S(1)}, f32[2,4,2,16,128]{4,3,2,1,0:T(8,128)S(1)}, u32[]{:S(2)}, u32[]{:S(2)}) collective-permute-start(f32[2,4,2,16,128]{4,3,2,1,0:T(8,128)S(1)} %get-tuple-element.17), channel_id=1, source_target_pairs={{1,2},{3,4},{5,6},{7,8},{9,10},{11,12},{13,14},{15,16},{17,18},{19... | collective-permute-start | bytes 393224 | tf_op jit(solution)/shard_map/ppermute | solution.py:492
  7.7 1.9 %collective-permute-start.1 = (f32[2,4,2,16,128]{4,3,2,1,0:T(8,128)S(1)}, f32[2,4,2,16,128]{4,3,2,1,0:T(8,128)S(1)}, u32[]{:S(2)}, u32[]{:S(2)}) collective-permute-start(f32[2,4,2,16,128]{4,3,2,1,0:T(8,128)S(1)} %get-tuple-element.18), channel_id=1, source_target_pairs={{0,1},{2,3},{4,5},{6,7},{8,9},{10,11},{12,13},{14,15},{16,17},{18,... | collective-permute-start | bytes 393224 | tf_op jit(solution)/shard_map/ppermute | solution.py:493
  9.7 0.2 shard_map.30.inside_ref
  9.8 2.9 %collective-permute-start.2 = (f32[18,16,128]{2,1,0:T(8,128)S(1)}, f32[18,16,128]{2,1,0:T(8,128)S(1)}, u32[]{:S(2)}, u32[]{:S(2)}) collective-permute-start(f32[18,16,128]{2,1,0:T(8,128)S(1)} %shard_map.30.inside_ref), channel_id=1, source_target_pairs={{0,32},{32,64},{64,96},{96,128},{128,160},{160,192},{192,224},{224... | collective-permute-start | bytes 442376 | tf_op jit(solution)/shard_map/ppermute | solution.py:495
  12.8 0.0 collective-permute-done.outer_ref
  12.8 0.0 collective-permute-done.1.inner_ref
  12.8 0.2 shard_map.31
  13.0 2.9 %collective-permute-start.3 = (f32[12,16,128]{2,1,0:T(8,128)S(1)}, f32[12,16,128]{2,1,0:T(8,128)S(1)}, u32[]{:S(2)}, u32[]{:S(2)}) collective-permute-start(f32[12,16,128]{2,1,0:T(8,128)S(1)} %shard_map.31), channel_id=1, source_target_pairs={{0,32},{32,64},{64,96},{96,128},{128,160},{160,192},{192,224},{224... | collective-permute-start | bytes 294920 | tf_op jit(solution)/shard_map/ppermute | solution.py:497
  15.9 0.2 shard_map.32.coef_ref
  16.1 1.3 %collective-permute-start.4 = (f32[8,128]{1,0:T(8,128)S(1)}, f32[8,128]{1,0:T(8,128)S(1)}, u32[]{:S(2)}, u32[]{:S(2)}) collective-permute-start(f32[8,128]{1,0:T(8,128)S(1)} %shard_map.32.coef_ref), channel_id=1, source_target_pairs={{32,0},{96,64},{160,128},{224,192},{288,256},{352,320},{416,384},{... | collective-permute-start | bytes 12296 | tf_op jit(solution)/shard_map/ppermute | solution.py:509
  17.4 0.6 shard_map.29
  18.0 3.6 %collective-permute-done.4.other_coef_ref = f32[8,128]{1,0:T(8,128)S(1)} collective-permute-done((f32[8,128]{1,0:T(8,128)S(1)}, f32[8,128]{1,0:T(8,128)S(1)}, u32[]{:S(2)}, u32[]{:S(2)}) %collective-permute-start.4) | collective-permute-done | bytes 4128 | tf_op jit(solution)/shard_map/ppermute | solution.py:509
  21.6 0.0 collective-permute-done.2.inside_ref
  21.6 0.0 collective-permute-done.3.ends_ref
  21.6 0.5 shard_map.33
  22.2 10.5 %all_to_all.10.all_ref = f32[32,8,128]{2,1,0:T(8,128)S(1)} all-to-all(f32[32,8,128]{2,1,0:T(8,128)S(1)} %get-tuple-element.24), channel_id=1, replica_groups={{4,5,6,7,8,9,10,11,12,13,14,15,16,17,18,19,20,21,22,23,24,25,26,27,28,2..., dimensions={0} | all-to-all | bytes 262144 | tf_op jit(solution)/shard_map/all_to_all | solution.py:520
  32.7 14.1 %all_to_all.11.all_ref = f32[8,2,16,128]{3,2,1,0:T(8,128)S(1)} all-to-all(f32[8,2,16,128]{3,2,1,0:T(8,128)S(1)} %shard_map.34), channel_id=1, replica_groups={{160,224,192,128,96,64,32,0},{320,480,448,416,384,352,288,256},{161,225..., dimensions={0} | all-to-all | bytes 262144 | tf_op jit(solution)/shard_map/all_to_all | solution.py:530
  46.8 1.3 %collective-permute-start.5 = (f32[9,8,128]{2,1,0:T(8,128)S(1)}, f32[9,8,128]{2,1,0:T(8,128)S(1)}, u32[]{:S(2)}, u32[]{:S(2)}) collective-permute-start(f32[9,8,128]{2,1,0:T(8,128)S(1)} %get-tuple-element.25), channel_id=1, source_target_pairs={{128,256},{160,320},{192,288},{224,352},{0,448},{32,416},{64,384},... | collective-permute-start | bytes 110600 | tf_op jit(solution)/shard_map/ppermute | solution.py:536
  48.1 0.9 %shard_map.36._ = f32[4,8,16,128]{3,2,1,0:T(8,128)} custom-call(f32[4,8,16,128]{3,2,1,0:T(8,128)S(1)} %get-tuple-element.23.lp_ref, f32[16,128]{1,0:T(8,128)S(1)} %get-tuple-element.26.mine_ref), custom_call_target="tpu_custom_call" | custom-call | tf_op jit(solution)/shard_map/pallas_call | solution.py:538
  49.0 7.6 %collective-permute-done.5.bound_ref = f32[9,8,128]{2,1,0:T(8,128)S(1)} collective-permute-done((f32[9,8,128]{2,1,0:T(8,128)S(1)}, f32[9,8,128]{2,1,0:T(8,128)S(1)}, u32[]{:S(2)}, u32[]{:S(2)}) %collective-permute-start.5) | collective-permute-done | bytes 36896 | tf_op jit(solution)/shard_map/ppermute | solution.py:536
  56.6 1.7 %shard_map.37 = f32[4,8,16,128]{3,2,1,0:T(8,128)} custom-call(f32[4,8,16,128]{3,2,1,0:T(8,128)S(1)} %get-tuple-element.23.lp_ref, f32[8,2,16,128]{3,2,1,0:T(8,128)S(1)} %all_to_all.11.all_ref, f32[9,8,128]{2,1,0:T(8,128)S(1)} %collective-permute-done.5.bound_ref, f32[4,8,16,128]{3,2,1,0:T(8,128)} %shard_map.36._), custom_call_target="tpu_custom_call", output_to_operand_aliasing={{}: (3, {})} | custom-call | tf_op jit(solution)/shard_map/pallas_call | solution.py:540
  (2 shorter events, 0.0 us)
Async XLA Ops:
  1.2 11.6 %collective-permute-start = (f32[2,4,2,16,128]{4,3,2,1,0:T(8,128)S(1)}, f32[2,4,2,16,128]{4,3,2,1,0:T(8,128)S(1)}, u32[]{:S(2)}, u32[]{:S(2)}) collective-permute-start(f32[2,4,2,16,128]{4,3,2,1,0:T(8,128)S(1)} %get-tuple-element.17), channel_id=1, source_target_pairs={{1,2},{3,4},{5,6},{7,8},{9,10},{11,12},{13,14},{15,16},{17,18},{19... | collective-permute-start | bytes 393224 | tf_op jit(solution)/shard_map/ppermute | solution.py:492
  7.7 5.1 %collective-permute-start.1 = (f32[2,4,2,16,128]{4,3,2,1,0:T(8,128)S(1)}, f32[2,4,2,16,128]{4,3,2,1,0:T(8,128)S(1)}, u32[]{:S(2)}, u32[]{:S(2)}) collective-permute-start(f32[2,4,2,16,128]{4,3,2,1,0:T(8,128)S(1)} %get-tuple-element.18), channel_id=1, source_target_pairs={{0,1},{2,3},{4,5},{6,7},{8,9},{10,11},{12,13},{14,15},{16,17},{18,... | collective-permute-start | bytes 393224 | tf_op jit(solution)/shard_map/ppermute | solution.py:493
  9.8 11.8 %collective-permute-start.2 = (f32[18,16,128]{2,1,0:T(8,128)S(1)}, f32[18,16,128]{2,1,0:T(8,128)S(1)}, u32[]{:S(2)}, u32[]{:S(2)}) collective-permute-start(f32[18,16,128]{2,1,0:T(8,128)S(1)} %shard_map.30.inside_ref), channel_id=1, source_target_pairs={{0,32},{32,64},{64,96},{96,128},{128,160},{160,192},{192,224},{224... | collective-permute-start | bytes 442376 | tf_op jit(solution)/shard_map/ppermute | solution.py:495
  13.0 8.6 %collective-permute-start.3 = (f32[12,16,128]{2,1,0:T(8,128)S(1)}, f32[12,16,128]{2,1,0:T(8,128)S(1)}, u32[]{:S(2)}, u32[]{:S(2)}) collective-permute-start(f32[12,16,128]{2,1,0:T(8,128)S(1)} %shard_map.31), channel_id=1, source_target_pairs={{0,32},{32,64},{64,96},{96,128},{128,160},{160,192},{192,224},{224... | collective-permute-start | bytes 294920 | tf_op jit(solution)/shard_map/ppermute | solution.py:497
  16.1 5.5 %collective-permute-start.4 = (f32[8,128]{1,0:T(8,128)S(1)}, f32[8,128]{1,0:T(8,128)S(1)}, u32[]{:S(2)}, u32[]{:S(2)}) collective-permute-start(f32[8,128]{1,0:T(8,128)S(1)} %shard_map.32.coef_ref), channel_id=1, source_target_pairs={{32,0},{96,64},{160,128},{224,192},{288,256},{352,320},{416,384},{... | collective-permute-start | bytes 12296 | tf_op jit(solution)/shard_map/ppermute | solution.py:509
  46.8 9.7 %collective-permute-start.5 = (f32[9,8,128]{2,1,0:T(8,128)S(1)}, f32[9,8,128]{2,1,0:T(8,128)S(1)}, u32[]{:S(2)}, u32[]{:S(2)}) collective-permute-start(f32[9,8,128]{2,1,0:T(8,128)S(1)} %get-tuple-element.25), channel_id=1, source_target_pairs={{128,256},{160,320},{192,288},{224,352},{0,448},{32,416},{64,384},... | collective-permute-start | bytes 110600 | tf_op jit(solution)/shard_map/ppermute | solution.py:536

commit v9 on v8

--- a/solution.py
+++ b/solution.py
@@ -15,7 +15,7 @@
 LANES = 128
 NEAR = 4
 WINDOW = 16
-TURN = 4
+TURN = 5
 EARLY = (5, 7, 6, 4, 3, 2, 1, 0)
 LATE = (2, 7, 6, 5, 4, 3, 1, 0)
 

time: 58.6 us -> 58.3 us (level)
  no operation moved by 1% of the time
where the time goes in v9:
time: 58.3 us; the launch traced here: 58 us
  blocking collectives  24.4 us (42%)
  starting transfers between devices  16.9 us (29%)
  waiting for transfers between devices  11.2 us (19%)
  Pallas kernels  4.32 us (7%)
  other arithmetic  1.06 us (2%)
    all_to_all x1, blocking collectives, local(): every = lax.all_to_all(window, 'tm', 0, 0, axis_index_groups=halves)  14.1 us
    all_to_all x1, blocking collectives, local(): lax.all_to_all(sums, 'space', 0, 0, axis_index_groups=[[(p + TURN) % plan...  10.2 us
    ppermute x1, waiting for transfers between devices, local(): bound = lax.ppermute(last, 'tm', serve)  7.58 us
    ppermute x1, starting transfers between devices, local(): outer = lax.ppermute(outer, 'space', across)  6.56 us
    ppermute x1, waiting for transfers between devices, local(): lax.ppermute(coef, 'tm', [(i, i - 1) for i in range(1, slabs, 2)])  3.64 us
    ppermute x1, starting transfers between devices, local(): passed = lax.ppermute(inside, 'tm', onward)  2.93 us
    ppermute x1, starting transfers between devices, local(): ends = lax.ppermute(sent, 'tm', onward)  2.93 us
    ppermute x1, starting transfers between devices, local(): inner = lax.ppermute(inner, 'space', within)  1.92 us
  transfers between devices with their start and end apart: 6, of which 2 were waited for; matrix products, arithmetic and copies ran while one was open for 0% of the time, Pallas kernels for 3%

profile of v9, /device:TPU:256, one launch (start us, length us, event | category | flops | bytes accessed | tf_op | source)
XLA Modules:
  0.0 58.0 jit_solution(3900841767645259311)
XLA Ops:
  0.0 1.1 %pad_maximum_fusion.loaded_ref = f32[2,4,8,16,128]{4,3,2,1,0:T(8,128)S(1)} fusion(f32[1,4,8,16,128]{4,3,2,1,0:T(8,128)} %bitcast.2, f32[1,4,8,16,128]{4,3,2,1,0:T(8,128)} %bitcast.3), kind=kLoop, calls=%fused_computation | loop fusion | flops 131072 | bytes 1048576 | tf_op jit(solution)/shard_map/stack | solution.py:490
  1.1 0.1 shard_map.28
  1.2 6.6 %collective-permute-start = (f32[2,4,2,16,128]{4,3,2,1,0:T(8,128)S(1)}, f32[2,4,2,16,128]{4,3,2,1,0:T(8,128)S(1)}, u32[]{:S(2)}, u32[]{:S(2)}) collective-permute-start(f32[2,4,2,16,128]{4,3,2,1,0:T(8,128)S(1)} %get-tuple-element.17), channel_id=1, source_target_pairs={{1,2},{3,4},{5,6},{7,8},{9,10},{11,12},{13,14},{15,16},{17,18},{19... | collective-permute-start | bytes 393224 | tf_op jit(solution)/shard_map/ppermute | solution.py:492
  7.7 1.9 %collective-permute-start.1 = (f32[2,4,2,16,128]{4,3,2,1,0:T(8,128)S(1)}, f32[2,4,2,16,128]{4,3,2,1,0:T(8,128)S(1)}, u32[]{:S(2)}, u32[]{:S(2)}) collective-permute-start(f32[2,4,2,16,128]{4,3,2,1,0:T(8,128)S(1)} %get-tuple-element.18), channel_id=1, source_target_pairs={{0,1},{2,3},{4,5},{6,7},{8,9},{10,11},{12,13},{14,15},{16,17},{18,... | collective-permute-start | bytes 393224 | tf_op jit(solution)/shard_map/ppermute | solution.py:493
  9.7 0.2 shard_map.30.inside_ref
  9.8 2.9 %collective-permute-start.2 = (f32[18,16,128]{2,1,0:T(8,128)S(1)}, f32[18,16,128]{2,1,0:T(8,128)S(1)}, u32[]{:S(2)}, u32[]{:S(2)}) collective-permute-start(f32[18,16,128]{2,1,0:T(8,128)S(1)} %shard_map.30.inside_ref), channel_id=1, source_target_pairs={{0,32},{32,64},{64,96},{96,128},{128,160},{160,192},{192,224},{224... | collective-permute-start | bytes 442376 | tf_op jit(solution)/shard_map/ppermute | solution.py:495
  12.8 0.0 collective-permute-done.outer_ref
  12.8 0.0 collective-permute-done.1.inner_ref
  12.8 0.2 shard_map.31
  13.0 2.9 %collective-permute-start.3 = (f32[12,16,128]{2,1,0:T(8,128)S(1)}, f32[12,16,128]{2,1,0:T(8,128)S(1)}, u32[]{:S(2)}, u32[]{:S(2)}) collective-permute-start(f32[12,16,128]{2,1,0:T(8,128)S(1)} %shard_map.31), channel_id=1, source_target_pairs={{0,32},{32,64},{64,96},{96,128},{128,160},{160,192},{192,224},{224... | collective-permute-start | bytes 294920 | tf_op jit(solution)/shard_map/ppermute | solution.py:497
  15.9 0.2 shard_map.32.coef_ref
  16.1 1.3 %collective-permute-start.4 = (f32[8,128]{1,0:T(8,128)S(1)}, f32[8,128]{1,0:T(8,128)S(1)}, u32[]{:S(2)}, u32[]{:S(2)}) collective-permute-start(f32[8,128]{1,0:T(8,128)S(1)} %shard_map.32.coef_ref), channel_id=1, source_target_pairs={{32,0},{96,64},{160,128},{224,192},{288,256},{352,320},{416,384},{... | collective-permute-start | bytes 12296 | tf_op jit(solution)/shard_map/ppermute | solution.py:509
  17.4 0.6 shard_map.29
  18.0 3.6 %collective-permute-done.4.other_coef_ref = f32[8,128]{1,0:T(8,128)S(1)} collective-permute-done((f32[8,128]{1,0:T(8,128)S(1)}, f32[8,128]{1,0:T(8,128)S(1)}, u32[]{:S(2)}, u32[]{:S(2)}) %collective-permute-start.4) | collective-permute-done | bytes 4128 | tf_op jit(solution)/shard_map/ppermute | solution.py:509
  21.6 0.0 collective-permute-done.2.inside_ref
  21.6 0.0 collective-permute-done.3.ends_ref
  21.6 0.5 shard_map.33
  22.2 10.2 %all_to_all.10.all_ref = f32[32,8,128]{2,1,0:T(8,128)S(1)} all-to-all(f32[32,8,128]{2,1,0:T(8,128)S(1)} %get-tuple-element.24), channel_id=1, replica_groups={{5,6,7,8,9,10,11,12,13,14,15,16,17,18,19,20,21,22,23,24,25,26,27,28,29,..., dimensions={0} | all-to-all | bytes 262144 | tf_op jit(solution)/shard_map/all_to_all | solution.py:520
  32.4 14.1 %all_to_all.11.all_ref = f32[8,2,16,128]{3,2,1,0:T(8,128)S(1)} all-to-all(f32[8,2,16,128]{3,2,1,0:T(8,128)S(1)} %shard_map.34), channel_id=1, replica_groups={{160,224,192,128,96,64,32,0},{320,480,448,416,384,352,288,256},{161,225..., dimensions={0} | all-to-all | bytes 262144 | tf_op jit(solution)/shard_map/all_to_all | solution.py:530
  46.6 1.3 %collective-permute-start.5 = (f32[9,8,128]{2,1,0:T(8,128)S(1)}, f32[9,8,128]{2,1,0:T(8,128)S(1)}, u32[]{:S(2)}, u32[]{:S(2)}) collective-permute-start(f32[9,8,128]{2,1,0:T(8,128)S(1)} %get-tuple-element.25), channel_id=1, source_target_pairs={{128,256},{160,320},{192,288},{224,352},{0,448},{32,416},{64,384},... | collective-permute-start | bytes 110600 | tf_op jit(solution)/shard_map/ppermute | solution.py:536
  47.8 0.9 %shard_map.36._ = f32[4,8,16,128]{3,2,1,0:T(8,128)} custom-call(f32[4,8,16,128]{3,2,1,0:T(8,128)S(1)} %get-tuple-element.23.lp_ref, f32[16,128]{1,0:T(8,128)S(1)} %get-tuple-element.26.mine_ref), custom_call_target="tpu_custom_call" | custom-call | tf_op jit(solution)/shard_map/pallas_call | solution.py:538
  48.7 7.6 %collective-permute-done.5.bound_ref = f32[9,8,128]{2,1,0:T(8,128)S(1)} collective-permute-done((f32[9,8,128]{2,1,0:T(8,128)S(1)}, f32[9,8,128]{2,1,0:T(8,128)S(1)}, u32[]{:S(2)}, u32[]{:S(2)}) %collective-permute-start.5) | collective-permute-done | bytes 36896 | tf_op jit(solution)/shard_map/ppermute | solution.py:536
  56.3 1.7 %shard_map.37 = f32[4,8,16,128]{3,2,1,0:T(8,128)} custom-call(f32[4,8,16,128]{3,2,1,0:T(8,128)S(1)} %get-tuple-element.23.lp_ref, f32[8,2,16,128]{3,2,1,0:T(8,128)S(1)} %all_to_all.11.all_ref, f32[9,8,128]{2,1,0:T(8,128)S(1)} %collective-permute-done.5.bound_ref, f32[4,8,16,128]{3,2,1,0:T(8,128)} %shard_map.36._), custom_call_target="tpu_custom_call", output_to_operand_aliasing={{}: (3, {})} | custom-call | tf_op jit(solution)/shard_map/pallas_call | solution.py:540
  (2 shorter events, 0.0 us)
Async XLA Ops:
  1.2 11.6 %collective-permute-start = (f32[2,4,2,16,128]{4,3,2,1,0:T(8,128)S(1)}, f32[2,4,2,16,128]{4,3,2,1,0:T(8,128)S(1)}, u32[]{:S(2)}, u32[]{:S(2)}) collective-permute-start(f32[2,4,2,16,128]{4,3,2,1,0:T(8,128)S(1)} %get-tuple-element.17), channel_id=1, source_target_pairs={{1,2},{3,4},{5,6},{7,8},{9,10},{11,12},{13,14},{15,16},{17,18},{19... | collective-permute-start | bytes 393224 | tf_op jit(solution)/shard_map/ppermute | solution.py:492
  7.7 5.1 %collective-permute-start.1 = (f32[2,4,2,16,128]{4,3,2,1,0:T(8,128)S(1)}, f32[2,4,2,16,128]{4,3,2,1,0:T(8,128)S(1)}, u32[]{:S(2)}, u32[]{:S(2)}) collective-permute-start(f32[2,4,2,16,128]{4,3,2,1,0:T(8,128)S(1)} %get-tuple-element.18), channel_id=1, source_target_pairs={{0,1},{2,3},{4,5},{6,7},{8,9},{10,11},{12,13},{14,15},{16,17},{18,... | collective-permute-start | bytes 393224 | tf_op jit(solution)/shard_map/ppermute | solution.py:493
  9.8 11.8 %collective-permute-start.2 = (f32[18,16,128]{2,1,0:T(8,128)S(1)}, f32[18,16,128]{2,1,0:T(8,128)S(1)}, u32[]{:S(2)}, u32[]{:S(2)}) collective-permute-start(f32[18,16,128]{2,1,0:T(8,128)S(1)} %shard_map.30.inside_ref), channel_id=1, source_target_pairs={{0,32},{32,64},{64,96},{96,128},{128,160},{160,192},{192,224},{224... | collective-permute-start | bytes 442376 | tf_op jit(solution)/shard_map/ppermute | solution.py:495
  13.0 8.6 %collective-permute-start.3 = (f32[12,16,128]{2,1,0:T(8,128)S(1)}, f32[12,16,128]{2,1,0:T(8,128)S(1)}, u32[]{:S(2)}, u32[]{:S(2)}) collective-permute-start(f32[12,16,128]{2,1,0:T(8,128)S(1)} %shard_map.31), channel_id=1, source_target_pairs={{0,32},{32,64},{64,96},{96,128},{128,160},{160,192},{192,224},{224... | collective-permute-start | bytes 294920 | tf_op jit(solution)/shard_map/ppermute | solution.py:497
  16.1 5.5 %collective-permute-start.4 = (f32[8,128]{1,0:T(8,128)S(1)}, f32[8,128]{1,0:T(8,128)S(1)}, u32[]{:S(2)}, u32[]{:S(2)}) collective-permute-start(f32[8,128]{1,0:T(8,128)S(1)} %shard_map.32.coef_ref), channel_id=1, source_target_pairs={{32,0},{96,64},{160,128},{224,192},{288,256},{352,320},{416,384},{... | collective-permute-start | bytes 12296 | tf_op jit(solution)/shard_map/ppermute | solution.py:509
  46.6 9.7 %collective-permute-start.5 = (f32[9,8,128]{2,1,0:T(8,128)S(1)}, f32[9,8,128]{2,1,0:T(8,128)S(1)}, u32[]{:S(2)}, u32[]{:S(2)}) collective-permute-start(f32[9,8,128]{2,1,0:T(8,128)S(1)} %get-tuple-element.25), channel_id=1, source_target_pairs={{128,256},{160,320},{192,288},{224,352},{0,448},{32,416},{64,384},... | collective-permute-start | bytes 110600 | tf_op jit(solution)/shard_map/ppermute | solution.py:536

commit v10 on v9

--- a/solution.py
+++ b/solution.py
@@ -251,8 +251,6 @@
     rest_ref,
     inside_ref,
     ends_ref,
-    coef_ref,
-    other_coef_ref,
     lp_ref,
     sums_ref,
     v2,
@@ -308,10 +306,14 @@
         stack[4 + b] = jnp.where(odd, last, 0.0)
     stack[2] = planes[0]
     stack[3] = planes[CZ - 1]
-    coef = coef_ref[...] + other_coef_ref[...]
     none = jnp.zeros((2, LANES), F32)
-    sums = jnp.concatenate([fold(stack[...]), none], axis=0) + jnp.where(odd, 0.0, coef)
-    sums_ref[...] = jnp.broadcast_to(sums[None], sums_ref.shape)
+    sums_ref[...] = jnp.concatenate([fold(stack[...]), none], axis=0)
+
+
+def share_kernel(sums_ref, coef_ref, other_coef_ref, out_ref):
+    odd = (lax.axis_index("tm") & 1) == 1
+    sums = sums_ref[...] + jnp.where(odd, 0.0, coef_ref[...] + other_coef_ref[...])
+    out_ref[...] = jnp.broadcast_to(sums[None], out_ref.shape)
 
 
 def window_kernel(all_ref, out_ref, rows):
@@ -509,14 +511,15 @@
     other_coef = lax.ppermute(coef, "tm", [(i, i - 1) for i in range(1, slabs, 2)])
     lp, sums = call(
         main_kernel,
-        [arr(CT, CZ, CX, CY), arr(planes, 8, LANES)],
-        11,
+        [arr(CT, CZ, CX, CY), arr(8, LANES)],
+        9,
         [
             pltpu.VMEM((CZ + 4, CX, CY), F32),
             pltpu.VMEM((2, CZ + 2, CX, CY), F32),
             pltpu.VMEM((6, CX, CY), F32),
         ],
-    )(own, outer, inner, v2, v3, v4, rest, passed, ends, coef, other_coef)
+    )(own, outer, inner, v2, v3, v4, rest, passed, ends)
+    sums = call(share_kernel, arr(planes, 8, LANES), 3)(sums, coef, other_coef)
     column = lax.all_to_all(
         sums, "space", 0, 0, axis_index_groups=[[(p + TURN) % planes for p in range(planes)]]
     )

time: 58.3 us -> 58.1 us (level)
    ppermute x1, waiting for transfers between devices: 3.64 us -> 0.01 us  [local(): lax.ppermute(coef, 'tm', [(i, i - 1) for i in range(1, slabs, 2)])]
    ppermute x1, waiting for transfers between devices: 0.01 us -> 1.87 us  [local(): ends = lax.ppermute(sent, 'tm', onward)]
    ppermute x1, waiting for transfers between devices: 0.01 us -> 1.49 us  [local(): passed = lax.ppermute(inside, 'tm', onward)]
  transfers between devices with their start and end apart: 6 -> 6, of which waited for: 2 -> 3; matrix products, arithmetic and copies ran while one was open for 0% -> 0% of each run, Pallas kernels for 3% -> 4%
where the time goes in v10:
time: 58.1 us; the launch traced here: 57.8 us
  blocking collectives  24.4 us (42%)
  starting transfers between devices  16.9 us (29%)
  waiting for transfers between devices  10.9 us (19%)
  Pallas kernels  4.31 us (7%)
  other arithmetic  1.06 us (2%)
    all_to_all x1, blocking collectives, local(): every = lax.all_to_all(window, 'tm', 0, 0, axis_index_groups=halves)  14.2 us
    all_to_all x1, blocking collectives, local(): lax.all_to_all(sums, 'space', 0, 0, axis_index_groups=[[(p + TURN) % plan...  10.2 us
    ppermute x1, waiting for transfers between devices, local(): bound = lax.ppermute(last, 'tm', serve)  7.58 us
    ppermute x1, starting transfers between devices, local(): outer = lax.ppermute(outer, 'space', across)  6.56 us
    ppermute x1, starting transfers between devices, local(): passed = lax.ppermute(inside, 'tm', onward)  2.93 us
    ppermute x1, starting transfers between devices, local(): ends = lax.ppermute(sent, 'tm', onward)  2.93 us
    ppermute x1, starting transfers between devices, local(): inner = lax.ppermute(inner, 'space', within)  1.92 us
    ppermute x1, waiting for transfers between devices, local(): ends = lax.ppermute(sent, 'tm', onward)  1.87 us
  transfers between devices with their start and end apart: 6, of which 3 were waited for; matrix products, arithmetic and copies ran while one was open for 0% of the time, Pallas kernels for 4%

profile of v10, /device:TPU:256, one launch (start us, length us, event | category | flops | bytes accessed | tf_op | source)
XLA Modules:
  0.0 57.8 jit_solution(16192127754181305361)
XLA Ops:
  0.0 1.1 %pad_maximum_fusion.loaded_ref = f32[2,4,8,16,128]{4,3,2,1,0:T(8,128)S(1)} fusion(f32[1,4,8,16,128]{4,3,2,1,0:T(8,128)} %bitcast.2, f32[1,4,8,16,128]{4,3,2,1,0:T(8,128)} %bitcast.3), kind=kLoop, calls=%fused_computation | loop fusion | flops 131072 | bytes 1048576 | tf_op jit(solution)/shard_map/stack | solution.py:492
  1.1 0.1 shard_map.28
  1.2 6.6 %collective-permute-start = (f32[2,4,2,16,128]{4,3,2,1,0:T(8,128)S(1)}, f32[2,4,2,16,128]{4,3,2,1,0:T(8,128)S(1)}, u32[]{:S(2)}, u32[]{:S(2)}) collective-permute-start(f32[2,4,2,16,128]{4,3,2,1,0:T(8,128)S(1)} %get-tuple-element.17), channel_id=1, source_target_pairs={{1,2},{3,4},{5,6},{7,8},{9,10},{11,12},{13,14},{15,16},{17,18},{19... | collective-permute-start | bytes 393224 | tf_op jit(solution)/shard_map/ppermute | solution.py:494
  7.7 1.9 %collective-permute-start.1 = (f32[2,4,2,16,128]{4,3,2,1,0:T(8,128)S(1)}, f32[2,4,2,16,128]{4,3,2,1,0:T(8,128)S(1)}, u32[]{:S(2)}, u32[]{:S(2)}) collective-permute-start(f32[2,4,2,16,128]{4,3,2,1,0:T(8,128)S(1)} %get-tuple-element.18), channel_id=1, source_target_pairs={{0,1},{2,3},{4,5},{6,7},{8,9},{10,11},{12,13},{14,15},{16,17},{18,... | collective-permute-start | bytes 393224 | tf_op jit(solution)/shard_map/ppermute | solution.py:495
  9.7 0.2 shard_map.30.inside_ref
  9.8 2.9 %collective-permute-start.2 = (f32[18,16,128]{2,1,0:T(8,128)S(1)}, f32[18,16,128]{2,1,0:T(8,128)S(1)}, u32[]{:S(2)}, u32[]{:S(2)}) collective-permute-start(f32[18,16,128]{2,1,0:T(8,128)S(1)} %shard_map.30.inside_ref), channel_id=1, source_target_pairs={{0,32},{32,64},{64,96},{96,128},{128,160},{160,192},{192,224},{224... | collective-permute-start | bytes 442376 | tf_op jit(solution)/shard_map/ppermute | solution.py:497
  12.8 0.0 collective-permute-done.outer_ref
  12.8 0.0 collective-permute-done.1.inner_ref
  12.8 0.2 shard_map.31
  13.0 2.9 %collective-permute-start.3 = (f32[12,16,128]{2,1,0:T(8,128)S(1)}, f32[12,16,128]{2,1,0:T(8,128)S(1)}, u32[]{:S(2)}, u32[]{:S(2)}) collective-permute-start(f32[12,16,128]{2,1,0:T(8,128)S(1)} %shard_map.31), channel_id=1, source_target_pairs={{0,32},{32,64},{64,96},{96,128},{128,160},{160,192},{192,224},{224... | collective-permute-start | bytes 294920 | tf_op jit(solution)/shard_map/ppermute | solution.py:499
  15.9 0.2 shard_map.33.coef_ref
  16.1 1.3 %collective-permute-start.4 = (f32[8,128]{1,0:T(8,128)S(1)}, f32[8,128]{1,0:T(8,128)S(1)}, u32[]{:S(2)}, u32[]{:S(2)}) collective-permute-start(f32[8,128]{1,0:T(8,128)S(1)} %shard_map.33.coef_ref), channel_id=1, source_target_pairs={{32,0},{96,64},{160,128},{224,192},{288,256},{352,320},{416,384},{... | collective-permute-start | bytes 12296 | tf_op jit(solution)/shard_map/ppermute | solution.py:511
  17.4 0.5 shard_map.29
  17.9 1.5 %collective-permute-done.2.inside_ref = f32[18,16,128]{2,1,0:T(8,128)S(1)} collective-permute-done((f32[18,16,128]{2,1,0:T(8,128)S(1)}, f32[18,16,128]{2,1,0:T(8,128)S(1)}, u32[]{:S(2)}, u32[]{:S(2)}) %collective-permute-start.2) | collective-permute-done | bytes 147488 | tf_op jit(solution)/shard_map/ppermute | solution.py:497
  19.4 1.9 %collective-permute-done.3.ends_ref = f32[12,16,128]{2,1,0:T(8,128)S(1)} collective-permute-done((f32[12,16,128]{2,1,0:T(8,128)S(1)}, f32[12,16,128]{2,1,0:T(8,128)S(1)}, u32[]{:S(2)}, u32[]{:S(2)}) %collective-permute-start.3) | collective-permute-done | bytes 98336 | tf_op jit(solution)/shard_map/ppermute | solution.py:499
  21.3 0.5 shard_map.32
  21.8 0.0 collective-permute-done.4.other_coef_ref
  21.9 10.2 %all_to_all.10.all_ref = f32[32,8,128]{2,1,0:T(8,128)S(1)} all-to-all(f32[32,8,128]{2,1,0:T(8,128)S(1)} %shard_map.34), channel_id=1, replica_groups={{5,6,7,8,9,10,11,12,13,14,15,16,17,18,19,20,21,22,23,24,25,26,27,28,29,..., dimensions={0} | all-to-all | bytes 262144 | tf_op jit(solution)/shard_map/all_to_all | solution.py:523
  32.1 14.2 %all_to_all.11.all_ref = f32[8,2,16,128]{3,2,1,0:T(8,128)S(1)} all-to-all(f32[8,2,16,128]{3,2,1,0:T(8,128)S(1)} %shard_map.35), channel_id=1, replica_groups={{160,224,192,128,96,64,32,0},{320,480,448,416,384,352,288,256},{161,225..., dimensions={0} | all-to-all | bytes 262144 | tf_op jit(solution)/shard_map/all_to_all | solution.py:533
  46.3 1.3 %collective-permute-start.5 = (f32[9,8,128]{2,1,0:T(8,128)S(1)}, f32[9,8,128]{2,1,0:T(8,128)S(1)}, u32[]{:S(2)}, u32[]{:S(2)}) collective-permute-start(f32[9,8,128]{2,1,0:T(8,128)S(1)} %get-tuple-element.25), channel_id=1, source_target_pairs={{128,256},{160,320},{192,288},{224,352},{0,448},{32,416},{64,384},... | collective-permute-start | bytes 110600 | tf_op jit(solution)/shard_map/ppermute | solution.py:539
  47.6 0.9 %shard_map.37._ = f32[4,8,16,128]{3,2,1,0:T(8,128)} custom-call(f32[4,8,16,128]{3,2,1,0:T(8,128)S(1)} %get-tuple-element.23.lp_ref, f32[16,128]{1,0:T(8,128)S(1)} %get-tuple-element.26.mine_ref), custom_call_target="tpu_custom_call" | custom-call | tf_op jit(solution)/shard_map/pallas_call | solution.py:541
  48.5 7.6 %collective-permute-done.5.bound_ref = f32[9,8,128]{2,1,0:T(8,128)S(1)} collective-permute-done((f32[9,8,128]{2,1,0:T(8,128)S(1)}, f32[9,8,128]{2,1,0:T(8,128)S(1)}, u32[]{:S(2)}, u32[]{:S(2)}) %collective-permute-start.5) | collective-permute-done | bytes 36896 | tf_op jit(solution)/shard_map/ppermute | solution.py:539
  56.1 1.7 %shard_map.38 = f32[4,8,16,128]{3,2,1,0:T(8,128)} custom-call(f32[4,8,16,128]{3,2,1,0:T(8,128)S(1)} %get-tuple-element.23.lp_ref, f32[8,2,16,128]{3,2,1,0:T(8,128)S(1)} %all_to_all.11.all_ref, f32[9,8,128]{2,1,0:T(8,128)S(1)} %collective-permute-done.5.bound_ref, f32[4,8,16,128]{3,2,1,0:T(8,128)} %shard_map.37._), custom_call_target="tpu_custom_call", output_to_operand_aliasing={{}: (3, {})} | custom-call | tf_op jit(solution)/shard_map/pallas_call | solution.py:543
  (3 shorter events, 0.1 us)
Async XLA Ops:
  1.2 11.6 %collective-permute-start = (f32[2,4,2,16,128]{4,3,2,1,0:T(8,128)S(1)}, f32[2,4,2,16,128]{4,3,2,1,0:T(8,128)S(1)}, u32[]{:S(2)}, u32[]{:S(2)}) collective-permute-start(f32[2,4,2,16,128]{4,3,2,1,0:T(8,128)S(1)} %get-tuple-element.17), channel_id=1, source_target_pairs={{1,2},{3,4},{5,6},{7,8},{9,10},{11,12},{13,14},{15,16},{17,18},{19... | collective-permute-start | bytes 393224 | tf_op jit(solution)/shard_map/ppermute | solution.py:494
  7.7 5.0 %collective-permute-start.1 = (f32[2,4,2,16,128]{4,3,2,1,0:T(8,128)S(1)}, f32[2,4,2,16,128]{4,3,2,1,0:T(8,128)S(1)}, u32[]{:S(2)}, u32[]{:S(2)}) collective-permute-start(f32[2,4,2,16,128]{4,3,2,1,0:T(8,128)S(1)} %get-tuple-element.18), channel_id=1, source_target_pairs={{0,1},{2,3},{4,5},{6,7},{8,9},{10,11},{12,13},{14,15},{16,17},{18,... | collective-permute-start | bytes 393224 | tf_op jit(solution)/shard_map/ppermute | solution.py:495
  9.8 9.6 %collective-permute-start.2 = (f32[18,16,128]{2,1,0:T(8,128)S(1)}, f32[18,16,128]{2,1,0:T(8,128)S(1)}, u32[]{:S(2)}, u32[]{:S(2)}) collective-permute-start(f32[18,16,128]{2,1,0:T(8,128)S(1)} %shard_map.30.inside_ref), channel_id=1, source_target_pairs={{0,32},{32,64},{64,96},{96,128},{128,160},{160,192},{192,224},{224... | collective-permute-start | bytes 442376 | tf_op jit(solution)/shard_map/ppermute | solution.py:497
  13.0 8.3 %collective-permute-start.3 = (f32[12,16,128]{2,1,0:T(8,128)S(1)}, f32[12,16,128]{2,1,0:T(8,128)S(1)}, u32[]{:S(2)}, u32[]{:S(2)}) collective-permute-start(f32[12,16,128]{2,1,0:T(8,128)S(1)} %shard_map.31), channel_id=1, source_target_pairs={{0,32},{32,64},{64,96},{96,128},{128,160},{160,192},{192,224},{224... | collective-permute-start | bytes 294920 | tf_op jit(solution)/shard_map/ppermute | solution.py:499
  16.1 5.7 %collective-permute-start.4 = (f32[8,128]{1,0:T(8,128)S(1)}, f32[8,128]{1,0:T(8,128)S(1)}, u32[]{:S(2)}, u32[]{:S(2)}) collective-permute-start(f32[8,128]{1,0:T(8,128)S(1)} %shard_map.33.coef_ref), channel_id=1, source_target_pairs={{32,0},{96,64},{160,128},{224,192},{288,256},{352,320},{416,384},{... | collective-permute-start | bytes 12296 | tf_op jit(solution)/shard_map/ppermute | solution.py:511
  46.3 9.7 %collective-permute-start.5 = (f32[9,8,128]{2,1,0:T(8,128)S(1)}, f32[9,8,128]{2,1,0:T(8,128)S(1)}, u32[]{:S(2)}, u32[]{:S(2)}) collective-permute-start(f32[9,8,128]{2,1,0:T(8,128)S(1)} %get-tuple-element.25), channel_id=1, source_target_pairs={{128,256},{160,320},{192,288},{224,352},{0,448},{32,416},{64,384},... | collective-permute-start | bytes 110600 | tf_op jit(solution)/shard_map/ppermute | solution.py:539

commit v11 on v10

--- a/solution.py
+++ b/solution.py
@@ -230,15 +230,15 @@
 
 
 def coef_kernel(own_ref, out_ref, stack):
-    stack[...] = jnp.zeros_like(stack)
     for b in range(2):
-        total = None
+        sums = []
         for t in range(CT):
-            for z in range(4 * b, 4 * b + 4):
-                diag = own_ref[2, t, z]
-                total = diag if total is None else total + diag
-        stack[4 + b] = (total - 4 * CT * (rate + 6.0)) * (1.0 / react)
-    out_ref[...] = fold(stack[...])
+            near = [own_ref[2, t, z] for z in range(4 * b, 4 * b + 4)]
+            sums.append((near[0] + near[1]) + (near[2] + near[3]))
+        total = (sums[0] + sums[1]) + (sums[2] + sums[3])
+        stack[b] = (total - 4 * CT * (rate + 6.0)) * (1.0 / react)
+    out_ref[...] = jnp.zeros_like(out_ref)
+    out_ref[4:6] = fold(stack[...])
 
 
 def main_kernel(
@@ -507,7 +507,7 @@
         ],
         3,
     )(own, outer, inner)
-    coef = call(coef_kernel, arr(8, LANES), 1, [pltpu.VMEM((8, CX, CY), F32)])(own)
+    coef = call(coef_kernel, arr(8, LANES), 1, [pltpu.VMEM((2, CX, CY), F32)])(own)
     other_coef = lax.ppermute(coef, "tm", [(i, i - 1) for i in range(1, slabs, 2)])
     lp, sums = call(
         main_kernel,

time: 58.1 us -> 58.1 us (level)
  no operation moved by 1% of the time
where the time goes in v11:
time: 58.1 us; the launch traced here: 57.8 us
  blocking collectives  24.4 us (42%)
  starting transfers between devices  16.9 us (29%)
  waiting for transfers between devices  11 us (19%)
  Pallas kernels  4.29 us (7%)
  other arithmetic  1.06 us (2%)
    all_to_all x1, blocking collectives, local(): every = lax.all_to_all(window, 'tm', 0, 0, axis_index_groups=halves)  14.2 us
    all_to_all x1, blocking collectives, local(): lax.all_to_all(sums, 'space', 0, 0, axis_index_groups=[[(p + TURN) % plan...  10.2 us
    ppermute x1, waiting for transfers between devices, local(): bound = lax.ppermute(last, 'tm', serve)  7.58 us
    ppermute x1, starting transfers between devices, local(): outer = lax.ppermute(outer, 'space', across)  6.56 us
    ppermute x1, starting transfers between devices, local(): passed = lax.ppermute(inside, 'tm', onward)  2.93 us
    ppermute x1, starting transfers between devices, local(): ends = lax.ppermute(sent, 'tm', onward)  2.93 us
    ppermute x1, starting transfers between devices, local(): inner = lax.ppermute(inner, 'space', within)  1.92 us
    ppermute x1, waiting for transfers between devices, local(): ends = lax.ppermute(sent, 'tm', onward)  1.87 us
  transfers between devices with their start and end apart: 6, of which 3 were waited for; matrix products, arithmetic and copies ran while one was open for 0% of the time, Pallas kernels for 4%

profile of v11, /device:TPU:256, one launch (start us, length us, event | category | flops | bytes accessed | tf_op | source)
XLA Modules:
  0.0 57.8 jit_solution(6573036479444755022)
XLA Ops:
  0.0 1.1 %pad_maximum_fusion.loaded_ref = f32[2,4,8,16,128]{4,3,2,1,0:T(8,128)S(1)} fusion(f32[1,4,8,16,128]{4,3,2,1,0:T(8,128)} %bitcast.2, f32[1,4,8,16,128]{4,3,2,1,0:T(8,128)} %bitcast.3), kind=kLoop, calls=%fused_computation | loop fusion | flops 131072 | bytes 1048576 | tf_op jit(solution)/shard_map/stack | solution.py:492
  1.1 0.1 shard_map.28
  1.2 6.6 %collective-permute-start = (f32[2,4,2,16,128]{4,3,2,1,0:T(8,128)S(1)}, f32[2,4,2,16,128]{4,3,2,1,0:T(8,128)S(1)}, u32[]{:S(2)}, u32[]{:S(2)}) collective-permute-start(f32[2,4,2,16,128]{4,3,2,1,0:T(8,128)S(1)} %get-tuple-element.17), channel_id=1, source_target_pairs={{1,2},{3,4},{5,6},{7,8},{9,10},{11,12},{13,14},{15,16},{17,18},{19... | collective-permute-start | bytes 393224 | tf_op jit(solution)/shard_map/ppermute | solution.py:494
  7.7 1.9 %collective-permute-start.1 = (f32[2,4,2,16,128]{4,3,2,1,0:T(8,128)S(1)}, f32[2,4,2,16,128]{4,3,2,1,0:T(8,128)S(1)}, u32[]{:S(2)}, u32[]{:S(2)}) collective-permute-start(f32[2,4,2,16,128]{4,3,2,1,0:T(8,128)S(1)} %get-tuple-element.18), channel_id=1, source_target_pairs={{0,1},{2,3},{4,5},{6,7},{8,9},{10,11},{12,13},{14,15},{16,17},{18,... | collective-permute-start | bytes 393224 | tf_op jit(solution)/shard_map/ppermute | solution.py:495
  9.7 0.2 shard_map.30.inside_ref
  9.8 2.9 %collective-permute-start.2 = (f32[18,16,128]{2,1,0:T(8,128)S(1)}, f32[18,16,128]{2,1,0:T(8,128)S(1)}, u32[]{:S(2)}, u32[]{:S(2)}) collective-permute-start(f32[18,16,128]{2,1,0:T(8,128)S(1)} %shard_map.30.inside_ref), channel_id=1, source_target_pairs={{0,32},{32,64},{64,96},{96,128},{128,160},{160,192},{192,224},{224... | collective-permute-start | bytes 442376 | tf_op jit(solution)/shard_map/ppermute | solution.py:497
  12.8 0.0 collective-permute-done.outer_ref
  12.8 0.0 collective-permute-done.1.inner_ref
  12.8 0.2 shard_map.31
  13.0 2.9 %collective-permute-start.3 = (f32[12,16,128]{2,1,0:T(8,128)S(1)}, f32[12,16,128]{2,1,0:T(8,128)S(1)}, u32[]{:S(2)}, u32[]{:S(2)}) collective-permute-start(f32[12,16,128]{2,1,0:T(8,128)S(1)} %shard_map.31), channel_id=1, source_target_pairs={{0,32},{32,64},{64,96},{96,128},{128,160},{160,192},{192,224},{224... | collective-permute-start | bytes 294920 | tf_op jit(solution)/shard_map/ppermute | solution.py:499
  15.9 0.2 shard_map.33.coef_ref
  16.1 1.3 %collective-permute-start.4 = (f32[8,128]{1,0:T(8,128)S(1)}, f32[8,128]{1,0:T(8,128)S(1)}, u32[]{:S(2)}, u32[]{:S(2)}) collective-permute-start(f32[8,128]{1,0:T(8,128)S(1)} %shard_map.33.coef_ref), channel_id=1, source_target_pairs={{32,0},{96,64},{160,128},{224,192},{288,256},{352,320},{416,384},{... | collective-permute-start | bytes 12296 | tf_op jit(solution)/shard_map/ppermute | solution.py:511
  17.4 0.5 shard_map.29
  17.9 1.5 %collective-permute-done.2.inside_ref = f32[18,16,128]{2,1,0:T(8,128)S(1)} collective-permute-done((f32[18,16,128]{2,1,0:T(8,128)S(1)}, f32[18,16,128]{2,1,0:T(8,128)S(1)}, u32[]{:S(2)}, u32[]{:S(2)}) %collective-permute-start.2) | collective-permute-done | bytes 147488 | tf_op jit(solution)/shard_map/ppermute | solution.py:497
  19.4 1.9 %collective-permute-done.3.ends_ref = f32[12,16,128]{2,1,0:T(8,128)S(1)} collective-permute-done((f32[12,16,128]{2,1,0:T(8,128)S(1)}, f32[12,16,128]{2,1,0:T(8,128)S(1)}, u32[]{:S(2)}, u32[]{:S(2)}) %collective-permute-start.3) | collective-permute-done | bytes 98336 | tf_op jit(solution)/shard_map/ppermute | solution.py:499
  21.3 0.5 shard_map.32
  21.8 0.0 collective-permute-done.4.other_coef_ref
  21.9 10.2 %all_to_all.10.all_ref = f32[32,8,128]{2,1,0:T(8,128)S(1)} all-to-all(f32[32,8,128]{2,1,0:T(8,128)S(1)} %shard_map.34), channel_id=1, replica_groups={{5,6,7,8,9,10,11,12,13,14,15,16,17,18,19,20,21,22,23,24,25,26,27,28,29,..., dimensions={0} | all-to-all | bytes 262144 | tf_op jit(solution)/shard_map/all_to_all | solution.py:523
  32.1 14.2 %all_to_all.11.all_ref = f32[8,2,16,128]{3,2,1,0:T(8,128)S(1)} all-to-all(f32[8,2,16,128]{3,2,1,0:T(8,128)S(1)} %shard_map.35), channel_id=1, replica_groups={{160,224,192,128,96,64,32,0},{320,480,448,416,384,352,288,256},{161,225..., dimensions={0} | all-to-all | bytes 262144 | tf_op jit(solution)/shard_map/all_to_all | solution.py:533
  46.3 1.3 %collective-permute-start.5 = (f32[9,8,128]{2,1,0:T(8,128)S(1)}, f32[9,8,128]{2,1,0:T(8,128)S(1)}, u32[]{:S(2)}, u32[]{:S(2)}) collective-permute-start(f32[9,8,128]{2,1,0:T(8,128)S(1)} %get-tuple-element.25), channel_id=1, source_target_pairs={{128,256},{160,320},{192,288},{224,352},{0,448},{32,416},{64,384},... | collective-permute-start | bytes 110600 | tf_op jit(solution)/shard_map/ppermute | solution.py:539
  47.6 0.9 %shard_map.37._ = f32[4,8,16,128]{3,2,1,0:T(8,128)} custom-call(f32[4,8,16,128]{3,2,1,0:T(8,128)S(1)} %get-tuple-element.23.lp_ref, f32[16,128]{1,0:T(8,128)S(1)} %get-tuple-element.26.mine_ref), custom_call_target="tpu_custom_call" | custom-call | tf_op jit(solution)/shard_map/pallas_call | solution.py:541
  48.5 7.6 %collective-permute-done.5.bound_ref = f32[9,8,128]{2,1,0:T(8,128)S(1)} collective-permute-done((f32[9,8,128]{2,1,0:T(8,128)S(1)}, f32[9,8,128]{2,1,0:T(8,128)S(1)}, u32[]{:S(2)}, u32[]{:S(2)}) %collective-permute-start.5) | collective-permute-done | bytes 36896 | tf_op jit(solution)/shard_map/ppermute | solution.py:539
  56.1 1.7 %shard_map.38 = f32[4,8,16,128]{3,2,1,0:T(8,128)} custom-call(f32[4,8,16,128]{3,2,1,0:T(8,128)S(1)} %get-tuple-element.23.lp_ref, f32[8,2,16,128]{3,2,1,0:T(8,128)S(1)} %all_to_all.11.all_ref, f32[9,8,128]{2,1,0:T(8,128)S(1)} %collective-permute-done.5.bound_ref, f32[4,8,16,128]{3,2,1,0:T(8,128)} %shard_map.37._), custom_call_target="tpu_custom_call", output_to_operand_aliasing={{}: (3, {})} | custom-call | tf_op jit(solution)/shard_map/pallas_call | solution.py:543
  (3 shorter events, 0.1 us)
Async XLA Ops:
  1.2 11.6 %collective-permute-start = (f32[2,4,2,16,128]{4,3,2,1,0:T(8,128)S(1)}, f32[2,4,2,16,128]{4,3,2,1,0:T(8,128)S(1)}, u32[]{:S(2)}, u32[]{:S(2)}) collective-permute-start(f32[2,4,2,16,128]{4,3,2,1,0:T(8,128)S(1)} %get-tuple-element.17), channel_id=1, source_target_pairs={{1,2},{3,4},{5,6},{7,8},{9,10},{11,12},{13,14},{15,16},{17,18},{19... | collective-permute-start | bytes 393224 | tf_op jit(solution)/shard_map/ppermute | solution.py:494
  7.7 5.0 %collective-permute-start.1 = (f32[2,4,2,16,128]{4,3,2,1,0:T(8,128)S(1)}, f32[2,4,2,16,128]{4,3,2,1,0:T(8,128)S(1)}, u32[]{:S(2)}, u32[]{:S(2)}) collective-permute-start(f32[2,4,2,16,128]{4,3,2,1,0:T(8,128)S(1)} %get-tuple-element.18), channel_id=1, source_target_pairs={{0,1},{2,3},{4,5},{6,7},{8,9},{10,11},{12,13},{14,15},{16,17},{18,... | collective-permute-start | bytes 393224 | tf_op jit(solution)/shard_map/ppermute | solution.py:495
  9.8 9.6 %collective-permute-start.2 = (f32[18,16,128]{2,1,0:T(8,128)S(1)}, f32[18,16,128]{2,1,0:T(8,128)S(1)}, u32[]{:S(2)}, u32[]{:S(2)}) collective-permute-start(f32[18,16,128]{2,1,0:T(8,128)S(1)} %shard_map.30.inside_ref), channel_id=1, source_target_pairs={{0,32},{32,64},{64,96},{96,128},{128,160},{160,192},{192,224},{224... | collective-permute-start | bytes 442376 | tf_op jit(solution)/shard_map/ppermute | solution.py:497
  13.0 8.3 %collective-permute-start.3 = (f32[12,16,128]{2,1,0:T(8,128)S(1)}, f32[12,16,128]{2,1,0:T(8,128)S(1)}, u32[]{:S(2)}, u32[]{:S(2)}) collective-permute-start(f32[12,16,128]{2,1,0:T(8,128)S(1)} %shard_map.31), channel_id=1, source_target_pairs={{0,32},{32,64},{64,96},{96,128},{128,160},{160,192},{192,224},{224... | collective-permute-start | bytes 294920 | tf_op jit(solution)/shard_map/ppermute | solution.py:499
  16.1 5.8 %collective-permute-start.4 = (f32[8,128]{1,0:T(8,128)S(1)}, f32[8,128]{1,0:T(8,128)S(1)}, u32[]{:S(2)}, u32[]{:S(2)}) collective-permute-start(f32[8,128]{1,0:T(8,128)S(1)} %shard_map.33.coef_ref), channel_id=1, source_target_pairs={{32,0},{96,64},{160,128},{224,192},{288,256},{352,320},{416,384},{... | collective-permute-start | bytes 12296 | tf_op jit(solution)/shard_map/ppermute | solution.py:511
  46.3 9.7 %collective-permute-start.5 = (f32[9,8,128]{2,1,0:T(8,128)S(1)}, f32[9,8,128]{2,1,0:T(8,128)S(1)}, u32[]{:S(2)}, u32[]{:S(2)}) collective-permute-start(f32[9,8,128]{2,1,0:T(8,128)S(1)} %get-tuple-element.25), channel_id=1, source_target_pairs={{128,256},{160,320},{192,288},{224,352},{0,448},{32,416},{64,384},... | collective-permute-start | bytes 110600 | tf_op jit(solution)/shard_map/ppermute | solution.py:539

commit v12 on v11

--- a/solution.py
+++ b/solution.py
@@ -17,7 +17,7 @@
 WINDOW = 16
 TURN = 5
 EARLY = (5, 7, 6, 4, 3, 2, 1, 0)
-LATE = (2, 7, 6, 5, 4, 3, 1, 0)
+LATE = (2, 3, 4, 5, 6, 7, 1, 0)
 
 rate = 8.0
 react = 0.5

time: 58.1 us -> 58.3 us (level)
  no operation moved by 1% of the time
where the time goes in v12:
time: 58.3 us; the launch traced here: 57.9 us
  blocking collectives  24.6 us (42%)
  starting transfers between devices  16.9 us (29%)
  waiting for transfers between devices  11 us (19%)
  Pallas kernels  4.29 us (7%)
  other arithmetic  1.06 us (2%)
    all_to_all x1, blocking collectives, local(): every = lax.all_to_all(window, 'tm', 0, 0, axis_index_groups=halves)  14.4 us
    all_to_all x1, blocking collectives, local(): lax.all_to_all(sums, 'space', 0, 0, axis_index_groups=[[(p + TURN) % plan...  10.2 us
    ppermute x1, waiting for transfers between devices, local(): bound = lax.ppermute(last, 'tm', serve)  7.58 us
    ppermute x1, starting transfers between devices, local(): outer = lax.ppermute(outer, 'space', across)  6.56 us
    ppermute x1, starting transfers between devices, local(): passed = lax.ppermute(inside, 'tm', onward)  2.93 us
    ppermute x1, starting transfers between devices, local(): ends = lax.ppermute(sent, 'tm', onward)  2.93 us
    ppermute x1, starting transfers between devices, local(): inner = lax.ppermute(inner, 'space', within)  1.92 us
    ppermute x1, waiting for transfers between devices, local(): ends = lax.ppermute(sent, 'tm', onward)  1.87 us
  transfers between devices with their start and end apart: 6, of which 3 were waited for; matrix products, arithmetic and copies ran while one was open for 0% of the time, Pallas kernels for 4%

profile of v12, /device:TPU:256, one launch (start us, length us, event | category | flops | bytes accessed | tf_op | source)
XLA Modules:
  0.0 57.9 jit_solution(5468213373177821546)
XLA Ops:
  0.0 1.1 %pad_maximum_fusion.loaded_ref = f32[2,4,8,16,128]{4,3,2,1,0:T(8,128)S(1)} fusion(f32[1,4,8,16,128]{4,3,2,1,0:T(8,128)} %bitcast.2, f32[1,4,8,16,128]{4,3,2,1,0:T(8,128)} %bitcast.3), kind=kLoop, calls=%fused_computation | loop fusion | flops 131072 | bytes 1048576 | tf_op jit(solution)/shard_map/stack | solution.py:492
  1.1 0.1 shard_map.28
  1.2 6.6 %collective-permute-start = (f32[2,4,2,16,128]{4,3,2,1,0:T(8,128)S(1)}, f32[2,4,2,16,128]{4,3,2,1,0:T(8,128)S(1)}, u32[]{:S(2)}, u32[]{:S(2)}) collective-permute-start(f32[2,4,2,16,128]{4,3,2,1,0:T(8,128)S(1)} %get-tuple-element.17), channel_id=1, source_target_pairs={{1,2},{3,4},{5,6},{7,8},{9,10},{11,12},{13,14},{15,16},{17,18},{19... | collective-permute-start | bytes 393224 | tf_op jit(solution)/shard_map/ppermute | solution.py:494
  7.7 1.9 %collective-permute-start.1 = (f32[2,4,2,16,128]{4,3,2,1,0:T(8,128)S(1)}, f32[2,4,2,16,128]{4,3,2,1,0:T(8,128)S(1)}, u32[]{:S(2)}, u32[]{:S(2)}) collective-permute-start(f32[2,4,2,16,128]{4,3,2,1,0:T(8,128)S(1)} %get-tuple-element.18), channel_id=1, source_target_pairs={{0,1},{2,3},{4,5},{6,7},{8,9},{10,11},{12,13},{14,15},{16,17},{18,... | collective-permute-start | bytes 393224 | tf_op jit(solution)/shard_map/ppermute | solution.py:495
  9.7 0.2 shard_map.30.inside_ref
  9.8 2.9 %collective-permute-start.2 = (f32[18,16,128]{2,1,0:T(8,128)S(1)}, f32[18,16,128]{2,1,0:T(8,128)S(1)}, u32[]{:S(2)}, u32[]{:S(2)}) collective-permute-start(f32[18,16,128]{2,1,0:T(8,128)S(1)} %shard_map.30.inside_ref), channel_id=1, source_target_pairs={{0,32},{32,64},{64,96},{96,128},{128,160},{160,192},{192,224},{224... | collective-permute-start | bytes 442376 | tf_op jit(solution)/shard_map/ppermute | solution.py:497
  12.8 0.0 collective-permute-done.outer_ref
  12.8 0.0 collective-permute-done.1.inner_ref
  12.8 0.2 shard_map.31
  13.0 2.9 %collective-permute-start.3 = (f32[12,16,128]{2,1,0:T(8,128)S(1)}, f32[12,16,128]{2,1,0:T(8,128)S(1)}, u32[]{:S(2)}, u32[]{:S(2)}) collective-permute-start(f32[12,16,128]{2,1,0:T(8,128)S(1)} %shard_map.31), channel_id=1, source_target_pairs={{0,32},{32,64},{64,96},{96,128},{128,160},{160,192},{192,224},{224... | collective-permute-start | bytes 294920 | tf_op jit(solution)/shard_map/ppermute | solution.py:499
  15.9 0.2 shard_map.33.coef_ref
  16.1 1.3 %collective-permute-start.4 = (f32[8,128]{1,0:T(8,128)S(1)}, f32[8,128]{1,0:T(8,128)S(1)}, u32[]{:S(2)}, u32[]{:S(2)}) collective-permute-start(f32[8,128]{1,0:T(8,128)S(1)} %shard_map.33.coef_ref), channel_id=1, source_target_pairs={{32,0},{96,64},{160,128},{224,192},{288,256},{352,320},{416,384},{... | collective-permute-start | bytes 12296 | tf_op jit(solution)/shard_map/ppermute | solution.py:511
  17.4 0.5 shard_map.29
  17.9 1.5 %collective-permute-done.2.inside_ref = f32[18,16,128]{2,1,0:T(8,128)S(1)} collective-permute-done((f32[18,16,128]{2,1,0:T(8,128)S(1)}, f32[18,16,128]{2,1,0:T(8,128)S(1)}, u32[]{:S(2)}, u32[]{:S(2)}) %collective-permute-start.2) | collective-permute-done | bytes 147488 | tf_op jit(solution)/shard_map/ppermute | solution.py:497
  19.4 1.9 %collective-permute-done.3.ends_ref = f32[12,16,128]{2,1,0:T(8,128)S(1)} collective-permute-done((f32[12,16,128]{2,1,0:T(8,128)S(1)}, f32[12,16,128]{2,1,0:T(8,128)S(1)}, u32[]{:S(2)}, u32[]{:S(2)}) %collective-permute-start.3) | collective-permute-done | bytes 98336 | tf_op jit(solution)/shard_map/ppermute | solution.py:499
  21.3 0.5 shard_map.32
  21.8 0.0 collective-permute-done.4.other_coef_ref
  21.9 10.2 %all_to_all.10.all_ref = f32[32,8,128]{2,1,0:T(8,128)S(1)} all-to-all(f32[32,8,128]{2,1,0:T(8,128)S(1)} %shard_map.34), channel_id=1, replica_groups={{5,6,7,8,9,10,11,12,13,14,15,16,17,18,19,20,21,22,23,24,25,26,27,28,29,..., dimensions={0} | all-to-all | bytes 262144 | tf_op jit(solution)/shard_map/all_to_all | solution.py:523
  32.1 14.4 %all_to_all.11.all_ref = f32[8,2,16,128]{3,2,1,0:T(8,128)S(1)} all-to-all(f32[8,2,16,128]{3,2,1,0:T(8,128)S(1)} %shard_map.35), channel_id=1, replica_groups={{160,224,192,128,96,64,32,0},{320,352,384,416,448,480,288,256},{161,225..., dimensions={0} | all-to-all | bytes 262144 | tf_op jit(solution)/shard_map/all_to_all | solution.py:533
  46.5 1.3 %collective-permute-start.5 = (f32[9,8,128]{2,1,0:T(8,128)S(1)}, f32[9,8,128]{2,1,0:T(8,128)S(1)}, u32[]{:S(2)}, u32[]{:S(2)}) collective-permute-start(f32[9,8,128]{2,1,0:T(8,128)S(1)} %get-tuple-element.25), channel_id=1, source_target_pairs={{128,256},{160,320},{192,288},{224,352},{0,448},{32,416},{64,384},... | collective-permute-start | bytes 110600 | tf_op jit(solution)/shard_map/ppermute | solution.py:539
  47.8 0.9 %shard_map.37._ = f32[4,8,16,128]{3,2,1,0:T(8,128)} custom-call(f32[4,8,16,128]{3,2,1,0:T(8,128)S(1)} %get-tuple-element.23.lp_ref, f32[16,128]{1,0:T(8,128)S(1)} %get-tuple-element.26.mine_ref), custom_call_target="tpu_custom_call" | custom-call | tf_op jit(solution)/shard_map/pallas_call | solution.py:541
  48.7 7.6 %collective-permute-done.5.bound_ref = f32[9,8,128]{2,1,0:T(8,128)S(1)} collective-permute-done((f32[9,8,128]{2,1,0:T(8,128)S(1)}, f32[9,8,128]{2,1,0:T(8,128)S(1)}, u32[]{:S(2)}, u32[]{:S(2)}) %collective-permute-start.5) | collective-permute-done | bytes 36896 | tf_op jit(solution)/shard_map/ppermute | solution.py:539
  56.2 1.7 %shard_map.38 = f32[4,8,16,128]{3,2,1,0:T(8,128)} custom-call(f32[4,8,16,128]{3,2,1,0:T(8,128)S(1)} %get-tuple-element.23.lp_ref, f32[8,2,16,128]{3,2,1,0:T(8,128)S(1)} %all_to_all.11.all_ref, f32[9,8,128]{2,1,0:T(8,128)S(1)} %collective-permute-done.5.bound_ref, f32[4,8,16,128]{3,2,1,0:T(8,128)} %shard_map.37._), custom_call_target="tpu_custom_call", output_to_operand_aliasing={{}: (3, {})} | custom-call | tf_op jit(solution)/shard_map/pallas_call | solution.py:543
  (3 shorter events, 0.1 us)
Async XLA Ops:
  1.2 11.6 %collective-permute-start = (f32[2,4,2,16,128]{4,3,2,1,0:T(8,128)S(1)}, f32[2,4,2,16,128]{4,3,2,1,0:T(8,128)S(1)}, u32[]{:S(2)}, u32[]{:S(2)}) collective-permute-start(f32[2,4,2,16,128]{4,3,2,1,0:T(8,128)S(1)} %get-tuple-element.17), channel_id=1, source_target_pairs={{1,2},{3,4},{5,6},{7,8},{9,10},{11,12},{13,14},{15,16},{17,18},{19... | collective-permute-start | bytes 393224 | tf_op jit(solution)/shard_map/ppermute | solution.py:494
  7.7 5.0 %collective-permute-start.1 = (f32[2,4,2,16,128]{4,3,2,1,0:T(8,128)S(1)}, f32[2,4,2,16,128]{4,3,2,1,0:T(8,128)S(1)}, u32[]{:S(2)}, u32[]{:S(2)}) collective-permute-start(f32[2,4,2,16,128]{4,3,2,1,0:T(8,128)S(1)} %get-tuple-element.18), channel_id=1, source_target_pairs={{0,1},{2,3},{4,5},{6,7},{8,9},{10,11},{12,13},{14,15},{16,17},{18,... | collective-permute-start | bytes 393224 | tf_op jit(solution)/shard_map/ppermute | solution.py:495
  9.8 9.6 %collective-permute-start.2 = (f32[18,16,128]{2,1,0:T(8,128)S(1)}, f32[18,16,128]{2,1,0:T(8,128)S(1)}, u32[]{:S(2)}, u32[]{:S(2)}) collective-permute-start(f32[18,16,128]{2,1,0:T(8,128)S(1)} %shard_map.30.inside_ref), channel_id=1, source_target_pairs={{0,32},{32,64},{64,96},{96,128},{128,160},{160,192},{192,224},{224... | collective-permute-start | bytes 442376 | tf_op jit(solution)/shard_map/ppermute | solution.py:497
  13.0 8.3 %collective-permute-start.3 = (f32[12,16,128]{2,1,0:T(8,128)S(1)}, f32[12,16,128]{2,1,0:T(8,128)S(1)}, u32[]{:S(2)}, u32[]{:S(2)}) collective-permute-start(f32[12,16,128]{2,1,0:T(8,128)S(1)} %shard_map.31), channel_id=1, source_target_pairs={{0,32},{32,64},{64,96},{96,128},{128,160},{160,192},{192,224},{224... | collective-permute-start | bytes 294920 | tf_op jit(solution)/shard_map/ppermute | solution.py:499
  16.1 5.8 %collective-permute-start.4 = (f32[8,128]{1,0:T(8,128)S(1)}, f32[8,128]{1,0:T(8,128)S(1)}, u32[]{:S(2)}, u32[]{:S(2)}) collective-permute-start(f32[8,128]{1,0:T(8,128)S(1)} %shard_map.33.coef_ref), channel_id=1, source_target_pairs={{32,0},{96,64},{160,128},{224,192},{288,256},{352,320},{416,384},{... | collective-permute-start | bytes 12296 | tf_op jit(solution)/shard_map/ppermute | solution.py:511
  46.5 9.7 %collective-permute-start.5 = (f32[9,8,128]{2,1,0:T(8,128)S(1)}, f32[9,8,128]{2,1,0:T(8,128)S(1)}, u32[]{:S(2)}, u32[]{:S(2)}) collective-permute-start(f32[9,8,128]{2,1,0:T(8,128)S(1)} %get-tuple-element.25), channel_id=1, source_target_pairs={{128,256},{160,320},{192,288},{224,352},{0,448},{32,416},{64,384},... | collective-permute-start | bytes 110600 | tf_op jit(solution)/shard_map/ppermute | solution.py:539
